TPU v7x, 32 devices: a whole 2x2x4 slice. The times are simulated.
32 devices in a mesh: groups: 1, expert: 32 (over z, y, x, core), dp: 1.
Axes of the slice: x: 2, y: 2, z: 4, core: 2. Of those that a mesh axis runs over, the one named last changes fastest.
Arguments:
- grad_out: bfloat16 [4096, 1024], P(('groups', 'expert', 'dp')), may hold values from -6 to 6
- gates: float32 [4096, 8], P(('groups', 'expert', 'dp')), may hold values from 0.05 to 1
- expert_ids: int32 [4096, 8], P(('groups', 'expert', 'dp')), may hold values from 0 to 31, as said below
- pre_acts: bfloat16 [4096, 8, 768], P(('groups', 'expert', 'dp')), may hold values from -8 to 8
- w2: bfloat16 [32, 384, 1024], P('expert', None, 'dp'), may hold values from -0.1875 to 0.1875
Outputs:
- pre_grad: bfloat16 [4096, 8, 768], P(('groups', 'expert', 'dp'))
- w2_grad: bfloat16 [32, 384, 1024], P('expert', 'groups', 'dp')
Inputs may be any that keep to these rules, and one draw needn't show every extreme that they name: `expert_ids`: each token names 8 different experts. There is a hot list of 2 experts, the same for all devices of a part, that the 128 tokens of every device name exactly 64 times each; every other expert is named at most 31 times by one device's tokens, and in every draw one of them is named exactly 31 times by every device's tokens.
All inputs are finite; a program needn't handle non-finite values.
Results may differ from a plain program's by a relative error of at most 0.0057.
Values may be sent and summed in bfloat16 or wider, within the bound.
No kernel may reach another device: no remote copies, remote signals or barrier semaphores. Data moves between devices by JAX's collectives and lax.ppermute only.
A program may use at most 128 MiB of HBM per device.

v0:
```python
import jax
import jax.numpy as jnp
from jax import lax
from jax.sharding import PartitionSpec as P


def silu_parts(gate_pre):
    sigma = jax.nn.sigmoid(gate_pre)
    return (gate_pre * sigma, sigma * (1.0 + gate_pre * (1.0 - sigma)))


def split_rows(flat_pre, hidden_width):
    gate_pre = flat_pre[:, :hidden_width].astype(jnp.float32)
    up_pre = flat_pre[:, hidden_width:].astype(jnp.float32)
    activation, slopes = silu_parts(gate_pre)
    return (up_pre, activation, slopes)


def grads_from(hidden_grad, up_pre, activation, slopes):
    return jnp.concatenate([hidden_grad * up_pre * slopes, hidden_grad * activation], 1).astype(
        jnp.bfloat16
    )


def per_device(grad_out, gates, expert_ids, pre_acts, w2):
    expert_count = lax.axis_size("expert")
    token_count, top_count = expert_ids.shape
    model_width = grad_out.shape[1]
    hidden_width = w2.shape[1]
    row_count = token_count * top_count
    capacity = min(token_count, 2 * token_count * top_count // expert_count)
    grad_rows = (
        (gates[:, :, None] * grad_out[:, None, :].astype(jnp.float32))
        .astype(jnp.bfloat16)
        .reshape(row_count, model_width)
    )
    flat_pre = pre_acts.reshape(row_count, 2 * hidden_width)
    flat_ids = expert_ids.reshape(row_count)
    onehot = (flat_ids[:, None] == jnp.arange(expert_count, dtype=jnp.int32)[None, :]).astype(
        jnp.int32
    )
    ranks = jnp.sum(jnp.cumsum(onehot, 0) * onehot, 1) - 1
    slots = flat_ids * capacity + ranks
    whole_weights = lax.all_gather(w2, "dp", axis=2, tiled=True)
    grad_buffer = (
        jnp.zeros((expert_count * capacity, model_width), jnp.bfloat16)
        .at[slots]
        .set(grad_rows, mode="drop")
    )
    payload_buffer = (
        jnp.zeros((expert_count * capacity, flat_pre.shape[1]), jnp.bfloat16)
        .at[slots]
        .set(flat_pre, mode="drop")
    )
    arrived_grad, arrived_payload = (
        lax.all_to_all(
            grad_buffer.reshape(expert_count, capacity, model_width),
            "expert",
            split_axis=0,
            concat_axis=0,
            tiled=True,
        ),
        lax.all_to_all(
            payload_buffer.reshape(expert_count, capacity, flat_pre.shape[1]),
            "expert",
            split_axis=0,
            concat_axis=0,
            tiled=True,
        ),
    )
    arrived_grad = arrived_grad.reshape(expert_count * capacity, model_width)
    arrived_payload = arrived_payload.reshape(expert_count * capacity, flat_pre.shape[1])
    own_weight = whole_weights[0]
    arrived_slope = lax.dot_general(
        arrived_grad, own_weight, (((1,), (1,)), ((), ())), preferred_element_type=jnp.float32
    )
    arrived_up, arrived_act, arrived_slopes = split_rows(arrived_payload, hidden_width)
    arrived_hidden = (arrived_act * arrived_up).astype(jnp.bfloat16)
    outgoing = grads_from(arrived_slope, arrived_up, arrived_act, arrived_slopes)
    returned = lax.all_to_all(
        outgoing.reshape(expert_count, capacity, 2 * hidden_width),
        "expert",
        split_axis=0,
        concat_axis=0,
        tiled=True,
    )
    returned = returned.reshape(expert_count * capacity, 2 * hidden_width)
    weight_terms = lax.dot_general(
        arrived_hidden, arrived_grad, (((0,), (0,)), ((), ())), preferred_element_type=jnp.float32
    )
    picked = jnp.take(returned, slots, axis=0, mode="clip")
    weight_total = lax.psum_scatter(weight_terms, "dp", scatter_dimension=1, tiled=True)
    pre_grad = picked.reshape(token_count, top_count, 2 * hidden_width)
    return (pre_grad, weight_total[None].astype(jnp.bfloat16))


def solution(mesh):
    in_specs = (
        P(("groups", "expert", "dp"), None),
        P(("groups", "expert", "dp"), None),
        P(("groups", "expert", "dp"), None),
        P(("groups", "expert", "dp"), None, None),
        P("expert", None, "dp"),
    )
    out_specs = (P(("groups", "expert", "dp"), None, None), P("expert", "groups", "dp"))
    return jax.shard_map(
        per_device, mesh=mesh, in_specs=in_specs, out_specs=out_specs, check_vma=False
    )
```

profile of v0, /device:TPU:0, one launch (start us, length us, event | category | flops | bytes accessed | tf_op | source)
XLA Modules:
  0.0 288.2 jit_solution(5434512667610163051)
XLA Ops:
  0.6 0.0 copy-start
  0.6 0.8 broadcast_multiply_fusion
  1.5 0.8 copy.8
  2.2 0.1 eq.29
  2.3 0.1 eq.25
  2.4 0.1 copy.7
  2.5 0.1 mul.64
  2.6 9.0 %reduce-window.6 = s32[32,8,128]{2,1,0:T(8,128)S(1)} reduce-window(s32[32,8,128]{2,1,0:T(8,128)S(1)} %fusion.30, s32[]{:T(128)} %constant.8.clone.1), window={size=1x1x128 pad=0_0x0_0x127_0}, to_apply=%region_0.0 | reduce-window | flops 4161536 | bytes 262148 | tf_op jit(solution)/shard_map/reduce-window
  11.7 0.1 slice.18
  11.8 0.1 copy.10
  11.9 0.1 copy.11
  12.0 0.1 broadcast_add_fusion
  12.2 0.0 copy-done
  12.2 7.4 %scatter_custom_fusion.1 = bf16[2048,768]{1,0:T(8,128)(2,1)} fusion(s32[1024]{0:T(1024)S(1)} %bitcast.55, bf16[128,8,768]{2,1,0:T(8,128)(2,1)S(1)} %copy-done, bf16[]{:T(256)} %constant.6.clone.1), kind=kCustom, calls=%fused_computation.25 | custom fusion | bytes 4718594 | tf_op jit(solution)/shard_map/scatter | solution.py:53
  19.6 0.0 copy-start.3
  19.6 0.0 copy-start.2
  19.6 7.4 %all-to-all-start.1 = ((bf16[32,64,768]{2,1,0:T(8,128)(2,1)}), bf16[32,64,768]{2,1,0:T(8,128)(2,1)}, u32[]{:S(2)}, u32[]{:S(2)}) async-start(bf16[32,64,768]{2,1,0:T(8,128)(2,1)} %bitcast.45), calls=%async_computation.1 | async-start | bytes 6291456 | tf_op jit(solution)/shard_map/all_to_all | solution.py:63
  27.0 0.0 copy-done.3
  27.0 0.1 copy.12
  27.1 0.1 mul.66
  27.2 0.0 copy-done.2
  27.3 8.3 %scatter_custom_fusion = bf16[2048,1024]{1,0:T(8,128)(2,1)} fusion(s32[1024]{0:T(1024)S(1)} %bitcast.56, f32[128,1024]{1,0:T(8,128)S(1)} %convert_element_type.31, f32[1024]{0:T(1024)S(1)} %mul.66, bf16[]{:T(256)} %constant.6.clone.1), kind=kCustom, calls=%fused_computation.20 | custom fusion | flops 2097152 | bytes 4722690 | tf_op jit(solution)/shard_map/scatter | solution.py:48
  35.5 62.9 %all-to-all-done.1 = bf16[32,64,768]{2,1,0:T(8,128)(2,1)} async-done(((bf16[32,64,768]{2,1,0:T(8,128)(2,1)}), bf16[32,64,768]{2,1,0:T(8,128)(2,1)}, u32[]{:S(2)}, u32[]{:S(2)}) %all-to-all-start.1) | async-done | bytes 3145760 | tf_op jit(solution)/shard_map/all_to_all | solution.py:63
  98.4 0.0 copy-start.4
  98.4 97.6 %all_to_all.15 = bf16[32,64,1024]{2,1,0:T(8,128)(2,1)S(1)} all-to-all(bf16[32,64,1024]{2,1,0:T(8,128)(2,1)} %bitcast.44), channel_id=1, replica_groups=mesh['groups'=1,'expert'=32,'dp'=1] {'expert'}, dimensions={0} | all-to-all | bytes 8388608 | tf_op jit(solution)/shard_map/all_to_all | solution.py:56
  196.0 0.0 copy-start.1
  196.0 0.0 copy-done.4
  196.0 6.9 %fusion.2 = (bf16[2048,384]{1,0:T(8,128)(2,1)S(1)}, bf16[2048,384]{1,0:T(8,128)(2,1)S(1)}) fusion(bf16[2048,768]{1,0:T(8,128)(2,1)} %bitcast.10, bf16[2048,1024]{1,0:T(8,128)(2,1)S(1)} %bitcast.46, bf16[1,384,1024]{2,1,0:T(8,128)(2,1)S(1)} %copy-done.4), kind=kOutput, calls=%fused_computation.11 | convolution fusion | flops 1622409216 | bytes 11272192 | tf_op jit(solution)/shard_map/dot_general | solution.py:74
  203.0 0.0 copy-done.1
  203.0 2.1 pad_maximum_fusion
  205.1 3.8 %all-to-all-start.2 = ((bf16[32,64,768]{2,1,0:T(8,128)(2,1)}), bf16[32,64,768]{2,1,0:T(8,128)(2,1)}, u32[]{:S(2)}, u32[]{:S(2)}) async-start(bf16[32,64,768]{2,1,0:T(8,128)(2,1)} %pad_maximum_fusion), calls=%async_computation.2 | async-start | bytes 6291456 | tf_op jit(solution)/shard_map/all_to_all | solution.py:80
  208.9 6.0 %fusion.23 = bf16[1,384,1024]{2,1,0:T(8,128)(2,1)} fusion(bf16[2048,1024]{1,0:T(8,128)(2,1)} %bitcast.47, bf16[2048,768]{1,0:T(8,128)(2,1)} %bitcast.10), kind=kOutput, calls=%fused_computation.30 | convolution fusion | flops 1617297408 | bytes 8126464 | tf_op jit(solution)/shard_map/dot_general | solution.py:88
  214.9 65.4 %all-to-all-done.2 = bf16[32,64,768]{2,1,0:T(8,128)(2,1)} async-done(((bf16[32,64,768]{2,1,0:T(8,128)(2,1)}), bf16[32,64,768]{2,1,0:T(8,128)(2,1)}, u32[]{:S(2)}, u32[]{:S(2)}) %all-to-all-start.2) | async-done | bytes 3145760 | tf_op jit(solution)/shard_map/all_to_all | solution.py:80
  280.3 7.9 %gather_fusion = bf16[1024,768]{1,0:T(8,128)(2,1)} fusion(bf16[2048,768]{1,0:T(8,128)(2,1)} %bitcast.13, s32[1024]{0:T(1024)S(1)} %broadcast_clamp_fusion), kind=kCustom, calls=%fused_computation | custom fusion | bytes 3149824 | tf_op jit(solution)/shard_map/jit(_take)/gather | solution.py:91
  (8 shorter events, 0.1 us)
Async XLA Ops:
  0.6 11.6 %copy-start = (bf16[128,8,768]{2,1,0:T(8,128)(2,1)S(1)}, bf16[128,8,768]{2,1,0:T(8,128)(2,1)}, u32[]{:S(2)}) copy-start(bf16[128,8,768]{2,1,0:T(8,128)(2,1)} %param.8) | copy-start | bytes 4718596
  19.6 7.4 %copy-start.3 = (f32[128,8]{0,1:T(8,128)S(1)}, f32[128,8]{0,1:T(8,128)}, u32[]{:S(2)}) copy-start(f32[128,8]{0,1:T(8,128)} %param.6) | copy-start | bytes 12292
  19.6 7.6 %copy-start.2 = (bf16[128,1024]{1,0:T(8,128)(2,1)S(1)}, bf16[128,1024]{1,0:T(8,128)(2,1)}, u32[]{:S(2)}) copy-start(bf16[128,1024]{1,0:T(8,128)(2,1)} %param.5) | copy-start | bytes 786436
  19.6 78.9 %all-to-all-start.1 = ((bf16[32,64,768]{2,1,0:T(8,128)(2,1)}), bf16[32,64,768]{2,1,0:T(8,128)(2,1)}, u32[]{:S(2)}, u32[]{:S(2)}) async-start(bf16[32,64,768]{2,1,0:T(8,128)(2,1)} %bitcast.45), calls=%async_computation.1 | async-start | bytes 6291456 | tf_op jit(solution)/shard_map/all_to_all | solution.py:63
  98.4 97.6 %copy-start.4 = (bf16[1,384,1024]{2,1,0:T(8,128)(2,1)S(1)}, bf16[1,384,1024]{2,1,0:T(8,128)(2,1)}, u32[]{:S(2)}) copy-start(bf16[1,384,1024]{2,1,0:T(8,128)(2,1)} %param.9) | copy-start | bytes 2359300
  196.0 6.9 %copy-start.1 = (bf16[32,64,1024]{2,1,0:T(8,128)(2,1)}, bf16[32,64,1024]{2,1,0:T(8,128)(2,1)S(1)}, u32[]{:S(2)}) copy-start(bf16[32,64,1024]{2,1,0:T(8,128)(2,1)S(1)} %all_to_all.15) | copy-start | bytes 12582916
  205.1 75.3 %all-to-all-start.2 = ((bf16[32,64,768]{2,1,0:T(8,128)(2,1)}), bf16[32,64,768]{2,1,0:T(8,128)(2,1)}, u32[]{:S(2)}, u32[]{:S(2)}) async-start(bf16[32,64,768]{2,1,0:T(8,128)(2,1)} %pad_maximum_fusion), calls=%async_computation.2 | async-start | bytes 6291456 | tf_op jit(solution)/shard_map/all_to_all | solution.py:80
where the time goes:
time: 289 us; the launch traced here: 288 us
  waiting for transfers between devices  128 us (44%)
  blocking collectives  97.6 us (34%)
  other arithmetic  20.4 us (7%)
  local copies, waits for them, and re-layouts  16.9 us (6%)
  matrix products  12.9 us (4%)
  starting transfers between devices  11.2 us (4%)
    all_to_all x1, blocking collectives, per_device(): lax.all_to_all(grad_buffer.reshape(expert_count, capacity, model_width),...  97.6 us
    all_to_all x1, waiting for transfers between devices, per_device(): lax.all_to_all(outgoing.reshape(expert_count, capacity, 2 * hidden_width)...  65.4 us
    all_to_all x1, waiting for transfers between devices, per_device(): lax.all_to_all(payload_buffer.reshape(expert_count, capacity, flat_pre.sh...  62.9 us
    another operation x3, other arithmetic  9.15 us
    scatter x1, other arithmetic, per_device(): grad_buffer = jnp.zeros((expert_count * capacity, model_width), jnp.bfloa...  8.28 us
    gather x1, local copies, waits for them, and re-layouts, per_device(): picked = jnp.take(returned, slots, axis=0, mode='clip')  7.86 us
    all_to_all x1, starting transfers between devices, per_device(): lax.all_to_all(payload_buffer.reshape(expert_count, capacity, flat_pre.sh...  7.41 us
    scatter x1, local copies, waits for them, and re-layouts, per_device(): payload_buffer = jnp.zeros((expert_count * capacity, flat_pre.shape[1]),...  7.38 us
  transfers between devices with their start and end apart: 2, of which 2 were waited for; matrix products, arithmetic and copies ran while one was open for 5% of the time, Pallas kernels for 0%

commit v1 on v0

v1 whole, which is shorter than its diff:
```python
import jax
import jax.numpy as jnp
from jax import lax
from jax.experimental import pallas as pl
from jax.experimental.pallas import tpu as pltpu
from jax.sharding import PartitionSpec as P

X_BIT, Y_BIT, CORE_BIT = 2, 4, 1
PLANE = (0, X_BIT, Y_BIT, X_BIT | Y_BIT)
ID_ROWS = 16
VMEM_BYTES = 56 * 1024 * 1024
F32, BF16 = jnp.float32, jnp.bfloat16


def params(steps=1):
    return pltpu.CompilerParams(
        dimension_semantics=("arbitrary",) * steps, vmem_limit_bytes=VMEM_BYTES
    )


def cost(flops, moved):
    return pl.CostEstimate(flops=flops, bytes_accessed=moved, transcendentals=0)


def swap(value, bit):
    count = lax.axis_size("expert")
    return lax.ppermute(value, "expert", [(j, j ^ bit) for j in range(count)])


def iota_f32(shape, dim):
    return lax.broadcasted_iota(jnp.int32, shape, dim).astype(F32)


def pack_kernel(cap, ids_ref, gates_ref, pre_ref, out_ref, place_ref, hidden, place):
    step = pl.program_id(0)
    members = pl.num_programs(0)
    rows = ids_ref.shape[1]
    width = hidden.shape[1]

    @pl.when(step == 0)
    def _():
        gate_pre = pre_ref[:, :width].astype(F32)
        up_pre = pre_ref[:, width:].astype(F32)
        value = gate_pre * jax.nn.sigmoid(gate_pre) * up_pre
        hidden[...] = (value * gates_ref[...]).astype(BF16)
        ids = ids_ref[...]
        member = (ids >> 3) * 2 + (ids & 1)
        own = lax.broadcasted_iota(jnp.int32, (members, rows), 0) == member
        before = lax.broadcasted_iota(jnp.int32, (rows, rows), 0) < lax.broadcasted_iota(
            jnp.int32, (rows, rows), 1
        )
        rank = jnp.dot(
            own.astype(F32).astype(BF16),
            before.astype(F32).astype(BF16),
            preferred_element_type=F32,
        )
        slot = jnp.sum(jnp.where(own, rank, 0.0), 0, keepdims=True)
        where = member * cap + slot.astype(jnp.int32)
        place[...] = where
        place_ref[...] = where

    wanted = lax.broadcasted_iota(jnp.int32, (cap, rows), 0) + step * cap
    pick = (wanted == place[...]).astype(F32).astype(BF16)
    out_ref[0] = jnp.dot(pick, hidden[...], preferred_element_type=F32).astype(BF16)


def pack_hidden(ids, gate_column, flat_pre, members, cap):
    rows, both = flat_pre.shape
    width = both // 2
    return pl.pallas_call(
        lambda *refs: pack_kernel(cap, *refs),
        grid=(members,),
        in_specs=[
            pl.BlockSpec((1, rows), lambda q: (0, 0)),
            pl.BlockSpec((rows, 1), lambda q: (0, 0)),
            pl.BlockSpec((rows, both), lambda q: (0, 0)),
        ],
        out_specs=[
            pl.BlockSpec((1, cap, width), lambda q: (q, 0, 0)),
            pl.BlockSpec((1, rows), lambda q: (0, 0)),
        ],
        out_shape=[
            jax.ShapeDtypeStruct((members, cap, width), BF16),
            jax.ShapeDtypeStruct((1, rows), jnp.int32),
        ],
        scratch_shapes=[pltpu.VMEM((rows, width), BF16), pltpu.VMEM((1, rows), jnp.int32)],
        compiler_params=params(),
        cost_estimate=cost(2 * members * cap * rows * width, 2 * rows * both),
    )(ids, gate_column, flat_pre)


def picks(ids, me, cap):
    top, tokens = ids.shape
    experts = [(me ^ mask).astype(F32) for mask in PLANE]
    hits = [(ids == expert).astype(F32) for expert in experts]
    any_hit = hits[0] + hits[1] + hits[2] + hits[3]
    earlier = []
    total = jnp.zeros((1, tokens), F32)
    for k in range(top):
        earlier.append(total)
        total = total + any_hit[k : k + 1]
    before = iota_f32((tokens, tokens), 0) < iota_f32((tokens, tokens), 1)
    base = jnp.dot(
        jnp.broadcast_to(total, (8, tokens)).astype(BF16),
        before.astype(F32).astype(BF16),
        preferred_element_type=F32,
    )[:1]
    rank = base + jnp.concatenate(earlier, 0) + 1.0
    row = iota_f32((cap, tokens), 0) + 1.0
    parts = []
    for hit in hits:
        slot = jnp.sum(hit * rank, 0, keepdims=True)
        parts.append((row == slot).astype(F32).astype(BF16))
    return jnp.concatenate(parts, 1)


def source_ids(block, tokens, top):
    return block[tokens : tokens + ID_ROWS, :tokens].astype(F32)[:top]


def slope_kernel(cap, tokens, top, info, near_ref, far_ref, w0, w1, w2, w3a, w3b, out_ref):
    me = info[0]
    core = me & 1
    near, far = near_ref[...], far_ref[...]
    grads = jnp.concatenate([near[:tokens], far[:tokens]], 0)
    weights = (w0[...], w1[...], w2[...], jnp.concatenate([w3a[...], w3b[...]], 0))
    slopes = [
        lax.dot_general(
            grads, weight, (((1,), (1,)), ((), ())), preferred_element_type=F32
        ).astype(BF16)
        for weight in weights
    ]
    for side, block in enumerate((near, far)):
        pick = picks(source_ids(block, tokens, top), me, cap)
        stacked = jnp.concatenate(
            [slope[side * tokens : (side + 1) * tokens] for slope in slopes], 0
        )
        packed = jnp.dot(pick, stacked, preferred_element_type=F32).astype(BF16)
        out_ref[core if side == 0 else 1 - core] = packed


def packed_slopes(info, near, far, weights, cap, tokens, top):
    block_rows = tokens + ID_ROWS
    blocks = near.shape[0] // block_rows
    model = near.shape[1]
    width = weights[0].shape[0]
    whole = lambda w: pl.BlockSpec(w.shape, lambda j, s: (0, 0))
    return pl.pallas_call(
        lambda *refs: slope_kernel(cap, tokens, top, *refs),
        grid_spec=pltpu.PrefetchScalarGridSpec(
            num_scalar_prefetch=1,
            grid=(blocks,),
            in_specs=[
                pl.BlockSpec((block_rows, model), lambda j, s: (j, 0)),
                pl.BlockSpec((block_rows, model), lambda j, s: (j, 0)),
            ]
            + [whole(w) for w in weights],
            out_specs=pl.BlockSpec((2, cap, width), lambda j, s: (s[1 + j], 0, 0)),
        ),
        out_shape=jax.ShapeDtypeStruct((2 * blocks, cap, width), BF16),
        compiler_params=params(),
        cost_estimate=cost(2 * 2 * blocks * tokens * model * 4 * width, 4 * near.size),
    )(info, near, far, *weights)


def weight_kernel(
    cap, tokens, top, info, near_ref, far_ref, hidden_ref, own_ref, x_ref, y_ref, xk_ref, yk_ref, spread, grads
):
    me = info[0]
    core = me & 1
    block_rows = tokens + ID_ROWS
    blocks = near_ref.shape[0] // block_rows
    width = hidden_ref.shape[2]
    half = width // 2

    def fill(j, carry):
        for side, ref in enumerate((near_ref, far_ref)):
            start = pl.multiple_of(j * block_rows, ID_ROWS)
            block = ref[pl.ds(start, block_rows), :]
            pick = picks(source_ids(block, tokens, top), me, cap)
            member = info[1 + j] * 2 + (core if side == 0 else 1 - core)
            arrived = hidden_ref[member].astype(F32).T.astype(BF16)
            wide = jnp.dot(arrived, pick, preferred_element_type=F32).astype(BF16)
            at = pl.multiple_of((side * blocks + j) * tokens, tokens)
            for e in range(4):
                spread[pl.ds(e * width, width), pl.ds(at, tokens)] = wide[
                    :, e * tokens : (e + 1) * tokens
                ]
            grads[pl.ds(at, tokens), :] = block[:tokens]
        return carry

    lax.fori_loop(0, blocks, fill, 0)

    def product(expert, first, count):
        at = expert * width + first
        return jnp.dot(
            spread[at : at + count, :], grads[...], preferred_element_type=F32
        )

    x_ref[:half] = product(1, 0, half).astype(BF16)
    x_ref[half:] = product(3, 0, half).astype(BF16)
    y_ref[:half] = product(2, half, half).astype(BF16)
    y_ref[half:] = product(3, half, half).astype(BF16)
    own_ref[...] = product(0, 0, width)
    xk_ref[...] = product(1, half, half).astype(BF16)
    yk_ref[...] = product(2, 0, half).astype(BF16)


def weight_partials(info, near, far, hidden, cap, tokens, top):
    blocks = near.shape[0] // (tokens + ID_ROWS)
    model = near.shape[1]
    width = hidden.shape[2]
    half = width // 2
    every = 2 * blocks * tokens
    vmem = pl.BlockSpec(memory_space=pltpu.VMEM)
    return pl.pallas_call(
        lambda *refs: weight_kernel(cap, tokens, top, *refs),
        in_specs=[pl.BlockSpec(memory_space=pltpu.SMEM), vmem, vmem, vmem],
        out_specs=[vmem] * 5,
        out_shape=[
            jax.ShapeDtypeStruct((width, model), F32),
            jax.ShapeDtypeStruct((width, model), BF16),
            jax.ShapeDtypeStruct((width, model), BF16),
            jax.ShapeDtypeStruct((half, model), BF16),
            jax.ShapeDtypeStruct((half, model), BF16),
        ],
        scratch_shapes=[pltpu.VMEM((4 * width, every), BF16), pltpu.VMEM((every, model), BF16)],
        compiler_params=params(0),
        cost_estimate=cost(2 * every * model * 4 * width, 4 * near.size),
    )(info, near, far, hidden)


def finish_kernel(place_ref, gates_ref, pre_ref, back_ref, out_ref):
    rows, both = pre_ref.shape
    width = both // 2
    slots = back_ref.shape[0]
    pick = lax.broadcasted_iota(jnp.int32, (rows, slots), 1) == place_ref[...]
    slope = jnp.dot(
        pick.astype(F32).astype(BF16), back_ref[...], preferred_element_type=F32
    )
    slope = slope * gates_ref[...]
    gate_pre = pre_ref[:, :width].astype(F32)
    up_pre = pre_ref[:, width:].astype(F32)
    sigma = jax.nn.sigmoid(gate_pre)
    out_ref[:, :width] = (
        slope * up_pre * (sigma * (1.0 + gate_pre * (1.0 - sigma)))
    ).astype(BF16)
    out_ref[:, width:] = (slope * (gate_pre * sigma)).astype(BF16)


def finish(place, gate_column, flat_pre, back):
    rows, both = flat_pre.shape
    tile = rows // 4
    return pl.pallas_call(
        finish_kernel,
        grid=(4,),
        in_specs=[
            pl.BlockSpec((tile, 1), lambda i: (i, 0)),
            pl.BlockSpec((tile, 1), lambda i: (i, 0)),
            pl.BlockSpec((tile, both), lambda i: (i, 0)),
            pl.BlockSpec(back.shape, lambda i: (0, 0)),
        ],
        out_specs=pl.BlockSpec((tile, both), lambda i: (i, 0)),
        out_shape=jax.ShapeDtypeStruct((rows, both), BF16),
        compiler_params=params(),
        cost_estimate=cost(2 * rows * both * back.shape[0], 4 * rows * both),
    )(place, gate_column, flat_pre, back)


def per_device(grad_out, gates, expert_ids, pre_acts, w2):
    count = lax.axis_size("expert")
    me = lax.axis_index("expert")
    tokens, top = expert_ids.shape
    model = grad_out.shape[1]
    width = w2.shape[1]
    half = width // 2
    rows = tokens * top
    members = count // 4
    hot = 2 * rows // count
    cold = (rows - 2 * hot) // (count - 2) + 2
    cap = -(-(2 * hot + 2 * cold) // 16) * 16
    groups = [[j for j in range(count) if j & 6 == mask] for mask in PLANE]

    def exchange(chunks):
        return lax.all_to_all(
            chunks, "expert", split_axis=0, concat_axis=0, tiled=True, axis_index_groups=groups
        )

    id_rows = jnp.zeros((ID_ROWS, model), BF16)
    id_rows = lax.dynamic_update_slice(id_rows, expert_ids.T.astype(BF16), (0, 0))
    near = jnp.concatenate([grad_out, id_rows], 0)
    masks = [0]
    bit = count // 2
    while bit >= 8:
        near = jnp.concatenate([near, swap(near, bit)], 0)
        masks = masks + [mask ^ bit for mask in masks]
        bit //= 2
    far = swap(near, CORE_BIT)
    info = jnp.stack([me] + [(me ^ mask) // 8 for mask in masks]).astype(jnp.int32)

    own_w = lax.all_gather(w2, "dp", axis=2, tiled=True)[0]
    x_w, y_w = swap(own_w, X_BIT), swap(own_w, Y_BIT)
    diag_a, diag_b = swap(x_w[:half], Y_BIT), swap(y_w[half:], X_BIT)

    flat_pre = pre_acts.reshape(rows, 2 * width)
    gate_column = gates.reshape(rows, 1)
    packed, place = pack_hidden(expert_ids.reshape(1, rows), gate_column, flat_pre, members, cap)
    arrived = exchange(packed)

    slopes = packed_slopes(info, near, far, (own_w, x_w, y_w, diag_a, diag_b), cap, tokens, top)
    back = exchange(slopes).reshape(members * cap, width)

    own, x_send, y_send, x_keep, y_keep = weight_partials(
        info, near, far, arrived, cap, tokens, top
    )
    from_x, from_y = swap(x_send, X_BIT), swap(y_send, Y_BIT)
    to_y = (y_keep.astype(F32) + from_x[half:].astype(F32)).astype(BF16)
    to_x = (x_keep.astype(F32) + from_y[half:].astype(F32)).astype(BF16)
    last_a, last_b = swap(to_y, Y_BIT), swap(to_x, X_BIT)
    total = own + jnp.concatenate(
        [
            from_x[:half].astype(F32) + last_a.astype(F32),
            from_y[:half].astype(F32) + last_b.astype(F32),
        ],
        0,
    )
    total = lax.psum_scatter(total, "dp", scatter_dimension=1, tiled=True)

    pre_grad = finish(place.reshape(rows, 1), gate_column, flat_pre, back)
    return pre_grad.reshape(tokens, top, 2 * width), total[None].astype(BF16)


def solution(mesh):
    in_specs = (
        P(("groups", "expert", "dp"), None),
        P(("groups", "expert", "dp"), None),
        P(("groups", "expert", "dp"), None),
        P(("groups", "expert", "dp"), None, None),
        P("expert", None, "dp"),
    )
    out_specs = (P(("groups", "expert", "dp"), None, None), P("expert", "groups", "dp"))
    return jax.shard_map(
        per_device, mesh=mesh, in_specs=in_specs, out_specs=out_specs, check_vma=False
    )
```

time: 289 us -> 147 us (0.51)
  blocking collectives: 97.6 us -> 0 us
  waiting for transfers between devices: 128 us -> 75.8 us
  Pallas kernels: 0 us -> 32.2 us
  other arithmetic: 20.4 us -> 5.98 us
  matrix products: 12.9 us -> 0 us
  starting transfers between devices: 11.2 us -> 23.5 us
  local copies, waits for them, and re-layouts: 16.9 us -> 7.87 us
    all_to_all x2, waiting for transfers between devices: 128 us -> 0.01 us  [exchange(): lax.all_to_all(chunks, 'expert', split_axis=0, concat_axis=0, tiled=True,...]
    all_to_all x1 -> x0, blocking collectives: 97.6 us -> none  [per_device(): lax.all_to_all(grad_buffer.reshape(expert_count, capacity, model_width),...]
    ppermute x0 -> x11, waiting for transfers between devices: none -> 75.8 us  [swap(): return lax.ppermute(value, 'expert', [(j, j ^ bit) for j in range(count)])]
    pallas_call x0 -> x4, Pallas kernels: none -> 32.2 us  [the longest x1 10.5 us: packed_slopes(): pl.pallas_call(lambda *refs: slope_kernel(cap, tokens, top, *refs), grid_...]
    ppermute x0 -> x11, starting transfers between devices: none -> 16 us  [swap(): return lax.ppermute(value, 'expert', [(j, j ^ bit) for j in range(count)])]
    dot_general x2 -> x0, matrix products: 12.9 us -> none  [the longest x1 6.9 us: per_device(): lax.dot_general(arrived_grad, own_weight, (((1,), (1,)), ((), ())), prefe...]
    another operation x3 -> x0, other arithmetic: 9.15 us -> none
    scatter x1 -> x0, other arithmetic: 8.28 us -> none  [per_device(): grad_buffer = jnp.zeros((expert_count * capacity, model_width), jnp.bfloa...]
  transfers between devices with their start and end apart: 2 -> 13, of which waited for: 2 -> 6; matrix products, arithmetic and copies ran while one was open for 5% -> 6% of each run, Pallas kernels for 0% -> 18%
where the time goes in v1:
time: 147 us; the launch traced here: 146 us
  waiting for transfers between devices  75.8 us (52%)
  Pallas kernels  32.2 us (22%)
  starting transfers between devices  23.5 us (16%)
  local copies, waits for them, and re-layouts  7.87 us (5%)
  other arithmetic  5.98 us (4%)
    ppermute x11, waiting for transfers between devices, swap(): return lax.ppermute(value, 'expert', [(j, j ^ bit) for j in range(count)])  75.8 us
    ppermute x11, starting transfers between devices, swap(): return lax.ppermute(value, 'expert', [(j, j ^ bit) for j in range(count)])  16 us
    pallas_call x1, Pallas kernels, packed_slopes(): pl.pallas_call(lambda *refs: slope_kernel(cap, tokens, top, *refs), grid_...  10.5 us
    pallas_call x1, Pallas kernels, weight_partials(): pl.pallas_call(lambda *refs: weight_kernel(cap, tokens, top, *refs), in_s...  9.12 us
    all_to_all x2, starting transfers between devices, exchange(): lax.all_to_all(chunks, 'expert', split_axis=0, concat_axis=0, tiled=True,...  7.58 us
    pallas_call x1, Pallas kernels, pack_hidden(): pl.pallas_call(lambda *refs: pack_kernel(cap, *refs), grid=(members,), in...  6.65 us
    pallas_call x1, Pallas kernels, finish(): pl.pallas_call(finish_kernel, grid=(4,), in_specs=[pl.BlockSpec((tile, 1)...  5.91 us
    unnamed x30, local copies, waits for them, and re-layouts  4.41 us
  transfers between devices with their start and end apart: 13, of which 6 were waited for; matrix products, arithmetic and copies ran while one was open for 6% of the time, Pallas kernels for 18%

profile of v1, /device:TPU:0, one launch (start us, length us, event | category | flops | bytes accessed | tf_op | source)
XLA Modules:
  0.0 146.2 jit_solution(6195836597372609293)
XLA Ops:
  0.6 0.7 convert_bitcast_fusion
  1.3 1.0 pad_maximum_fusion.2
  2.3 4.1 %collective-permute-start = (bf16[144,1024]{1,0:T(8,128)(2,1)S(1)}, bf16[144,1024]{1,0:T(8,128)(2,1)S(1)}, u32[]{:S(2)}, u32[]{:S(2)}) collective-permute-start(bf16[144,1024]{1,0:T(8,128)(2,1)S(1)} %pad_maximum_fusion.2), channel_id=1, source_target_pairs={{0,16},{1,17},{2,18},{3,19},{4,20},{5,21},{6,22},{7,23},{8,24},{9,... | collective-permute-start | bytes 884744 | tf_op jit(solution)/shard_map/ppermute | solution.py:27
  6.4 0.8 copy.9
  7.2 0.8 copy.10
  8.0 1.0 reshape.29.refs_1_.gates_ref
  9.0 0.7 reshape.23.refs_0_
  9.7 6.6 %shard_map.68 = (bf16[8,192,384]{2,1,0:T(8,128)(2,1)}, s32[1,1024]{1,0:T(1,128)}) custom-call(s32[1,1024]{1,0:T(1,128)} %reshape.23.refs_0_, f32[1024,1]{1,0:T(8,128)} %reshape.29.refs_1_.gates_ref, bf16[1024,768]{1,0:T(8,128)(2,1)} %bitcast.16), custom_call_target="tpu_custom_call" | custom-call | flops 1207959552 | bytes 1572864 | tf_op jit(solution)/shard_map/pallas_call | solution.py:70
  16.3 0.0 copy-start
  16.3 3.7 %all-to-all-start.1 = ((bf16[8,192,384]{2,1,0:T(8,128)(2,1)}), bf16[8,192,384]{2,1,0:T(8,128)(2,1)S(1)}, u32[]{:S(2)}, u32[]{:S(2)}) async-start(bf16[8,192,384]{2,1,0:T(8,128)(2,1)} %get-tuple-element.10), calls=%async_computation.1 | async-start | bytes 2359296 | tf_op jit(solution)/shard_map/all_to_all | solution.py:285
  20.0 0.0 collective-permute-done
  20.0 0.0 copy-done
  20.1 0.0 copy-start.12
  20.1 2.0 %collective-permute-start.1 = (bf16[288,1024]{1,0:T(8,128)(2,1)S(1)}, bf16[288,1024]{1,0:T(8,128)(2,1)S(1)}, u32[]{:S(2)}, u32[]{:S(2)}) collective-permute-start(bf16[288,1024]{1,0:T(8,128)(2,1)S(1)} %pad_maximum_fusion.1), channel_id=1, source_target_pairs={{0,8},{1,9},{2,10},{3,11},{4,12},{5,13},{6,14},{7,15},{8,0},{9,1},... | collective-permute-start | bytes 1769480 | tf_op jit(solution)/shard_map/ppermute | solution.py:27
  22.1 32.7 %collective-permute-done.1 = bf16[288,1024]{1,0:T(8,128)(2,1)S(1)} collective-permute-done((bf16[288,1024]{1,0:T(8,128)(2,1)S(1)}, bf16[288,1024]{1,0:T(8,128)(2,1)S(1)}, u32[]{:S(2)}, u32[]{:S(2)}) %collective-permute-start.1) | collective-permute-done | bytes 589856 | tf_op jit(solution)/shard_map/ppermute | solution.py:27
  54.8 0.1 pad_maximum_fusion.refs_1_
  54.8 0.0 copy-start.3
  54.9 0.1 collective-permute-start.2
  54.9 0.0 copy-done.12
  54.9 1.6 %collective-permute-start.3 = (bf16[384,1024]{1,0:T(8,128)(2,1)S(1)}, bf16[384,1024]{1,0:T(8,128)(2,1)S(1)}, u32[]{:S(2)}, u32[]{:S(2)}) collective-permute-start(bf16[384,1024]{1,0:T(8,128)(2,1)S(1)} %bitcast.19), channel_id=1, source_target_pairs={{0,2},{1,3},{2,0},{3,1},{4,6},{5,7},{6,4},{7,5},{8,10},{9,11},{10,... | collective-permute-start | bytes 2359304 | tf_op jit(solution)/shard_map/ppermute | solution.py:27
  56.5 1.5 %collective-permute-start.4 = (bf16[384,1024]{1,0:T(8,128)(2,1)S(1)}, bf16[384,1024]{1,0:T(8,128)(2,1)S(1)}, u32[]{:S(2)}, u32[]{:S(2)}) collective-permute-start(bf16[384,1024]{1,0:T(8,128)(2,1)S(1)} %bitcast.20), channel_id=1, source_target_pairs={{0,4},{1,5},{2,6},{3,7},{4,0},{5,1},{6,2},{7,3},{8,12},{9,13},{10,... | collective-permute-start | bytes 2359304 | tf_op jit(solution)/shard_map/ppermute | solution.py:27
  58.0 16.9 %collective-permute-done.3.refs_4_ = bf16[384,1024]{1,0:T(8,128)(2,1)S(1)} collective-permute-done((bf16[384,1024]{1,0:T(8,128)(2,1)S(1)}, bf16[384,1024]{1,0:T(8,128)(2,1)S(1)}, u32[]{:S(2)}, u32[]{:S(2)}) %collective-permute-start.3) | collective-permute-done | bytes 786464 | tf_op jit(solution)/shard_map/ppermute | solution.py:27
  74.9 0.0 copy-start.9
  74.9 1.6 %collective-permute-start.5 = (bf16[192,1024]{1,0:T(8,128)(2,1)S(1)}, bf16[192,1024]{1,0:T(8,128)(2,1)S(1)}, u32[]{:S(2)}, u32[]{:S(2)}) collective-permute-start(bf16[192,1024]{1,0:T(8,128)(2,1)S(1)} %slice.24), channel_id=1, source_target_pairs={{0,4},{1,5},{2,6},{3,7},{4,0},{5,1},{6,2},{7,3},{8,12},{9,13},{10,... | collective-permute-start | bytes 1179656 | tf_op jit(solution)/shard_map/ppermute | solution.py:27
  76.5 0.0 collective-permute-done.4.refs_5_
  76.5 0.0 copy-start.10
  76.5 1.6 %collective-permute-start.6 = (bf16[192,1024]{1,0:T(8,128)(2,1)S(1)}, bf16[192,1024]{1,0:T(8,128)(2,1)}, u32[]{:S(2)}, u32[]{:S(2)}) collective-permute-start(bf16[192,1024]{1,0:T(8,128)(2,1)S(1)} %slice.25), channel_id=1, source_target_pairs={{0,2},{1,3},{2,0},{3,1},{4,6},{5,7},{6,4},{7,5},{8,10},{9,11},{10,... | collective-permute-start | bytes 1179656 | tf_op jit(solution)/shard_map/ppermute | solution.py:27
  78.1 0.0 copy-done.9
  78.1 0.0 copy-done.10
  78.1 0.7 stack.23.refs_0_
  78.8 0.0 all-to-all-done.1.refs_3_
  78.8 0.0 collective-permute-done.2.refs_2_
  78.8 0.0 copy-done.3
  78.8 1.0 copy-done.2
  79.8 9.1 %shard_map.71 = (f32[384,1024]{1,0:T(8,128)}, bf16[384,1024]{1,0:T(8,128)(2,1)}, bf16[384,1024]{1,0:T(8,128)(2,1)}, bf16[192,1024]{1,0:T(8,128)(2,1)}, bf16[192,1024]{1,0:T(8,128)(2,1)}) custom-call(s32[5]{0:T(128)} %stack.23.refs_0_, bf16[576,1024]{1,0:T(8,128)(2,1)} %copy-done.3, bf16[576,1024]{1,0:T(8,128)(2,1)} %collective-permute-done.2.refs_2_, ...), custom_call_target="tpu_custom_call" | custom-call | flops 3221225472 | bytes 2359296 | tf_op jit(solution)/shard_map/pallas_call | solution.py:216
  88.9 0.8 collective-permute-start.7
  89.7 0.0 collective-permute-done.5.refs_6_
  89.7 0.0 collective-permute-done.6.refs_7_
  89.7 0.8 copy-done.13
  90.5 10.5 %shard_map.69 = bf16[8,192,384]{2,1,0:T(8,128)(2,1)} custom-call(s32[5]{0:T(128)} %stack.23.refs_0_, bf16[576,1024]{1,0:T(8,128)(2,1)} %copy-done.3, bf16[576,1024]{1,0:T(8,128)(2,1)} %collective-permute-done.2.refs_2_, bf16[384,1024]{1,0:T(8,128)(2,1)} %bitcast.18, bf16[384,1024]{1,0:T(8,128)(2,1)} %copy-done.9, bf16[384,1024]{1,0:T(8,128)(2,1)} %copy-done.10, ...), custom_call_target="tpu_custom_call" | custom-call | flops 3221225472 | bytes 2359296 | tf_op jit(solution)/shard_map/pallas_call | solution.py:148
  101.0 3.9 %all-to-all-start = ((bf16[8,192,384]{2,1,0:T(8,128)(2,1)}), bf16[8,192,384]{2,1,0:T(8,128)(2,1)S(1)}, u32[]{:S(2)}, u32[]{:S(2)}) async-start(bf16[8,192,384]{2,1,0:T(8,128)(2,1)} %shard_map.69), calls=%async_computation | async-start | bytes 2359296 | tf_op jit(solution)/shard_map/all_to_all | solution.py:285
  104.9 0.9 collective-permute-start.9
  105.8 1.8 %collective-permute-done.7 = bf16[384,1024]{1,0:T(8,128)(2,1)S(1)} collective-permute-done((bf16[384,1024]{1,0:T(8,128)(2,1)}, bf16[384,1024]{1,0:T(8,128)(2,1)S(1)}, u32[]{:S(2)}, u32[]{:S(2)}) %collective-permute-start.7) | collective-permute-done | bytes 786464 | tf_op jit(solution)/shard_map/ppermute | solution.py:27
  107.6 0.0 copy-done.8
  107.6 0.9 add_convert_fusion.1
  108.5 0.6 collective-permute-start.8
  109.2 16.3 %collective-permute-done.9 = bf16[384,1024]{1,0:T(8,128)(2,1)S(1)} collective-permute-done((bf16[384,1024]{1,0:T(8,128)(2,1)}, bf16[384,1024]{1,0:T(8,128)(2,1)S(1)}, u32[]{:S(2)}, u32[]{:S(2)}) %collective-permute-start.9) | collective-permute-done | bytes 786464 | tf_op jit(solution)/shard_map/ppermute | solution.py:27
  125.5 0.0 copy-done.7
  125.5 1.0 add_convert_fusion
  126.5 1.2 collective-permute-start.10
  127.7 0.0 copy-done.11
  127.8 1.0 copy.12.place_ref
  128.8 0.0 copy-done.5
  128.8 4.7 %collective-permute-done.8 = bf16[192,1024]{1,0:T(8,128)(2,1)S(1)} collective-permute-done((bf16[192,1024]{1,0:T(8,128)(2,1)}, bf16[192,1024]{1,0:T(8,128)(2,1)S(1)}, u32[]{:S(2)}, u32[]{:S(2)}) %collective-permute-start.8) | collective-permute-done | bytes 393248 | tf_op jit(solution)/shard_map/ppermute | solution.py:27
  133.5 0.1 convert_add_fusion.1
  133.6 0.0 copy-start.1
  133.6 3.4 %collective-permute-done.10 = bf16[192,1024]{1,0:T(8,128)(2,1)} collective-permute-done((bf16[192,1024]{1,0:T(8,128)(2,1)}, bf16[192,1024]{1,0:T(8,128)(2,1)}, u32[]{:S(2)}, u32[]{:S(2)}) %collective-permute-start.10) | collective-permute-done | bytes 393248 | tf_op jit(solution)/shard_map/ppermute | solution.py:27
  137.0 0.0 copy-done.6
  137.0 1.1 convert_add_fusion
  138.1 0.0 copy-done.1
  138.1 1.1 fusion.1
  139.2 0.0 all-to-all-done
  139.2 1.0 copy-done.4
  140.3 5.9 %shard_map.70 = bf16[1024,768]{1,0:T(8,128)(2,1)} custom-call(s32[1024,1]{1,0:T(8,128)} %copy.12.place_ref, f32[1024,1]{1,0:T(8,128)} %reshape.29.refs_1_.gates_ref, bf16[1024,768]{1,0:T(8,128)(2,1)} %bitcast.17, bf16[1536,384]{1,0:T(8,128)(2,1)} %bitcast.14), custom_call_target="tpu_custom_call" | custom-call | flops 2415919104 | bytes 3145728 | tf_op jit(solution)/shard_map/pallas_call | solution.py:254
  (12 shorter events, 0.1 us)
Async XLA Ops:
  2.3 17.7 %collective-permute-start = (bf16[144,1024]{1,0:T(8,128)(2,1)S(1)}, bf16[144,1024]{1,0:T(8,128)(2,1)S(1)}, u32[]{:S(2)}, u32[]{:S(2)}) collective-permute-start(bf16[144,1024]{1,0:T(8,128)(2,1)S(1)} %pad_maximum_fusion.2), channel_id=1, source_target_pairs={{0,16},{1,17},{2,18},{3,19},{4,20},{5,21},{6,22},{7,23},{8,24},{9,... | collective-permute-start | bytes 884744 | tf_op jit(solution)/shard_map/ppermute | solution.py:27
  16.3 3.7 %copy-start = (bf16[128,1024]{1,0:T(8,128)(2,1)S(1)}, bf16[128,1024]{1,0:T(8,128)(2,1)}, u32[]{:S(2)}) copy-start(bf16[128,1024]{1,0:T(8,128)(2,1)} %param.5) | copy-start | bytes 786436
  16.3 62.4 %all-to-all-start.1 = ((bf16[8,192,384]{2,1,0:T(8,128)(2,1)}), bf16[8,192,384]{2,1,0:T(8,128)(2,1)S(1)}, u32[]{:S(2)}, u32[]{:S(2)}) async-start(bf16[8,192,384]{2,1,0:T(8,128)(2,1)} %get-tuple-element.10), calls=%async_computation.1 | async-start | bytes 2359296 | tf_op jit(solution)/shard_map/all_to_all | solution.py:285
  20.1 34.8 %copy-start.12 = (bf16[1,384,1024]{2,1,0:T(8,128)(2,1)S(1)}, bf16[1,384,1024]{2,1,0:T(8,128)(2,1)}, u32[]{:S(2)}) copy-start(bf16[1,384,1024]{2,1,0:T(8,128)(2,1)} %param.9) | copy-start | bytes 2359300
  20.1 34.6 %collective-permute-start.1 = (bf16[288,1024]{1,0:T(8,128)(2,1)S(1)}, bf16[288,1024]{1,0:T(8,128)(2,1)S(1)}, u32[]{:S(2)}, u32[]{:S(2)}) collective-permute-start(bf16[288,1024]{1,0:T(8,128)(2,1)S(1)} %pad_maximum_fusion.1), channel_id=1, source_target_pairs={{0,8},{1,9},{2,10},{3,11},{4,12},{5,13},{6,14},{7,15},{8,0},{9,1},... | collective-permute-start | bytes 1769480 | tf_op jit(solution)/shard_map/ppermute | solution.py:27
  54.8 23.9 %copy-start.3 = (bf16[576,1024]{1,0:T(8,128)(2,1)}, bf16[576,1024]{1,0:T(8,128)(2,1)S(1)}, u32[]{:S(2)}) copy-start(bf16[576,1024]{1,0:T(8,128)(2,1)S(1)} %pad_maximum_fusion.refs_1_) | copy-start | bytes 3538948
  54.9 23.9 %collective-permute-start.2 = (bf16[576,1024]{1,0:T(8,128)(2,1)S(1)}, bf16[576,1024]{1,0:T(8,128)(2,1)}, u32[]{:S(2)}, u32[]{:S(2)}) collective-permute-start(bf16[576,1024]{1,0:T(8,128)(2,1)S(1)} %pad_maximum_fusion.refs_1_), channel_id=1, source_target_pairs={{0,1},{1,0},{2,3},{3,2},{4,5},{5,4},{6,7},{7,6},{8,9},{9,8},{10,11... | collective-permute-start | bytes 3538952 | tf_op jit(solution)/shard_map/ppermute | solution.py:27
  54.9 19.9 %collective-permute-start.3 = (bf16[384,1024]{1,0:T(8,128)(2,1)S(1)}, bf16[384,1024]{1,0:T(8,128)(2,1)S(1)}, u32[]{:S(2)}, u32[]{:S(2)}) collective-permute-start(bf16[384,1024]{1,0:T(8,128)(2,1)S(1)} %bitcast.19), channel_id=1, source_target_pairs={{0,2},{1,3},{2,0},{3,1},{4,6},{5,7},{6,4},{7,5},{8,10},{9,11},{10,... | collective-permute-start | bytes 2359304 | tf_op jit(solution)/shard_map/ppermute | solution.py:27
  56.5 20.0 %collective-permute-start.4 = (bf16[384,1024]{1,0:T(8,128)(2,1)S(1)}, bf16[384,1024]{1,0:T(8,128)(2,1)S(1)}, u32[]{:S(2)}, u32[]{:S(2)}) collective-permute-start(bf16[384,1024]{1,0:T(8,128)(2,1)S(1)} %bitcast.20), channel_id=1, source_target_pairs={{0,4},{1,5},{2,6},{3,7},{4,0},{5,1},{6,2},{7,3},{8,12},{9,13},{10,... | collective-permute-start | bytes 2359304 | tf_op jit(solution)/shard_map/ppermute | solution.py:27
  74.9 3.2 %copy-start.9 = (bf16[384,1024]{1,0:T(8,128)(2,1)}, bf16[384,1024]{1,0:T(8,128)(2,1)S(1)}, u32[]{:S(2)}) copy-start(bf16[384,1024]{1,0:T(8,128)(2,1)S(1)} %collective-permute-done.3.refs_4_) | copy-start | bytes 2359300
  74.9 14.8 %collective-permute-start.5 = (bf16[192,1024]{1,0:T(8,128)(2,1)S(1)}, bf16[192,1024]{1,0:T(8,128)(2,1)S(1)}, u32[]{:S(2)}, u32[]{:S(2)}) collective-permute-start(bf16[192,1024]{1,0:T(8,128)(2,1)S(1)} %slice.24), channel_id=1, source_target_pairs={{0,4},{1,5},{2,6},{3,7},{4,0},{5,1},{6,2},{7,3},{8,12},{9,13},{10,... | collective-permute-start | bytes 1179656 | tf_op jit(solution)/shard_map/ppermute | solution.py:27
  76.5 1.6 %copy-start.10 = (bf16[384,1024]{1,0:T(8,128)(2,1)}, bf16[384,1024]{1,0:T(8,128)(2,1)S(1)}, u32[]{:S(2)}) copy-start(bf16[384,1024]{1,0:T(8,128)(2,1)S(1)} %collective-permute-done.4.refs_5_) | copy-start | bytes 2359300
  76.5 13.1 %collective-permute-start.6 = (bf16[192,1024]{1,0:T(8,128)(2,1)S(1)}, bf16[192,1024]{1,0:T(8,128)(2,1)}, u32[]{:S(2)}, u32[]{:S(2)}) collective-permute-start(bf16[192,1024]{1,0:T(8,128)(2,1)S(1)} %slice.25), channel_id=1, source_target_pairs={{0,2},{1,3},{2,0},{3,1},{4,6},{5,7},{6,4},{7,5},{8,10},{9,11},{10,... | collective-permute-start | bytes 1179656 | tf_op jit(solution)/shard_map/ppermute | solution.py:27
  78.8 1.0 copy-start.2
  88.9 18.7 %collective-permute-start.7 = (bf16[384,1024]{1,0:T(8,128)(2,1)}, bf16[384,1024]{1,0:T(8,128)(2,1)S(1)}, u32[]{:S(2)}, u32[]{:S(2)}) collective-permute-start(bf16[384,1024]{1,0:T(8,128)(2,1)} %get-tuple-element.12), channel_id=1, source_target_pairs={{0,2},{1,3},{2,0},{3,1},{4,6},{5,7},{6,4},{7,5},{8,10},{9,11},{10,... | collective-permute-start | bytes 2359304 | tf_op jit(solution)/shard_map/ppermute | solution.py:27
  89.7 0.8 copy-start.13
  101.0 6.7 %copy-start.8 = (bf16[192,1024]{1,0:T(8,128)(2,1)S(1)}, bf16[192,1024]{1,0:T(8,128)(2,1)}, u32[]{:S(2)}) copy-start(bf16[192,1024]{1,0:T(8,128)(2,1)} %get-tuple-element.13) | copy-start | bytes 1179652
  101.0 38.2 %all-to-all-start = ((bf16[8,192,384]{2,1,0:T(8,128)(2,1)}), bf16[8,192,384]{2,1,0:T(8,128)(2,1)S(1)}, u32[]{:S(2)}, u32[]{:S(2)}) async-start(bf16[8,192,384]{2,1,0:T(8,128)(2,1)} %shard_map.69), calls=%async_computation | async-start | bytes 2359296 | tf_op jit(solution)/shard_map/all_to_all | solution.py:285
  104.9 20.6 %copy-start.7 = (bf16[192,1024]{1,0:T(8,128)(2,1)S(1)}, bf16[192,1024]{1,0:T(8,128)(2,1)}, u32[]{:S(2)}) copy-start(bf16[192,1024]{1,0:T(8,128)(2,1)} %get-tuple-element.15) | copy-start | bytes 1179652
  104.9 20.6 %collective-permute-start.9 = (bf16[384,1024]{1,0:T(8,128)(2,1)}, bf16[384,1024]{1,0:T(8,128)(2,1)S(1)}, u32[]{:S(2)}, u32[]{:S(2)}) collective-permute-start(bf16[384,1024]{1,0:T(8,128)(2,1)} %get-tuple-element.14), channel_id=1, source_target_pairs={{0,4},{1,5},{2,6},{3,7},{4,0},{5,1},{6,2},{7,3},{8,12},{9,13},{10,... | collective-permute-start | bytes 2359304 | tf_op jit(solution)/shard_map/ppermute | solution.py:27
  107.6 20.1 %copy-start.11 = (s32[1,1024]{1,0:T(1,128)S(1)}, s32[1,1024]{1,0:T(1,128)}, u32[]{:S(2)}) copy-start(s32[1,1024]{1,0:T(1,128)} %get-tuple-element.9) | copy-start | bytes 12292
  108.5 24.9 %collective-permute-start.8 = (bf16[192,1024]{1,0:T(8,128)(2,1)}, bf16[192,1024]{1,0:T(8,128)(2,1)S(1)}, u32[]{:S(2)}, u32[]{:S(2)}) collective-permute-start(bf16[192,1024]{1,0:T(8,128)(2,1)} %add_convert_fusion.1), channel_id=1, source_target_pairs={{0,4},{1,5},{2,6},{3,7},{4,0},{5,1},{6,2},{7,3},{8,12},{9,13},{10,... | collective-permute-start | bytes 1179656 | tf_op jit(solution)/shard_map/ppermute | solution.py:27
  125.5 3.3 %copy-start.5 = (bf16[384,1024]{1,0:T(8,128)(2,1)}, bf16[384,1024]{1,0:T(8,128)(2,1)S(1)}, u32[]{:S(2)}) copy-start(bf16[384,1024]{1,0:T(8,128)(2,1)S(1)} %collective-permute-done.9) | copy-start | bytes 2359300
  126.5 10.5 %collective-permute-start.10 = (bf16[192,1024]{1,0:T(8,128)(2,1)}, bf16[192,1024]{1,0:T(8,128)(2,1)}, u32[]{:S(2)}, u32[]{:S(2)}) collective-permute-start(bf16[192,1024]{1,0:T(8,128)(2,1)} %add_convert_fusion), channel_id=1, source_target_pairs={{0,2},{1,3},{2,0},{3,1},{4,6},{5,7},{6,4},{7,5},{8,10},{9,11},{10,... | collective-permute-start | bytes 1179656 | tf_op jit(solution)/shard_map/ppermute | solution.py:27
  133.5 3.6 %copy-start.6 = (bf16[384,1024]{1,0:T(8,128)(2,1)S(1)}, bf16[384,1024]{1,0:T(8,128)(2,1)}, u32[]{:S(2)}) copy-start(bf16[384,1024]{1,0:T(8,128)(2,1)} %copy-done.5) | copy-start | bytes 2359300
  133.6 4.6 %copy-start.1 = (f32[384,1024]{1,0:T(8,128)S(1)}, f32[384,1024]{1,0:T(8,128)}, u32[]{:S(2)}) copy-start(f32[384,1024]{1,0:T(8,128)} %get-tuple-element.11) | copy-start | bytes 4718596
  139.2 1.0 copy-start.4

commit v2 on v1

--- a/solution.py
+++ b/solution.py
@@ -295,12 +295,13 @@
         near = jnp.concatenate([near, swap(near, bit)], 0)
         masks = masks + [mask ^ bit for mask in masks]
         bit //= 2
-    far = swap(near, CORE_BIT)
-    info = jnp.stack([me] + [(me ^ mask) // 8 for mask in masks]).astype(jnp.int32)
 
     own_w = lax.all_gather(w2, "dp", axis=2, tiled=True)[0]
     x_w, y_w = swap(own_w, X_BIT), swap(own_w, Y_BIT)
     diag_a, diag_b = swap(x_w[:half], Y_BIT), swap(y_w[half:], X_BIT)
+    near, diag_a, diag_b = lax.optimization_barrier((near, diag_a, diag_b))
+    far = swap(near, CORE_BIT)
+    info = jnp.stack([me] + [(me ^ mask) >> 3 for mask in masks]).astype(jnp.int32)
 
     flat_pre = pre_acts.reshape(rows, 2 * width)
     gate_column = gates.reshape(rows, 1)

time: 147 us -> 129 us (0.88)
  waiting for transfers between devices: 75.8 us -> 58.1 us
  local copies, waits for them, and re-layouts: 7.87 us -> 10.6 us
  starting transfers between devices: 23.5 us -> 21 us
    ppermute x11, waiting for transfers between devices: 75.8 us -> 58.1 us  [swap(): return lax.ppermute(value, 'expert', [(j, j ^ bit) for j in range(count)])]
    ppermute x11, starting transfers between devices: 16 us -> 13.5 us  [swap(): return lax.ppermute(value, 'expert', [(j, j ^ bit) for j in range(count)])]
    slice x2, local copies, waits for them, and re-layouts: 0.05 us -> 2.04 us  [per_device(): diag_a, diag_b = (swap(x_w[:half], Y_BIT), swap(y_w[half:], X_BIT))]
    unnamed x30 -> x24, local copies, waits for them, and re-layouts: 4.41 us -> 5.2 us
  transfers between devices with their start and end apart: 13 -> 13, of which waited for: 6 -> 6; matrix products, arithmetic and copies ran while one was open for 6% -> 9% of each run, Pallas kernels for 18% -> 13%
where the time goes in v2:
time: 129 us; the launch traced here: 128 us
  waiting for transfers between devices  58.1 us (45%)
  Pallas kernels  32.3 us (25%)
  starting transfers between devices  21 us (16%)
  local copies, waits for them, and re-layouts  10.6 us (8%)
  other arithmetic  5.1 us (4%)
    ppermute x11, waiting for transfers between devices, swap(): return lax.ppermute(value, 'expert', [(j, j ^ bit) for j in range(count)])  58.1 us
    ppermute x11, starting transfers between devices, swap(): return lax.ppermute(value, 'expert', [(j, j ^ bit) for j in range(count)])  13.5 us
    pallas_call x1, Pallas kernels, packed_slopes(): pl.pallas_call(lambda *refs: slope_kernel(cap, tokens, top, *refs), grid_...  10.5 us
    pallas_call x1, Pallas kernels, weight_partials(): pl.pallas_call(lambda *refs: weight_kernel(cap, tokens, top, *refs), in_s...  9.17 us
    all_to_all x2, starting transfers between devices, exchange(): lax.all_to_all(chunks, 'expert', split_axis=0, concat_axis=0, tiled=True,...  7.56 us
    pallas_call x1, Pallas kernels, pack_hidden(): pl.pallas_call(lambda *refs: pack_kernel(cap, *refs), grid=(members,), in...  6.67 us
    pallas_call x1, Pallas kernels, finish(): pl.pallas_call(finish_kernel, grid=(4,), in_specs=[pl.BlockSpec((tile, 1)...  5.91 us
    unnamed x24, local copies, waits for them, and re-layouts  5.2 us
  transfers between devices with their start and end apart: 13, of which 6 were waited for; matrix products, arithmetic and copies ran while one was open for 9% of the time, Pallas kernels for 13%

profile of v2, /device:TPU:0, one launch (start us, length us, event | category | flops | bytes accessed | tf_op | source)
XLA Modules:
  0.0 127.9 jit_solution(17483840994218533302)
XLA Ops:
  0.6 3.0 %collective-permute-start.4 = (bf16[384,1024]{1,0:T(8,128)(2,1)}, bf16[384,1024]{1,0:T(8,128)(2,1)}, u32[]{:S(2)}, u32[]{:S(2)}) collective-permute-start(bf16[384,1024]{1,0:T(8,128)(2,1)} %bitcast.18), channel_id=1, source_target_pairs={{0,4},{1,5},{2,6},{3,7},{4,0},{5,1},{6,2},{7,3},{8,12},{9,13},{10,... | collective-permute-start | bytes 2359304 | tf_op jit(solution)/shard_map/ppermute | solution.py:27
  3.7 1.5 %collective-permute-start.2 = (bf16[384,1024]{1,0:T(8,128)(2,1)}, bf16[384,1024]{1,0:T(8,128)(2,1)}, u32[]{:S(2)}, u32[]{:S(2)}) collective-permute-start(bf16[384,1024]{1,0:T(8,128)(2,1)} %bitcast.19), channel_id=1, source_target_pairs={{0,2},{1,3},{2,0},{3,1},{4,6},{5,7},{6,4},{7,5},{8,10},{9,11},{10,... | collective-permute-start | bytes 2359304 | tf_op jit(solution)/shard_map/ppermute | solution.py:27
  5.2 0.7 convert_bitcast_fusion
  5.9 1.0 pad_maximum_fusion.2
  6.8 2.7 %collective-permute-start = (bf16[144,1024]{1,0:T(8,128)(2,1)S(1)}, bf16[144,1024]{1,0:T(8,128)(2,1)S(1)}, u32[]{:S(2)}, u32[]{:S(2)}) collective-permute-start(bf16[144,1024]{1,0:T(8,128)(2,1)S(1)} %pad_maximum_fusion.2), channel_id=1, source_target_pairs={{0,16},{1,17},{2,18},{3,19},{4,20},{5,21},{6,22},{7,23},{8,24},{9,... | collective-permute-start | bytes 884744 | tf_op jit(solution)/shard_map/ppermute | solution.py:27
  9.5 0.8 copy.9
  10.3 0.8 copy.10
  11.1 0.7 reshape.23.refs_0_
  11.7 1.0 reshape.29.refs_1_.gates_ref
  12.7 6.7 %shard_map.68 = (bf16[8,192,384]{2,1,0:T(8,128)(2,1)}, s32[1,1024]{1,0:T(1,128)}) custom-call(s32[1,1024]{1,0:T(1,128)} %reshape.23.refs_0_, f32[1024,1]{1,0:T(8,128)} %reshape.29.refs_1_.gates_ref, bf16[1024,768]{1,0:T(8,128)(2,1)} %bitcast.16), custom_call_target="tpu_custom_call" | custom-call | flops 1207959552 | bytes 1572864 | tf_op jit(solution)/shard_map/pallas_call | solution.py:70
  19.4 0.0 copy-start
  19.4 3.7 %all-to-all-start.1 = ((bf16[8,192,384]{2,1,0:T(8,128)(2,1)}), bf16[8,192,384]{2,1,0:T(8,128)(2,1)S(1)}, u32[]{:S(2)}, u32[]{:S(2)}) async-start(bf16[8,192,384]{2,1,0:T(8,128)(2,1)} %get-tuple-element.16), calls=%async_computation.1 | async-start | bytes 2359296 | tf_op jit(solution)/shard_map/all_to_all | solution.py:285
  23.1 0.0 collective-permute-done
  23.1 0.0 copy-done
  23.2 2.0 %collective-permute-start.1 = (bf16[288,1024]{1,0:T(8,128)(2,1)S(1)}, bf16[288,1024]{1,0:T(8,128)(2,1)S(1)}, u32[]{:S(2)}, u32[]{:S(2)}) collective-permute-start(bf16[288,1024]{1,0:T(8,128)(2,1)S(1)} %pad_maximum_fusion.1), channel_id=1, source_target_pairs={{0,8},{1,9},{2,10},{3,11},{4,12},{5,13},{6,14},{7,15},{8,0},{9,1},... | collective-permute-start | bytes 1769480 | tf_op jit(solution)/shard_map/ppermute | solution.py:27
  25.2 0.0 collective-permute-done.4.refs_5_
  25.2 1.0 slice.25
  26.2 0.6 collective-permute-start.5
  26.8 0.0 collective-permute-done.2.refs_4_
  26.8 1.0 slice.24
  27.8 0.6 collective-permute-start.3
  28.4 29.5 %collective-permute-done.1 = bf16[288,1024]{1,0:T(8,128)(2,1)S(1)} collective-permute-done((bf16[288,1024]{1,0:T(8,128)(2,1)S(1)}, bf16[288,1024]{1,0:T(8,128)(2,1)S(1)}, u32[]{:S(2)}, u32[]{:S(2)}) %collective-permute-start.1) | collective-permute-done | bytes 589856 | tf_op jit(solution)/shard_map/ppermute | solution.py:27
  57.8 0.1 pad_maximum_fusion.refs_1_
  57.9 0.0 copy-start.3
  57.9 0.0 collective-permute-done.5.refs_7_
  57.9 0.0 copy-start.9
  58.0 0.0 collective-permute-done.3.refs_6_
  58.0 0.8 copy-done.9
  58.7 0.0 copy-start.10
  58.7 0.0 collective-permute-start.6
  58.7 0.8 copy-done.10
  59.5 0.7 stack.23.refs_0_
  60.2 0.0 all-to-all-done.1.refs_3_
  60.2 0.0 copy-start.2
  60.2 1.4 %collective-permute-done.6.refs_2_ = bf16[576,1024]{1,0:T(8,128)(2,1)S(1)} collective-permute-done((bf16[576,1024]{1,0:T(8,128)(2,1)S(1)}, bf16[576,1024]{1,0:T(8,128)(2,1)S(1)}, u32[]{:S(2)}, u32[]{:S(2)}) %collective-permute-start.6) | collective-permute-done | bytes 1179680 | tf_op jit(solution)/shard_map/ppermute | solution.py:27
  61.6 0.0 copy-done.3
  61.6 0.0 copy-done.2
  61.6 0.0 copy-start.8
  61.6 1.0 copy-done.8
  62.6 9.2 %shard_map.71 = (f32[384,1024]{1,0:T(8,128)}, bf16[384,1024]{1,0:T(8,128)(2,1)}, bf16[384,1024]{1,0:T(8,128)(2,1)}, bf16[192,1024]{1,0:T(8,128)(2,1)}, bf16[192,1024]{1,0:T(8,128)(2,1)}) custom-call(s32[5]{0:T(128)} %stack.23.refs_0_, bf16[576,1024]{1,0:T(8,128)(2,1)} %copy-done.3, bf16[576,1024]{1,0:T(8,128)(2,1)} %copy-done.8, bf16[8,192,384]{2,1,0:T(8,128)(2,1)} %copy-done.2), custom_call_target="tpu_custom_call" | custom-call | flops 3221225472 | bytes 2359296 | tf_op jit(solution)/shard_map/pallas_call | solution.py:216
  71.8 0.5 collective-permute-start.7
  72.3 10.5 %shard_map.69 = bf16[8,192,384]{2,1,0:T(8,128)(2,1)} custom-call(s32[5]{0:T(128)} %stack.23.refs_0_, bf16[576,1024]{1,0:T(8,128)(2,1)} %copy-done.3, bf16[576,1024]{1,0:T(8,128)(2,1)} %copy-done.8, bf16[384,1024]{1,0:T(8,128)(2,1)} %bitcast.20, bf16[384,1024]{1,0:T(8,128)(2,1)} %collective-permute-done.2.refs_4_, ...), custom_call_target="tpu_custom_call" | custom-call | flops 3221225472 | bytes 2359296 | tf_op jit(solution)/shard_map/pallas_call | solution.py:148
  82.8 3.9 %all-to-all-start = ((bf16[8,192,384]{2,1,0:T(8,128)(2,1)}), bf16[8,192,384]{2,1,0:T(8,128)(2,1)S(1)}, u32[]{:S(2)}, u32[]{:S(2)}) async-start(bf16[8,192,384]{2,1,0:T(8,128)(2,1)} %shard_map.69), calls=%async_computation | async-start | bytes 2359296 | tf_op jit(solution)/shard_map/all_to_all | solution.py:285
  86.7 0.6 collective-permute-start.9
  87.2 4.3 %collective-permute-done.7 = bf16[384,1024]{1,0:T(8,128)(2,1)S(1)} collective-permute-done((bf16[384,1024]{1,0:T(8,128)(2,1)}, bf16[384,1024]{1,0:T(8,128)(2,1)S(1)}, u32[]{:S(2)}, u32[]{:S(2)}) %collective-permute-start.7) | collective-permute-done | bytes 786464 | tf_op jit(solution)/shard_map/ppermute | solution.py:27
  91.6 0.0 copy-done.6
  91.6 0.1 add_convert_fusion.1
  91.7 0.5 collective-permute-start.8
  92.3 15.0 %collective-permute-done.9 = bf16[384,1024]{1,0:T(8,128)(2,1)S(1)} collective-permute-done((bf16[384,1024]{1,0:T(8,128)(2,1)}, bf16[384,1024]{1,0:T(8,128)(2,1)S(1)}, u32[]{:S(2)}, u32[]{:S(2)}) %collective-permute-start.9) | collective-permute-done | bytes 786464 | tf_op jit(solution)/shard_map/ppermute | solution.py:27
  107.3 0.0 copy-done.5
  107.3 0.9 add_convert_fusion
  108.2 1.5 %collective-permute-start.10 = (bf16[192,1024]{1,0:T(8,128)(2,1)}, bf16[192,1024]{1,0:T(8,128)(2,1)}, u32[]{:S(2)}, u32[]{:S(2)}) collective-permute-start(bf16[192,1024]{1,0:T(8,128)(2,1)} %add_convert_fusion), channel_id=1, source_target_pairs={{0,2},{1,3},{2,0},{3,1},{4,6},{5,7},{6,4},{7,5},{8,10},{9,11},{10,... | collective-permute-start | bytes 1179656 | tf_op jit(solution)/shard_map/ppermute | solution.py:27
  109.7 0.0 copy-done.7
  109.7 1.0 copy.12.place_ref
  110.7 4.5 %collective-permute-done.8 = bf16[192,1024]{1,0:T(8,128)(2,1)S(1)} collective-permute-done((bf16[192,1024]{1,0:T(8,128)(2,1)S(1)}, bf16[192,1024]{1,0:T(8,128)(2,1)S(1)}, u32[]{:S(2)}, u32[]{:S(2)}) %collective-permute-start.8) | collective-permute-done | bytes 393248 | tf_op jit(solution)/shard_map/ppermute | solution.py:27
  115.3 0.1 convert_add_fusion.1
  115.4 0.0 copy-start.1
  115.4 3.3 %collective-permute-done.10 = bf16[192,1024]{1,0:T(8,128)(2,1)} collective-permute-done((bf16[192,1024]{1,0:T(8,128)(2,1)}, bf16[192,1024]{1,0:T(8,128)(2,1)}, u32[]{:S(2)}, u32[]{:S(2)}) %collective-permute-start.10) | collective-permute-done | bytes 393248 | tf_op jit(solution)/shard_map/ppermute | solution.py:27
  118.7 1.1 convert_add_fusion
  119.8 0.0 copy-done.1
  119.8 1.1 fusion.1
  120.9 0.0 all-to-all-done
  120.9 1.0 copy-done.4
  122.0 5.9 %shard_map.70 = bf16[1024,768]{1,0:T(8,128)(2,1)} custom-call(s32[1024,1]{1,0:T(8,128)} %copy.12.place_ref, f32[1024,1]{1,0:T(8,128)} %reshape.29.refs_1_.gates_ref, bf16[1024,768]{1,0:T(8,128)(2,1)} %bitcast.17, bf16[1536,384]{1,0:T(8,128)(2,1)} %bitcast.14), custom_call_target="tpu_custom_call" | custom-call | flops 2415919104 | bytes 3145728 | tf_op jit(solution)/shard_map/pallas_call | solution.py:254
  (6 shorter events, 0.1 us)
Async XLA Ops:
  0.6 24.5 %collective-permute-start.4 = (bf16[384,1024]{1,0:T(8,128)(2,1)}, bf16[384,1024]{1,0:T(8,128)(2,1)}, u32[]{:S(2)}, u32[]{:S(2)}) collective-permute-start(bf16[384,1024]{1,0:T(8,128)(2,1)} %bitcast.18), channel_id=1, source_target_pairs={{0,4},{1,5},{2,6},{3,7},{4,0},{5,1},{6,2},{7,3},{8,12},{9,13},{10,... | collective-permute-start | bytes 2359304 | tf_op jit(solution)/shard_map/ppermute | solution.py:27
  3.7 23.1 %collective-permute-start.2 = (bf16[384,1024]{1,0:T(8,128)(2,1)}, bf16[384,1024]{1,0:T(8,128)(2,1)}, u32[]{:S(2)}, u32[]{:S(2)}) collective-permute-start(bf16[384,1024]{1,0:T(8,128)(2,1)} %bitcast.19), channel_id=1, source_target_pairs={{0,2},{1,3},{2,0},{3,1},{4,6},{5,7},{6,4},{7,5},{8,10},{9,11},{10,... | collective-permute-start | bytes 2359304 | tf_op jit(solution)/shard_map/ppermute | solution.py:27
  6.8 16.3 %collective-permute-start = (bf16[144,1024]{1,0:T(8,128)(2,1)S(1)}, bf16[144,1024]{1,0:T(8,128)(2,1)S(1)}, u32[]{:S(2)}, u32[]{:S(2)}) collective-permute-start(bf16[144,1024]{1,0:T(8,128)(2,1)S(1)} %pad_maximum_fusion.2), channel_id=1, source_target_pairs={{0,16},{1,17},{2,18},{3,19},{4,20},{5,21},{6,22},{7,23},{8,24},{9,... | collective-permute-start | bytes 884744 | tf_op jit(solution)/shard_map/ppermute | solution.py:27
  19.4 3.7 %copy-start = (bf16[128,1024]{1,0:T(8,128)(2,1)S(1)}, bf16[128,1024]{1,0:T(8,128)(2,1)}, u32[]{:S(2)}) copy-start(bf16[128,1024]{1,0:T(8,128)(2,1)} %param.5) | copy-start | bytes 786436
  19.4 40.8 %all-to-all-start.1 = ((bf16[8,192,384]{2,1,0:T(8,128)(2,1)}), bf16[8,192,384]{2,1,0:T(8,128)(2,1)S(1)}, u32[]{:S(2)}, u32[]{:S(2)}) async-start(bf16[8,192,384]{2,1,0:T(8,128)(2,1)} %get-tuple-element.16), calls=%async_computation.1 | async-start | bytes 2359296 | tf_op jit(solution)/shard_map/all_to_all | solution.py:285
  23.2 34.7 %collective-permute-start.1 = (bf16[288,1024]{1,0:T(8,128)(2,1)S(1)}, bf16[288,1024]{1,0:T(8,128)(2,1)S(1)}, u32[]{:S(2)}, u32[]{:S(2)}) collective-permute-start(bf16[288,1024]{1,0:T(8,128)(2,1)S(1)} %pad_maximum_fusion.1), channel_id=1, source_target_pairs={{0,8},{1,9},{2,10},{3,11},{4,12},{5,13},{6,14},{7,15},{8,0},{9,1},... | collective-permute-start | bytes 1769480 | tf_op jit(solution)/shard_map/ppermute | solution.py:27
  26.2 31.8 %collective-permute-start.5 = (bf16[192,1024]{1,0:T(8,128)(2,1)S(1)}, bf16[192,1024]{1,0:T(8,128)(2,1)S(1)}, u32[]{:S(2)}, u32[]{:S(2)}) collective-permute-start(bf16[192,1024]{1,0:T(8,128)(2,1)S(1)} %slice.25), channel_id=1, source_target_pairs={{0,2},{1,3},{2,0},{3,1},{4,6},{5,7},{6,4},{7,5},{8,10},{9,11},{10,... | collective-permute-start | bytes 1179656 | tf_op jit(solution)/shard_map/ppermute | solution.py:27
  27.8 30.2 %collective-permute-start.3 = (bf16[192,1024]{1,0:T(8,128)(2,1)S(1)}, bf16[192,1024]{1,0:T(8,128)(2,1)S(1)}, u32[]{:S(2)}, u32[]{:S(2)}) collective-permute-start(bf16[192,1024]{1,0:T(8,128)(2,1)S(1)} %slice.24), channel_id=1, source_target_pairs={{0,4},{1,5},{2,6},{3,7},{4,0},{5,1},{6,2},{7,3},{8,12},{9,13},{10,... | collective-permute-start | bytes 1179656 | tf_op jit(solution)/shard_map/ppermute | solution.py:27
  57.9 3.7 %copy-start.3 = (bf16[576,1024]{1,0:T(8,128)(2,1)}, bf16[576,1024]{1,0:T(8,128)(2,1)S(1)}, u32[]{:S(2)}) copy-start(bf16[576,1024]{1,0:T(8,128)(2,1)S(1)} %pad_maximum_fusion.refs_1_) | copy-start | bytes 3538948
  57.9 0.8 copy-start.9
  58.7 0.8 copy-start.10
  58.7 2.8 %collective-permute-start.6 = (bf16[576,1024]{1,0:T(8,128)(2,1)S(1)}, bf16[576,1024]{1,0:T(8,128)(2,1)S(1)}, u32[]{:S(2)}, u32[]{:S(2)}) collective-permute-start(bf16[576,1024]{1,0:T(8,128)(2,1)S(1)} %pad_maximum_fusion.refs_1_), channel_id=1, source_target_pairs={{0,1},{1,0},{2,3},{3,2},{4,5},{5,4},{6,7},{7,6},{8,9},{9,8},{10,11... | collective-permute-start | bytes 3538952 | tf_op jit(solution)/shard_map/ppermute | solution.py:27
  60.2 1.4 %copy-start.2 = (bf16[8,192,384]{2,1,0:T(8,128)(2,1)}, bf16[8,192,384]{2,1,0:T(8,128)(2,1)S(1)}, u32[]{:S(2)}) copy-start(bf16[8,192,384]{2,1,0:T(8,128)(2,1)S(1)} %all-to-all-done.1.refs_3_) | copy-start | bytes 3538948
  61.6 1.0 copy-start.8
  71.8 19.8 %collective-permute-start.7 = (bf16[384,1024]{1,0:T(8,128)(2,1)}, bf16[384,1024]{1,0:T(8,128)(2,1)S(1)}, u32[]{:S(2)}, u32[]{:S(2)}) collective-permute-start(bf16[384,1024]{1,0:T(8,128)(2,1)} %get-tuple-element.18), channel_id=1, source_target_pairs={{0,2},{1,3},{2,0},{3,1},{4,6},{5,7},{6,4},{7,5},{8,10},{9,11},{10,... | collective-permute-start | bytes 2359304 | tf_op jit(solution)/shard_map/ppermute | solution.py:27
  82.8 8.8 %copy-start.6 = (bf16[192,1024]{1,0:T(8,128)(2,1)S(1)}, bf16[192,1024]{1,0:T(8,128)(2,1)}, u32[]{:S(2)}) copy-start(bf16[192,1024]{1,0:T(8,128)(2,1)} %get-tuple-element.19) | copy-start | bytes 1179652
  82.8 38.1 %all-to-all-start = ((bf16[8,192,384]{2,1,0:T(8,128)(2,1)}), bf16[8,192,384]{2,1,0:T(8,128)(2,1)S(1)}, u32[]{:S(2)}, u32[]{:S(2)}) async-start(bf16[8,192,384]{2,1,0:T(8,128)(2,1)} %shard_map.69), calls=%async_computation | async-start | bytes 2359296 | tf_op jit(solution)/shard_map/all_to_all | solution.py:285
  86.7 20.6 %copy-start.5 = (bf16[192,1024]{1,0:T(8,128)(2,1)S(1)}, bf16[192,1024]{1,0:T(8,128)(2,1)}, u32[]{:S(2)}) copy-start(bf16[192,1024]{1,0:T(8,128)(2,1)} %get-tuple-element.21) | copy-start | bytes 1179652
  86.7 20.6 %collective-permute-start.9 = (bf16[384,1024]{1,0:T(8,128)(2,1)}, bf16[384,1024]{1,0:T(8,128)(2,1)S(1)}, u32[]{:S(2)}, u32[]{:S(2)}) collective-permute-start(bf16[384,1024]{1,0:T(8,128)(2,1)} %get-tuple-element.20), channel_id=1, source_target_pairs={{0,4},{1,5},{2,6},{3,7},{4,0},{5,1},{6,2},{7,3},{8,12},{9,13},{10,... | collective-permute-start | bytes 2359304 | tf_op jit(solution)/shard_map/ppermute | solution.py:27
  91.6 18.1 %copy-start.7 = (s32[1,1024]{1,0:T(1,128)S(1)}, s32[1,1024]{1,0:T(1,128)}, u32[]{:S(2)}) copy-start(s32[1,1024]{1,0:T(1,128)} %get-tuple-element.12) | copy-start | bytes 12292
  91.7 23.5 %collective-permute-start.8 = (bf16[192,1024]{1,0:T(8,128)(2,1)S(1)}, bf16[192,1024]{1,0:T(8,128)(2,1)S(1)}, u32[]{:S(2)}, u32[]{:S(2)}) collective-permute-start(bf16[192,1024]{1,0:T(8,128)(2,1)S(1)} %add_convert_fusion.1), channel_id=1, source_target_pairs={{0,4},{1,5},{2,6},{3,7},{4,0},{5,1},{6,2},{7,3},{8,12},{9,13},{10,... | collective-permute-start | bytes 1179656 | tf_op jit(solution)/shard_map/ppermute | solution.py:27
  108.2 10.5 %collective-permute-start.10 = (bf16[192,1024]{1,0:T(8,128)(2,1)}, bf16[192,1024]{1,0:T(8,128)(2,1)}, u32[]{:S(2)}, u32[]{:S(2)}) collective-permute-start(bf16[192,1024]{1,0:T(8,128)(2,1)} %add_convert_fusion), channel_id=1, source_target_pairs={{0,2},{1,3},{2,0},{3,1},{4,6},{5,7},{6,4},{7,5},{8,10},{9,11},{10,... | collective-permute-start | bytes 1179656 | tf_op jit(solution)/shard_map/ppermute | solution.py:27
  115.4 4.4 %copy-start.1 = (f32[384,1024]{1,0:T(8,128)S(1)}, f32[384,1024]{1,0:T(8,128)}, u32[]{:S(2)}) copy-start(f32[384,1024]{1,0:T(8,128)} %get-tuple-element.17) | copy-start | bytes 4718596
  120.9 1.0 copy-start.4

commit v3 on v0

v3 whole, which is shorter than its diff:
```python
import jax
import jax.numpy as jnp
from jax import lax
from jax.experimental import pallas as pl
from jax.experimental.pallas import tpu as pltpu
from jax.sharding import PartitionSpec as P

X_BIT, Y_BIT, CORE_BIT = 2, 4, 1
PLANE = (0, X_BIT, Y_BIT, X_BIT | Y_BIT)
TAIL = 16
F32, BF16 = jnp.float32, jnp.bfloat16
HIGHEST = lax.Precision.HIGHEST


def params(mebibytes):
    return pltpu.CompilerParams(vmem_limit_bytes=mebibytes * 1024 * 1024)


def cost(flops, moved):
    return pl.CostEstimate(flops=flops, bytes_accessed=moved, transcendentals=0)


def swap(value, bit):
    count = lax.axis_size("expert")
    return lax.ppermute(value, "expert", [(j, j ^ bit) for j in range(count)])


def number(shape, dim):
    return lax.broadcasted_iota(jnp.int32, shape, dim)


def ones_where(condition):
    return condition.astype(F32).astype(BF16)


def dot(a, b):
    return jnp.dot(a, b, preferred_element_type=F32)


def transposed_dot(a, b):
    return lax.dot_general(a, b, (((1,), (1,)), ((), ())), preferred_element_type=F32)


VMEM = pl.BlockSpec(memory_space=pltpu.VMEM)
ANY = pl.BlockSpec(memory_space=pl.ANY)
HBM = pl.BlockSpec(memory_space=pltpu.HBM)
SMEM = pl.BlockSpec(memory_space=pltpu.SMEM)


def pack_kernel(cap, ids_ref, gates_ref, pre_hbm, out_ref, column_ref, pre, sem):
    copy = pltpu.make_async_copy(pre_hbm, pre, sem)
    copy.start()
    members = out_ref.shape[0]
    rows, both = pre.shape
    width = both // 2
    top, tokens = gates_ref.shape
    ids = ids_ref[...]
    member = (ids >> 3) * 2 + (ids & 1)
    hits = jnp.concatenate([(member == q).astype(F32) for q in range(members)], 0)
    size = members * top
    row, col = number((size, size), 0), number((size, size), 1)
    same = row // top == col // top
    earlier = dot(ones_where(same & (col < row)), hits.astype(BF16))
    total = dot(ones_where(same), hits.astype(BF16))
    before = ones_where(number((tokens, tokens), 0) < number((tokens, tokens), 1))
    ranks = hits * (dot(total.astype(BF16), before) + earlier)
    slot = ranks[:top]
    for q in range(1, members):
        slot = slot + ranks[q * top : (q + 1) * top]
    place = member.astype(F32) * cap + slot

    token_of = (number((rows, tokens), 0) // top == number((rows, tokens), 1)).astype(F32)
    wide = lax.dot_general(
        token_of,
        jnp.concatenate([gates_ref[...], place], 0),
        (((1,), (1,)), ((), ())),
        precision=HIGHEST,
        preferred_element_type=F32,
    )
    mine = number((rows, top), 0) % top == number((rows, top), 1)
    gate_column = jnp.sum(jnp.where(mine, wide[:, :top], 0.0), 1, keepdims=True)
    place_column = jnp.sum(jnp.where(mine, wide[:, top:], 0.0), 1, keepdims=True)
    column_ref[...] = jnp.concatenate([gate_column, place_column], 1)
    spread = ones_where(number((tokens, rows), 1) // top == number((tokens, rows), 0))
    labels = jnp.concatenate([slot, member.astype(F32)], 0).astype(BF16)
    wide = dot(labels, spread)
    mine = number((top, rows), 1) % top == number((top, rows), 0)
    slot_line = jnp.sum(jnp.where(mine, wide[:top], 0.0), 0, keepdims=True)
    member_line = jnp.sum(jnp.where(mine, wide[top:], 0.0), 0, keepdims=True)
    place_line = (member_line * cap + slot_line).astype(jnp.int32)

    copy.wait()
    gate_pre = pre[:, :width].astype(F32)
    up_pre = pre[:, width:].astype(F32)
    hidden = (gate_pre * jax.nn.sigmoid(gate_pre) * up_pre * gate_column).astype(BF16)
    line = number((cap, rows), 0)
    tail = number((TAIL, width), 0)
    for q in range(members):
        packed = dot(ones_where(line == place_line - q * cap), hidden)
        first = (q >> 1) * 8 + (q & 1)
        table = [
            jnp.sum(jnp.where(ids == first + mask, slot + 1.0, 0.0), 0, keepdims=True)
            for mask in PLANE
        ]
        rest = jnp.zeros((1, width - tokens), F32)
        upper, lower = jnp.concatenate(table[:3], 1), jnp.concatenate([table[3], rest], 1)
        block = jnp.where(tail == TAIL - 2, upper, jnp.where(tail == TAIL - 1, lower, 0.0))
        out_ref[q, : cap - TAIL] = packed[: cap - TAIL].astype(BF16)
        out_ref[q, cap - TAIL :] = (packed[cap - TAIL :] + block).astype(BF16)


def pack_hidden(ids, gates, flat_pre, members, cap):
    rows, both = flat_pre.shape
    width = both // 2
    return pl.pallas_call(
        lambda *refs: pack_kernel(cap, *refs),
        in_specs=[VMEM, VMEM, HBM],
        out_specs=[VMEM] * 2,
        out_shape=[
            jax.ShapeDtypeStruct((members, cap, width), BF16),
            jax.ShapeDtypeStruct((rows, 2), F32),
        ],
        scratch_shapes=[pltpu.VMEM((rows, both), BF16), pltpu.SemaphoreType.DMA],
        compiler_params=params(60),
        cost_estimate=cost(2 * members * cap * rows * width, 2 * rows * both),
        name="pack_hidden",
    )(ids.T, gates.T, flat_pre)


def picks(chunk, cap, tokens):
    table = chunk[chunk.shape[0] - TAIL :].astype(F32)
    upper, lower = table[TAIL - 2 : TAIL - 1], table[TAIL - 1 :]
    row = (number((cap, tokens), 0) + 1).astype(F32)
    slots = [upper[:, e * tokens : (e + 1) * tokens] for e in range(3)] + [lower[:, :tokens]]
    return slots, row


def pick_for(chunk, me, cap, tokens):
    slots, row = picks(chunk, cap, tokens)
    parts = []
    for mask in PLANE:
        index = ((me ^ mask) >> 1) & 3
        slot = slots[0]
        for e in range(1, 4):
            slot = jnp.where(index == e, slots[e], slot)
        parts.append(ones_where(row == slot))
    return jnp.concatenate(parts, 1)


def gather_copies(sources, target, sem):
    tokens = sources[0].shape[0]
    return [
        pltpu.make_async_copy(ref, target.at[pl.ds(at * tokens, tokens), :], sem.at[at])
        for at, ref in enumerate(sources)
    ]


def place_of(info, at, blocks):
    core = info[0] & 1
    return info[1 + at % blocks] * 2 + (core if at < blocks else 1 - core)


def slope_kernel(cap, count, info, *refs):
    sources, refs = refs[:count], refs[count:]
    w, chunks_ref, out_ref, grads, weights, slopes, chunks, sem, wsem, csem = refs[:7], *refs[7:]
    me = info[0]
    tokens = sources[0].shape[0]
    width = w[0].shape[0]
    half = width // 2
    token_copies = gather_copies(sources, grads, sem)
    starts = (0,) + tuple(width + half * i for i in range(6))
    weight_copies = [
        pltpu.make_async_copy(ref, weights.at[pl.ds(at, ref.shape[0]), :], wsem.at[i])
        for i, (ref, at) in enumerate(zip(w, starts))
    ]
    chunk_copy = pltpu.make_async_copy(chunks_ref.at[:, pl.ds(cap - TAIL, TAIL), :], chunks, csem)
    for copy in token_copies + weight_copies + [chunk_copy]:
        copy.start()
    for copy in token_copies:
        copy.wait()
    for pair in range(2):
        for copy in weight_copies[:3] if pair == 0 else weight_copies[3:]:
            copy.wait()
        two = transposed_dot(
            grads[...], weights[pair * 2 * width : (pair + 1) * 2 * width]
        ).astype(BF16)
        for at in range(count):
            for e in range(2):
                slopes[at, (2 * pair + e) * tokens : (2 * pair + e + 1) * tokens] = two[
                    at * tokens : (at + 1) * tokens, e * width : (e + 1) * width
                ]
    chunk_copy.wait()
    for at in range(count):
        place = place_of(info, at, count // 2)
        pick = pick_for(chunks[place], me, cap, tokens)
        out_ref[place] = dot(pick, slopes[at]).astype(BF16)


def packed_slopes(info, sources, weights, chunks):
    count = len(sources)
    tokens, model = sources[0].shape
    _, cap, width = chunks.shape
    return pl.pallas_call(
        lambda *refs: slope_kernel(cap, count, *refs),
        in_specs=[SMEM] + [ANY] * (count + 8),
        out_specs=VMEM,
        out_shape=jax.ShapeDtypeStruct((count, cap, width), BF16),
        scratch_shapes=[
            pltpu.VMEM((count * tokens, model), BF16),
            pltpu.VMEM((4 * width, model), BF16),
            pltpu.VMEM((count, 4 * tokens, width), BF16),
            pltpu.VMEM((count, TAIL, width), BF16),
            pltpu.SemaphoreType.DMA((count,)),
            pltpu.SemaphoreType.DMA((7,)),
            pltpu.SemaphoreType.DMA,
        ],
        compiler_params=params(60),
        cost_estimate=cost(2 * count * tokens * model * 4 * width, 4 * count * tokens * model),
        name="packed_slopes",
    )(info, *sources, *weights, chunks)


def weight_kernel(cap, count, info, *refs):
    sources, refs = refs[:count], refs[count:]
    hidden, x_send, y_send, own, keep, spread, grads, rows, result, kept, sem, hsem, osem = refs
    me = info[0]
    tokens = sources[0].shape[0]
    width = rows.shape[2]
    half = width // 2
    hidden_copy = pltpu.make_async_copy(hidden, rows, hsem)
    hidden_copy.start()
    token_copies = gather_copies(sources, grads, sem)
    for copy in token_copies:
        copy.start()
    hidden_copy.wait()
    layout = ((2 * width, 2 * width + half), (0, 3 * width), (3 * width + half, width), (half, width + half))
    for at in range(count):
        chunk = rows[place_of(info, at, count // 2)]
        pick = pick_for(chunk, me, cap, tokens)
        wide = dot(chunk.astype(F32).T.astype(BF16), pick).astype(BF16)
        for e in range(4):
            for h in range(2):
                spread[pl.ds(layout[e][h], half), at * tokens : (at + 1) * tokens] = wide[
                    h * half : (h + 1) * half, e * tokens : (e + 1) * tokens
                ]
    for copy in token_copies:
        copy.wait()

    out_copies = []

    def send(source, target):
        copy = pltpu.make_async_copy(source, target, osem.at[len(out_copies)])
        copy.start()
        out_copies.append(copy)

    result[: 2 * width] = dot(spread[: 2 * width], grads[...]).astype(BF16)
    send(result.at[pl.ds(0, width), :], x_send)
    send(result.at[pl.ds(width, width), :], y_send)
    kept[...] = dot(spread[2 * width : 3 * width], grads[...])
    send(kept, own)
    result[2 * width :] = dot(spread[3 * width :], grads[...]).astype(BF16)
    send(result.at[pl.ds(2 * width, width), :], keep)
    for copy in out_copies:
        copy.wait()


def weight_partials(info, sources, hidden):
    count = len(sources)
    tokens, model = sources[0].shape
    _, cap, width = hidden.shape
    every = count * tokens
    return pl.pallas_call(
        lambda *refs: weight_kernel(cap, count, *refs),
        in_specs=[SMEM] + [ANY] * (count + 1),
        out_specs=[ANY] * 4,
        out_shape=[
            jax.ShapeDtypeStruct((width, model), BF16),
            jax.ShapeDtypeStruct((width, model), BF16),
            jax.ShapeDtypeStruct((width, model), F32),
            jax.ShapeDtypeStruct((width, model), BF16),
        ],
        scratch_shapes=[
            pltpu.VMEM((4 * width, every), BF16),
            pltpu.VMEM((every, model), BF16),
            pltpu.VMEM(hidden.shape, BF16),
            pltpu.VMEM((3 * width, model), BF16),
            pltpu.VMEM((width, model), F32),
            pltpu.SemaphoreType.DMA((count,)),
            pltpu.SemaphoreType.DMA,
            pltpu.SemaphoreType.DMA((4,)),
        ],
        compiler_params=params(60),
        cost_estimate=cost(2 * every * model * 4 * width, 4 * every * model),
        name="weight_partials",
    )(info, *sources, hidden)


def finish_kernel(column_ref, pre_ref, back_ref, out_ref):
    rows, both = pre_ref.shape
    width = both // 2
    slots = back_ref.shape[0]
    place = column_ref[:, 1:2].astype(jnp.int32)
    pick = ones_where(number((rows, slots), 1) == place)
    slope = dot(pick, back_ref[...]) * column_ref[:, 0:1]
    gate_pre = pre_ref[:, :width].astype(F32)
    up_pre = pre_ref[:, width:].astype(F32)
    sigma = jax.nn.sigmoid(gate_pre)
    out_ref[:, :width] = (
        slope * up_pre * (sigma * (1.0 + gate_pre * (1.0 - sigma)))
    ).astype(BF16)
    out_ref[:, width:] = (slope * (gate_pre * sigma)).astype(BF16)


def finish(column, flat_pre, back):
    rows, both = flat_pre.shape
    tile = rows // 4
    return pl.pallas_call(
        finish_kernel,
        grid=(4,),
        in_specs=[
            pl.BlockSpec((tile, 2), lambda i: (i, 0)),
            pl.BlockSpec((tile, both), lambda i: (i, 0)),
            pl.BlockSpec(back.shape, lambda i: (0, 0)),
        ],
        out_specs=pl.BlockSpec((tile, both), lambda i: (i, 0)),
        out_shape=jax.ShapeDtypeStruct((rows, both), BF16),
        compiler_params=params(32),
        cost_estimate=cost(rows * both, 4 * rows * both),
        name="finish",
    )(column, flat_pre, back)


def per_device(grad_out, gates, expert_ids, pre_acts, w2):
    count = lax.axis_size("expert")
    me = lax.axis_index("expert")
    tokens, top = expert_ids.shape
    width = w2.shape[1]
    half = width // 2
    rows = tokens * top
    members = count // 4
    hot = 2 * rows // count
    cold = (rows - 2 * hot) // (count - 2) + 2
    cap = -(-(2 * hot + 2 * cold) // 16) * 16
    groups = [[j for j in range(count) if j & 6 == mask] for mask in PLANE]

    def exchange(chunks):
        return lax.all_to_all(
            chunks, "expert", split_axis=0, concat_axis=0, tiled=True, axis_index_groups=groups
        )

    flat_pre = pre_acts.reshape(rows, 2 * width)
    bits = [1 << b for b in reversed(range(3, count.bit_length() - 1))]
    first = [grad_out] + [swap(grad_out, bit) for bit in bits]

    own_w = lax.all_gather(w2, "dp", axis=2, tiled=True)[0]
    upper, lower = own_w[:half], own_w[half:]
    x_a, y_b = swap(upper, X_BIT), swap(lower, Y_BIT)
    diag_a, diag_b = swap(x_a, Y_BIT), swap(y_b, X_BIT)
    x_b, y_a = swap(lower, X_BIT), swap(upper, Y_BIT)

    packed, column = pack_hidden(expert_ids, gates, flat_pre, members, cap)
    masks, path = [0] + bits, {}
    for bit in bits:
        for mask in [m for m in masks if m and not m & bit]:
            masks.append(mask | bit)
            path[mask | bit] = (mask, bit)
    info = jnp.stack([me] + [(me ^ mask) >> 3 for mask in masks]).astype(jnp.int32)

    *first, packed, info = lax.optimization_barrier((*first, packed, info))
    arrived = exchange(packed)
    blocks = dict(zip([0] + bits, first))
    for mask, (known, bit) in path.items():
        blocks[mask] = swap(blocks[known], bit)
    near = list(blocks.values())
    near[-1], x_b, y_a = lax.optimization_barrier((near[-1], x_b, y_a))
    sources = near + [swap(block, CORE_BIT) for block in near]

    x_send, y_send, own, keep = weight_partials(info, sources, arrived)
    slopes = packed_slopes(info, sources, (own_w, x_a, x_b, y_a, y_b, diag_a, diag_b), arrived)
    back = exchange(slopes).reshape(members * cap, width)

    from_x, from_y = swap(x_send, X_BIT), swap(y_send, Y_BIT)
    from_x, from_y = lax.optimization_barrier((from_x, from_y))
    to_y = (keep[half:].astype(F32) + from_x[half:].astype(F32)).astype(BF16)
    to_x = (keep[:half].astype(F32) + from_y[half:].astype(F32)).astype(BF16)
    last_y, last_x = swap(to_y, Y_BIT), swap(to_x, X_BIT)
    total = own + jnp.concatenate(
        [
            from_x[:half].astype(F32) + last_y.astype(F32),
            from_y[:half].astype(F32) + last_x.astype(F32),
        ],
        0,
    )
    total = lax.psum_scatter(total, "dp", scatter_dimension=1, tiled=True)

    pre_grad = finish(column, flat_pre, back)
    return pre_grad.reshape(tokens, top, 2 * width), total[None].astype(BF16)


def solution(mesh):
    in_specs = (
        P(("groups", "expert", "dp"), None),
        P(("groups", "expert", "dp"), None),
        P(("groups", "expert", "dp"), None),
        P(("groups", "expert", "dp"), None, None),
        P("expert", None, "dp"),
    )
    out_specs = (P(("groups", "expert", "dp"), None, None), P("expert", "groups", "dp"))
    return jax.shard_map(
        per_device, mesh=mesh, in_specs=in_specs, out_specs=out_specs, check_vma=False
    )
```

time: 289 us -> 112 us (0.39)
  blocking collectives: 97.6 us -> 0 us
  waiting for transfers between devices: 128 us -> 48.2 us
  Pallas kernels: 0 us -> 28.8 us
  other arithmetic: 20.4 us -> 1.61 us
  starting transfers between devices: 11.2 us -> 29.1 us
  local copies, waits for them, and re-layouts: 16.9 us -> 3.21 us
  matrix products: 12.9 us -> 0 us
    all_to_all x2, waiting for transfers between devices: 128 us -> 14.7 us  [exchange(): lax.all_to_all(chunks, 'expert', split_axis=0, concat_axis=0, tiled=True,...]
    all_to_all x1 -> x0, blocking collectives: 97.6 us -> none  [per_device(): lax.all_to_all(grad_buffer.reshape(expert_count, capacity, model_width),...]
    ppermute x0 -> x17, waiting for transfers between devices: none -> 33.5 us  [swap(): return lax.ppermute(value, 'expert', [(j, j ^ bit) for j in range(count)])]
    pallas_call x0 -> x4, Pallas kernels: none -> 28.8 us  [the longest x1 9.84 us: packed_slopes(): pl.pallas_call(lambda *refs: slope_kernel(cap, count, *refs), in_specs=[S...]
    ppermute x0 -> x17, starting transfers between devices: none -> 19.2 us  [swap(): return lax.ppermute(value, 'expert', [(j, j ^ bit) for j in range(count)])]
    dot_general x2 -> x0, matrix products: 12.9 us -> none  [the longest x1 6.9 us: per_device(): lax.dot_general(arrived_grad, own_weight, (((1,), (1,)), ((), ())), prefe...]
    another operation x3 -> x0, other arithmetic: 9.15 us -> none
    scatter x1 -> x0, other arithmetic: 8.28 us -> none  [per_device(): grad_buffer = jnp.zeros((expert_count * capacity, model_width), jnp.bfloa...]
  transfers between devices with their start and end apart: 2 -> 19, of which waited for: 2 -> 10; matrix products, arithmetic and copies ran while one was open for 5% -> 2% of each run, Pallas kernels for 0% -> 22%
where the time goes in v3:
time: 112 us
  waiting for transfers between devices  48.2 us (43%)
  starting transfers between devices  29.1 us (26%)
  Pallas kernels  28.8 us (26%)
  local copies, waits for them, and re-layouts  3.21 us (3%)
  other arithmetic  1.61 us (1%)
    ppermute x17, waiting for transfers between devices, swap(): return lax.ppermute(value, 'expert', [(j, j ^ bit) for j in range(count)])  33.5 us
    ppermute x17, starting transfers between devices, swap(): return lax.ppermute(value, 'expert', [(j, j ^ bit) for j in range(count)])  19.2 us
    all_to_all x2, waiting for transfers between devices, exchange(): lax.all_to_all(chunks, 'expert', split_axis=0, concat_axis=0, tiled=True,...  14.7 us
    all_to_all x2, starting transfers between devices, exchange(): lax.all_to_all(chunks, 'expert', split_axis=0, concat_axis=0, tiled=True,...  9.93 us
    pallas_call x1, Pallas kernels, packed_slopes(): pl.pallas_call(lambda *refs: slope_kernel(cap, count, *refs), in_specs=[S...  9.84 us
    pallas_call x1, Pallas kernels, weight_partials(): pl.pallas_call(lambda *refs: weight_kernel(cap, count, *refs), in_specs=[...  8.17 us
    pallas_call x1, Pallas kernels, pack_hidden(): pl.pallas_call(lambda *refs: pack_kernel(cap, *refs), in_specs=[VMEM, VME...  7.13 us
    pallas_call x1, Pallas kernels, finish(): pl.pallas_call(finish_kernel, grid=(4,), in_specs=[pl.BlockSpec((tile, 2)...  3.64 us
  transfers between devices with their start and end apart: 19, of which 10 were waited for; matrix products, arithmetic and copies ran while one was open for 2% of the time, Pallas kernels for 22%

profile of v3, /device:TPU:0, one launch (start us, length us, event | category | flops | bytes accessed | tf_op | source)
XLA Modules:
  0.0 111.8 jit_solution(9837039110337112162)
XLA Ops:
  0.6 4.1 %collective-permute-start = (bf16[128,1024]{1,0:T(8,128)(2,1)}, bf16[128,1024]{1,0:T(8,128)(2,1)S(1)}, u32[]{:S(2)}, u32[]{:S(2)}) collective-permute-start(bf16[128,1024]{1,0:T(8,128)(2,1)} %refs_1_.1), channel_id=1, source_target_pairs={{0,16},{1,17},{2,18},{3,19},{4,20},{5,21},{6,22},{7,23},{8,24},{9,... | collective-permute-start | bytes 786440 | tf_op jit(solution)/shard_map/ppermute | solution.py:25
  4.7 1.6 %collective-permute-start.1 = (bf16[128,1024]{1,0:T(8,128)(2,1)}, bf16[128,1024]{1,0:T(8,128)(2,1)S(1)}, u32[]{:S(2)}, u32[]{:S(2)}) collective-permute-start(bf16[128,1024]{1,0:T(8,128)(2,1)} %refs_1_.1), channel_id=1, source_target_pairs={{0,8},{1,9},{2,10},{3,11},{4,12},{5,13},{6,14},{7,15},{8,0},{9,1},... | collective-permute-start | bytes 786440 | tf_op jit(solution)/shard_map/ppermute | solution.py:25
  6.3 0.7 stack.24.refs_0_
  7.0 7.1 %pack_hidden.1 = (bf16[8,192,384]{2,1,0:T(8,128)(2,1)}, f32[1024,2]{1,0:T(8,128)}) custom-call(s32[8,128]{1,0:T(8,128)} %bitcast.22, f32[8,128]{1,0:T(8,128)} %bitcast.23, bf16[1024,768]{1,0:T(8,128)(2,1)} %bitcast.18), custom_call_target="tpu_custom_call" | custom-call | flops 1207959552 | bytes 1572864 | tf_op jit(solution)/shard_map/pack_hidden/pallas_call | solution.py:115
  14.1 0.0 copy-start.4
  14.1 2.9 %collective-permute-done.refs_2_ = bf16[128,1024]{1,0:T(8,128)(2,1)S(1)} collective-permute-done((bf16[128,1024]{1,0:T(8,128)(2,1)}, bf16[128,1024]{1,0:T(8,128)(2,1)S(1)}, u32[]{:S(2)}, u32[]{:S(2)}) %collective-permute-start) | collective-permute-done | bytes 262176 | tf_op jit(solution)/shard_map/ppermute | solution.py:25
  17.0 0.2 collective-permute-done.1.refs_3_
  17.2 4.7 %all-to-all-start = ((bf16[8,192,384]{2,1,0:T(8,128)(2,1)}), bf16[8,192,384]{2,1,0:T(8,128)(2,1)S(1)}, u32[]{:S(2)}, u32[]{:S(2)}) async-start(bf16[8,192,384]{2,1,0:T(8,128)(2,1)} %get-tuple-element.27), calls=%async_computation | async-start | bytes 2359296 | tf_op jit(solution)/shard_map/all_to_all | solution.py:347
  21.8 0.0 copy-done.4
  21.8 0.1 slice_bitcast_fusion
  21.9 1.6 %collective-permute-start.4 = (bf16[192,1024]{1,0:T(8,128)(2,1)S(1)}, bf16[192,1024]{1,0:T(8,128)(2,1)S(1)}, u32[]{:S(2)}, u32[]{:S(2)}) collective-permute-start(bf16[192,1024]{1,0:T(8,128)(2,1)S(1)} %get-tuple-element.36), channel_id=1, source_target_pairs={{0,4},{1,5},{2,6},{3,7},{4,0},{5,1},{6,2},{7,3},{8,12},{9,13},{10,... | collective-permute-start | bytes 1179656 | tf_op jit(solution)/shard_map/ppermute | solution.py:25
  23.5 1.5 %collective-permute-start.3 = (bf16[192,1024]{1,0:T(8,128)(2,1)S(1)}, bf16[192,1024]{1,0:T(8,128)(2,1)S(1)}, u32[]{:S(2)}, u32[]{:S(2)}) collective-permute-start(bf16[192,1024]{1,0:T(8,128)(2,1)S(1)} %get-tuple-element.37), channel_id=1, source_target_pairs={{0,2},{1,3},{2,0},{3,1},{4,6},{5,7},{6,4},{7,5},{8,10},{9,11},{10,... | collective-permute-start | bytes 1179656 | tf_op jit(solution)/shard_map/ppermute | solution.py:25
  25.0 0.5 collective-permute-start.9
  25.5 2.0 %collective-permute-start.2 = (bf16[128,1024]{1,0:T(8,128)(2,1)S(1)}, bf16[128,1024]{1,0:T(8,128)(2,1)S(1)}, u32[]{:S(2)}, u32[]{:S(2)}) collective-permute-start(bf16[128,1024]{1,0:T(8,128)(2,1)S(1)} %collective-permute-done.refs_2_), channel_id=1, source_target_pairs={{0,8},{1,9},{2,10},{3,11},{4,12},{5,13},{6,14},{7,15},{8,0},{9,1},... | collective-permute-start | bytes 786440 | tf_op jit(solution)/shard_map/ppermute | solution.py:25
  27.5 0.5 collective-permute-start.10
  28.0 5.8 %collective-permute-done.4.refs_12_ = bf16[192,1024]{1,0:T(8,128)(2,1)S(1)} collective-permute-done((bf16[192,1024]{1,0:T(8,128)(2,1)S(1)}, bf16[192,1024]{1,0:T(8,128)(2,1)S(1)}, u32[]{:S(2)}, u32[]{:S(2)}) %collective-permute-start.4) | collective-permute-done | bytes 393248 | tf_op jit(solution)/shard_map/ppermute | solution.py:25
  33.9 0.0 copy-done.8
  33.9 0.0 collective-permute-start.5
  33.9 1.5 %collective-permute-done.3.refs_11_ = bf16[192,1024]{1,0:T(8,128)(2,1)S(1)} collective-permute-done((bf16[192,1024]{1,0:T(8,128)(2,1)S(1)}, bf16[192,1024]{1,0:T(8,128)(2,1)S(1)}, u32[]{:S(2)}, u32[]{:S(2)}) %collective-permute-start.3) | collective-permute-done | bytes 393248 | tf_op jit(solution)/shard_map/ppermute | solution.py:25
  35.4 0.0 copy-done.9
  35.4 0.0 collective-permute-start.6
  35.5 12.1 %collective-permute-done.2.refs_4_ = bf16[128,1024]{1,0:T(8,128)(2,1)S(1)} collective-permute-done((bf16[128,1024]{1,0:T(8,128)(2,1)S(1)}, bf16[128,1024]{1,0:T(8,128)(2,1)S(1)}, u32[]{:S(2)}, u32[]{:S(2)}) %collective-permute-start.2) | collective-permute-done | bytes 262176 | tf_op jit(solution)/shard_map/ppermute | solution.py:25
  47.6 0.0 copy-done.10
  47.6 0.0 collective-permute-start.7
  47.6 0.0 collective-permute-done.9.refs_10_
  47.6 0.5 collective-permute-start.8
  48.1 0.0 collective-permute-done.10.refs_13_
  48.1 1.5 %collective-permute-start.11 = (bf16[192,1024]{1,0:T(8,128)(2,1)}, bf16[192,1024]{1,0:T(8,128)(2,1)}, u32[]{:S(2)}, u32[]{:S(2)}) collective-permute-start(bf16[192,1024]{1,0:T(8,128)(2,1)} %collective-permute-done.9.refs_10_), channel_id=1, source_target_pairs={{0,4},{1,5},{2,6},{3,7},{4,0},{5,1},{6,2},{7,3},{8,12},{9,13},{10,... | collective-permute-start | bytes 1179656 | tf_op jit(solution)/shard_map/ppermute | solution.py:25
  49.6 0.0 collective-permute-done.5.refs_5_
  49.6 1.5 %collective-permute-start.12 = (bf16[192,1024]{1,0:T(8,128)(2,1)}, bf16[192,1024]{1,0:T(8,128)(2,1)}, u32[]{:S(2)}, u32[]{:S(2)}) collective-permute-start(bf16[192,1024]{1,0:T(8,128)(2,1)} %collective-permute-done.10.refs_13_), channel_id=1, source_target_pairs={{0,2},{1,3},{2,0},{3,1},{4,6},{5,7},{6,4},{7,5},{8,10},{9,11},{10,... | collective-permute-start | bytes 1179656 | tf_op jit(solution)/shard_map/ppermute | solution.py:25
  51.1 0.0 collective-permute-done.7.refs_7_
  51.1 0.0 collective-permute-done.6.refs_6_
  51.1 0.7 copy-done.14
  51.8 0.0 collective-permute-done.8.refs_8_
  51.8 0.0 all-to-all-done.refs_16_.refs_9_
  51.8 0.0 copy-done.11
  51.8 0.0 copy-done.12
  51.8 0.7 copy-done.13
  52.5 1.0 copy-done.3
  53.6 8.2 %weight_partials.1 = (bf16[384,1024]{1,0:T(8,128)(2,1)}, bf16[384,1024]{1,0:T(8,128)(2,1)}, f32[384,1024]{1,0:T(8,128)}, bf16[384,1024]{1,0:T(8,128)(2,1)}) custom-call(s32[6]{0:T(128)} %stack.24.refs_0_, bf16[128,1024]{1,0:T(8,128)(2,1)} %refs_1_.1, bf16[128,1024]{1,0:T(8,128)(2,1)} %copy-done.9, bf16[128,1024]{1,0:T(8,128)(2,1)} %copy-done.10, ...), custom_call_target="tpu_custom_call" | custom-call | flops 3221225472 | bytes 4194304 | tf_op jit(solution)/shard_map/weight_partials/pallas_call | solution.py:272
  61.8 0.0 copy-done.6
  61.8 0.0 copy-done.7
  61.8 0.6 collective-permute-start.13
  62.4 1.2 %collective-permute-start.14 = (bf16[384,1024]{1,0:T(8,128)(2,1)}, bf16[384,1024]{1,0:T(8,128)(2,1)S(1)}, u32[]{:S(2)}, u32[]{:S(2)}) collective-permute-start(bf16[384,1024]{1,0:T(8,128)(2,1)} %get-tuple-element.30), channel_id=1, source_target_pairs={{0,4},{1,5},{2,6},{3,7},{4,0},{5,1},{6,2},{7,3},{8,12},{9,13},{10,... | collective-permute-start | bytes 2359304 | tf_op jit(solution)/shard_map/ppermute | solution.py:25
  63.6 0.0 collective-permute-done.11.refs_14_
  63.6 0.0 collective-permute-done.12.refs_15_
  63.6 9.8 %packed_slopes.1 = bf16[8,192,384]{2,1,0:T(8,128)(2,1)} custom-call(s32[6]{0:T(128)} %stack.24.refs_0_, bf16[128,1024]{1,0:T(8,128)(2,1)} %refs_1_.1, bf16[128,1024]{1,0:T(8,128)(2,1)} %copy-done.9, bf16[128,1024]{1,0:T(8,128)(2,1)} %copy-done.10, bf16[128,1024]{1,0:T(8,128)(2,1)} %copy-done.11, bf16[128,1024]{1,0:T(8,128)(2,1)} %copy-done.12, ...), custom_call_target="tpu_custom_call" | custom-call | flops 3221225472 | bytes 4194304 | tf_op jit(solution)/shard_map/packed_slopes/pallas_call | solution.py:203
  73.4 5.3 %all-to-all-start.1 = ((bf16[8,192,384]{2,1,0:T(8,128)(2,1)}), bf16[8,192,384]{2,1,0:T(8,128)(2,1)S(1)}, u32[]{:S(2)}, u32[]{:S(2)}) async-start(bf16[8,192,384]{2,1,0:T(8,128)(2,1)} %packed_slopes.1), calls=%async_computation.1 | async-start | bytes 2359296 | tf_op jit(solution)/shard_map/all_to_all | solution.py:347
  78.7 2.3 %collective-permute-done.13 = bf16[384,1024]{1,0:T(8,128)(2,1)S(1)} collective-permute-done((bf16[384,1024]{1,0:T(8,128)(2,1)}, bf16[384,1024]{1,0:T(8,128)(2,1)S(1)}, u32[]{:S(2)}, u32[]{:S(2)}) %collective-permute-start.13) | collective-permute-done | bytes 786464 | tf_op jit(solution)/shard_map/ppermute | solution.py:25
  81.0 0.3 collective-permute-done.14
  81.3 0.0 copy-done.5
  81.3 0.3 add_convert_fusion.1
  81.6 1.4 %collective-permute-start.15 = (bf16[192,1024]{1,0:T(8,128)(2,1)S(1)}, bf16[192,1024]{1,0:T(8,128)(2,1)S(1)}, u32[]{:S(2)}, u32[]{:S(2)}) collective-permute-start(bf16[192,1024]{1,0:T(8,128)(2,1)S(1)} %get-tuple-element.34), channel_id=1, source_target_pairs={{0,4},{1,5},{2,6},{3,7},{4,0},{5,1},{6,2},{7,3},{8,12},{9,13},{10,... | collective-permute-start | bytes 1179656 | tf_op jit(solution)/shard_map/ppermute | solution.py:25
  83.0 0.7 collective-permute-start.16
  83.7 7.4 %collective-permute-done.15 = bf16[192,1024]{1,0:T(8,128)(2,1)S(1)} collective-permute-done((bf16[192,1024]{1,0:T(8,128)(2,1)S(1)}, bf16[192,1024]{1,0:T(8,128)(2,1)S(1)}, u32[]{:S(2)}, u32[]{:S(2)}) %collective-permute-start.15) | collective-permute-done | bytes 393248 | tf_op jit(solution)/shard_map/ppermute | solution.py:25
  91.0 0.1 convert_add_fusion.1
  91.1 1.0 collective-permute-done.16
  92.1 0.1 convert_add_fusion
  92.3 0.0 copy-start
  92.3 0.0 copy-start.1
  92.3 1.1 fusion.1
  93.4 14.7 %all-to-all-done.1 = bf16[8,192,384]{2,1,0:T(8,128)(2,1)S(1)} async-done(((bf16[8,192,384]{2,1,0:T(8,128)(2,1)}), bf16[8,192,384]{2,1,0:T(8,128)(2,1)S(1)}, u32[]{:S(2)}, u32[]{:S(2)}) %all-to-all-start.1) | async-done | bytes 1179680 | tf_op jit(solution)/shard_map/all_to_all | solution.py:347
  108.1 0.0 copy-done
  108.1 3.6 %finish.1 = bf16[1024,768]{1,0:T(8,128)(2,1)} custom-call(f32[1024,2]{1,0:T(8,128)S(1)} %copy-done.1, bf16[1024,768]{1,0:T(8,128)(2,1)S(1)} %bitcast.19, bf16[1536,384]{1,0:T(8,128)(2,1)S(1)} %bitcast.17), custom_call_target="tpu_custom_call" | custom-call | flops 786432 | bytes 3145728 | tf_op jit(solution)/shard_map/finish/pallas_call | solution.py:317
  (14 shorter events, 0.0 us)
Async XLA Ops:
  0.6 16.3 %collective-permute-start = (bf16[128,1024]{1,0:T(8,128)(2,1)}, bf16[128,1024]{1,0:T(8,128)(2,1)S(1)}, u32[]{:S(2)}, u32[]{:S(2)}) collective-permute-start(bf16[128,1024]{1,0:T(8,128)(2,1)} %refs_1_.1), channel_id=1, source_target_pairs={{0,16},{1,17},{2,18},{3,19},{4,20},{5,21},{6,22},{7,23},{8,24},{9,... | collective-permute-start | bytes 786440 | tf_op jit(solution)/shard_map/ppermute | solution.py:25
  4.7 12.4 %collective-permute-start.1 = (bf16[128,1024]{1,0:T(8,128)(2,1)}, bf16[128,1024]{1,0:T(8,128)(2,1)S(1)}, u32[]{:S(2)}, u32[]{:S(2)}) collective-permute-start(bf16[128,1024]{1,0:T(8,128)(2,1)} %refs_1_.1), channel_id=1, source_target_pairs={{0,8},{1,9},{2,10},{3,11},{4,12},{5,13},{6,14},{7,15},{8,0},{9,1},... | collective-permute-start | bytes 786440 | tf_op jit(solution)/shard_map/ppermute | solution.py:25
  14.1 7.7 %copy-start.4 = (bf16[1,384,1024]{2,1,0:T(8,128)(2,1)S(1)}, bf16[1,384,1024]{2,1,0:T(8,128)(2,1)}, u32[]{:S(2)}) copy-start(bf16[1,384,1024]{2,1,0:T(8,128)(2,1)} %param.9) | copy-start | bytes 2359300
  17.0 18.5 %copy-start.9 = (bf16[128,1024]{1,0:T(8,128)(2,1)}, bf16[128,1024]{1,0:T(8,128)(2,1)S(1)}, u32[]{:S(2)}) copy-start(bf16[128,1024]{1,0:T(8,128)(2,1)S(1)} %collective-permute-done.refs_2_) | copy-start | bytes 786436
  17.2 30.4 %copy-start.10 = (bf16[128,1024]{1,0:T(8,128)(2,1)}, bf16[128,1024]{1,0:T(8,128)(2,1)S(1)}, u32[]{:S(2)}) copy-start(bf16[128,1024]{1,0:T(8,128)(2,1)S(1)} %collective-permute-done.1.refs_3_) | copy-start | bytes 786436
  17.2 16.7 %copy-start.8 = (bf16[128,1024]{1,0:T(8,128)(2,1)S(1)}, bf16[128,1024]{1,0:T(8,128)(2,1)}, u32[]{:S(2)}) copy-start(bf16[128,1024]{1,0:T(8,128)(2,1)} %refs_1_.1) | copy-start | bytes 786436
  17.2 34.7 %all-to-all-start = ((bf16[8,192,384]{2,1,0:T(8,128)(2,1)}), bf16[8,192,384]{2,1,0:T(8,128)(2,1)S(1)}, u32[]{:S(2)}, u32[]{:S(2)}) async-start(bf16[8,192,384]{2,1,0:T(8,128)(2,1)} %get-tuple-element.27), calls=%async_computation | async-start | bytes 2359296 | tf_op jit(solution)/shard_map/all_to_all | solution.py:347
  21.9 12.0 %collective-permute-start.4 = (bf16[192,1024]{1,0:T(8,128)(2,1)S(1)}, bf16[192,1024]{1,0:T(8,128)(2,1)S(1)}, u32[]{:S(2)}, u32[]{:S(2)}) collective-permute-start(bf16[192,1024]{1,0:T(8,128)(2,1)S(1)} %get-tuple-element.36), channel_id=1, source_target_pairs={{0,4},{1,5},{2,6},{3,7},{4,0},{5,1},{6,2},{7,3},{8,12},{9,13},{10,... | collective-permute-start | bytes 1179656 | tf_op jit(solution)/shard_map/ppermute | solution.py:25
  23.5 11.9 %collective-permute-start.3 = (bf16[192,1024]{1,0:T(8,128)(2,1)S(1)}, bf16[192,1024]{1,0:T(8,128)(2,1)S(1)}, u32[]{:S(2)}, u32[]{:S(2)}) collective-permute-start(bf16[192,1024]{1,0:T(8,128)(2,1)S(1)} %get-tuple-element.37), channel_id=1, source_target_pairs={{0,2},{1,3},{2,0},{3,1},{4,6},{5,7},{6,4},{7,5},{8,10},{9,11},{10,... | collective-permute-start | bytes 1179656 | tf_op jit(solution)/shard_map/ppermute | solution.py:25
  25.0 22.6 %collective-permute-start.9 = (bf16[192,1024]{1,0:T(8,128)(2,1)S(1)}, bf16[192,1024]{1,0:T(8,128)(2,1)}, u32[]{:S(2)}, u32[]{:S(2)}) collective-permute-start(bf16[192,1024]{1,0:T(8,128)(2,1)S(1)} %get-tuple-element.36), channel_id=1, source_target_pairs={{0,2},{1,3},{2,0},{3,1},{4,6},{5,7},{6,4},{7,5},{8,10},{9,11},{10,... | collective-permute-start | bytes 1179656 | tf_op jit(solution)/shard_map/ppermute | solution.py:25
  25.5 22.0 %collective-permute-start.2 = (bf16[128,1024]{1,0:T(8,128)(2,1)S(1)}, bf16[128,1024]{1,0:T(8,128)(2,1)S(1)}, u32[]{:S(2)}, u32[]{:S(2)}) collective-permute-start(bf16[128,1024]{1,0:T(8,128)(2,1)S(1)} %collective-permute-done.refs_2_), channel_id=1, source_target_pairs={{0,8},{1,9},{2,10},{3,11},{4,12},{5,13},{6,14},{7,15},{8,0},{9,1},... | collective-permute-start | bytes 786440 | tf_op jit(solution)/shard_map/ppermute | solution.py:25
  27.5 20.6 %collective-permute-start.10 = (bf16[192,1024]{1,0:T(8,128)(2,1)S(1)}, bf16[192,1024]{1,0:T(8,128)(2,1)}, u32[]{:S(2)}, u32[]{:S(2)}) collective-permute-start(bf16[192,1024]{1,0:T(8,128)(2,1)S(1)} %get-tuple-element.37), channel_id=1, source_target_pairs={{0,4},{1,5},{2,6},{3,7},{4,0},{5,1},{6,2},{7,3},{8,12},{9,13},{10,... | collective-permute-start | bytes 1179656 | tf_op jit(solution)/shard_map/ppermute | solution.py:25
  33.9 27.9 %copy-start.6 = (bf16[192,1024]{1,0:T(8,128)(2,1)}, bf16[192,1024]{1,0:T(8,128)(2,1)S(1)}, u32[]{:S(2)}) copy-start(bf16[192,1024]{1,0:T(8,128)(2,1)S(1)} %collective-permute-done.4.refs_12_) | copy-start | bytes 1179652
  33.9 15.7 %collective-permute-start.5 = (bf16[128,1024]{1,0:T(8,128)(2,1)S(1)}, bf16[128,1024]{1,0:T(8,128)(2,1)S(1)}, u32[]{:S(2)}, u32[]{:S(2)}) collective-permute-start(bf16[128,1024]{1,0:T(8,128)(2,1)S(1)} %copy-done.8), channel_id=1, source_target_pairs={{0,1},{1,0},{2,3},{3,2},{4,5},{5,4},{6,7},{7,6},{8,9},{9,8},{10,11... | collective-permute-start | bytes 786440 | tf_op jit(solution)/shard_map/ppermute | solution.py:25
  35.4 26.3 %copy-start.7 = (bf16[192,1024]{1,0:T(8,128)(2,1)}, bf16[192,1024]{1,0:T(8,128)(2,1)S(1)}, u32[]{:S(2)}) copy-start(bf16[192,1024]{1,0:T(8,128)(2,1)S(1)} %collective-permute-done.3.refs_11_) | copy-start | bytes 1179652
  35.4 15.7 %collective-permute-start.6 = (bf16[128,1024]{1,0:T(8,128)(2,1)S(1)}, bf16[128,1024]{1,0:T(8,128)(2,1)S(1)}, u32[]{:S(2)}, u32[]{:S(2)}) collective-permute-start(bf16[128,1024]{1,0:T(8,128)(2,1)S(1)} %collective-permute-done.refs_2_), channel_id=1, source_target_pairs={{0,1},{1,0},{2,3},{3,2},{4,5},{5,4},{6,7},{7,6},{8,9},{9,8},{10,11... | collective-permute-start | bytes 786440 | tf_op jit(solution)/shard_map/ppermute | solution.py:25
  47.6 4.3 %copy-start.11 = (bf16[128,1024]{1,0:T(8,128)(2,1)}, bf16[128,1024]{1,0:T(8,128)(2,1)S(1)}, u32[]{:S(2)}) copy-start(bf16[128,1024]{1,0:T(8,128)(2,1)S(1)} %collective-permute-done.2.refs_4_) | copy-start | bytes 786436
  47.6 3.5 %collective-permute-start.7 = (bf16[128,1024]{1,0:T(8,128)(2,1)S(1)}, bf16[128,1024]{1,0:T(8,128)(2,1)S(1)}, u32[]{:S(2)}, u32[]{:S(2)}) collective-permute-start(bf16[128,1024]{1,0:T(8,128)(2,1)S(1)} %collective-permute-done.1.refs_3_), channel_id=1, source_target_pairs={{0,1},{1,0},{2,3},{3,2},{4,5},{5,4},{6,7},{7,6},{8,9},{9,8},{10,11... | collective-permute-start | bytes 786440 | tf_op jit(solution)/shard_map/ppermute | solution.py:25
  47.6 4.2 %collective-permute-start.8 = (bf16[128,1024]{1,0:T(8,128)(2,1)S(1)}, bf16[128,1024]{1,0:T(8,128)(2,1)}, u32[]{:S(2)}, u32[]{:S(2)}) collective-permute-start(bf16[128,1024]{1,0:T(8,128)(2,1)S(1)} %collective-permute-done.2.refs_4_), channel_id=1, source_target_pairs={{0,1},{1,0},{2,3},{3,2},{4,5},{5,4},{6,7},{7,6},{8,9},{9,8},{10,11... | collective-permute-start | bytes 786440 | tf_op jit(solution)/shard_map/ppermute | solution.py:25
  48.1 15.5 %collective-permute-start.11 = (bf16[192,1024]{1,0:T(8,128)(2,1)}, bf16[192,1024]{1,0:T(8,128)(2,1)}, u32[]{:S(2)}, u32[]{:S(2)}) collective-permute-start(bf16[192,1024]{1,0:T(8,128)(2,1)} %collective-permute-done.9.refs_10_), channel_id=1, source_target_pairs={{0,4},{1,5},{2,6},{3,7},{4,0},{5,1},{6,2},{7,3},{8,12},{9,13},{10,... | collective-permute-start | bytes 1179656 | tf_op jit(solution)/shard_map/ppermute | solution.py:25
  49.6 2.2 %copy-start.12 = (bf16[128,1024]{1,0:T(8,128)(2,1)}, bf16[128,1024]{1,0:T(8,128)(2,1)S(1)}, u32[]{:S(2)}) copy-start(bf16[128,1024]{1,0:T(8,128)(2,1)S(1)} %collective-permute-done.5.refs_5_) | copy-start | bytes 786436
  49.6 14.0 %collective-permute-start.12 = (bf16[192,1024]{1,0:T(8,128)(2,1)}, bf16[192,1024]{1,0:T(8,128)(2,1)}, u32[]{:S(2)}, u32[]{:S(2)}) collective-permute-start(bf16[192,1024]{1,0:T(8,128)(2,1)} %collective-permute-done.10.refs_13_), channel_id=1, source_target_pairs={{0,2},{1,3},{2,0},{3,1},{4,6},{5,7},{6,4},{7,5},{8,10},{9,11},{10,... | collective-permute-start | bytes 1179656 | tf_op jit(solution)/shard_map/ppermute | solution.py:25
  51.1 0.7 copy-start.14
  51.8 0.7 copy-start.13
  52.5 1.0 copy-start.3
  61.8 19.2 %collective-permute-start.13 = (bf16[384,1024]{1,0:T(8,128)(2,1)}, bf16[384,1024]{1,0:T(8,128)(2,1)S(1)}, u32[]{:S(2)}, u32[]{:S(2)}) collective-permute-start(bf16[384,1024]{1,0:T(8,128)(2,1)} %get-tuple-element.29), channel_id=1, source_target_pairs={{0,2},{1,3},{2,0},{3,1},{4,6},{5,7},{6,4},{7,5},{8,10},{9,11},{10,... | collective-permute-start | bytes 2359304 | tf_op jit(solution)/shard_map/ppermute | solution.py:25
  62.4 18.9 %collective-permute-start.14 = (bf16[384,1024]{1,0:T(8,128)(2,1)}, bf16[384,1024]{1,0:T(8,128)(2,1)S(1)}, u32[]{:S(2)}, u32[]{:S(2)}) collective-permute-start(bf16[384,1024]{1,0:T(8,128)(2,1)} %get-tuple-element.30), channel_id=1, source_target_pairs={{0,4},{1,5},{2,6},{3,7},{4,0},{5,1},{6,2},{7,3},{8,12},{9,13},{10,... | collective-permute-start | bytes 2359304 | tf_op jit(solution)/shard_map/ppermute | solution.py:25
  73.4 7.8 %copy-start.5 = (bf16[384,1024]{1,0:T(8,128)(2,1)S(1)}, bf16[384,1024]{1,0:T(8,128)(2,1)}, u32[]{:S(2)}) copy-start(bf16[384,1024]{1,0:T(8,128)(2,1)} %get-tuple-element.32) | copy-start | bytes 2359300
  73.4 34.7 %all-to-all-start.1 = ((bf16[8,192,384]{2,1,0:T(8,128)(2,1)}), bf16[8,192,384]{2,1,0:T(8,128)(2,1)S(1)}, u32[]{:S(2)}, u32[]{:S(2)}) async-start(bf16[8,192,384]{2,1,0:T(8,128)(2,1)} %packed_slopes.1), calls=%async_computation.1 | async-start | bytes 2359296 | tf_op jit(solution)/shard_map/all_to_all | solution.py:347
  81.6 9.4 %collective-permute-start.15 = (bf16[192,1024]{1,0:T(8,128)(2,1)S(1)}, bf16[192,1024]{1,0:T(8,128)(2,1)S(1)}, u32[]{:S(2)}, u32[]{:S(2)}) collective-permute-start(bf16[192,1024]{1,0:T(8,128)(2,1)S(1)} %get-tuple-element.34), channel_id=1, source_target_pairs={{0,4},{1,5},{2,6},{3,7},{4,0},{5,1},{6,2},{7,3},{8,12},{9,13},{10,... | collective-permute-start | bytes 1179656 | tf_op jit(solution)/shard_map/ppermute | solution.py:25
  83.0 9.3 %copy-start.2 = (f32[384,1024]{1,0:T(8,128)S(1)}, f32[384,1024]{1,0:T(8,128)}, u32[]{:S(2)}) copy-start(f32[384,1024]{1,0:T(8,128)} %get-tuple-element.28) | copy-start | bytes 4718596
  83.0 9.2 %collective-permute-start.16 = (bf16[192,1024]{1,0:T(8,128)(2,1)S(1)}, bf16[192,1024]{1,0:T(8,128)(2,1)S(1)}, u32[]{:S(2)}, u32[]{:S(2)}) collective-permute-start(bf16[192,1024]{1,0:T(8,128)(2,1)S(1)} %get-tuple-element.35), channel_id=1, source_target_pairs={{0,2},{1,3},{2,0},{3,1},{4,6},{5,7},{6,4},{7,5},{8,10},{9,11},{10,... | collective-permute-start | bytes 1179656 | tf_op jit(solution)/shard_map/ppermute | solution.py:25
  92.3 15.8 %copy-start = (bf16[128,8,768]{2,1,0:T(8,128)(2,1)S(1)}, bf16[128,8,768]{2,1,0:T(8,128)(2,1)}, u32[]{:S(2)}) copy-start(bf16[128,8,768]{2,1,0:T(8,128)(2,1)} %param.8) | copy-start | bytes 4718596
  92.3 15.8 %copy-start.1 = (f32[1024,2]{1,0:T(8,128)S(1)}, f32[1024,2]{1,0:T(8,128)}, u32[]{:S(2)}) copy-start(f32[1024,2]{1,0:T(8,128)} %get-tuple-element.18.column_ref) | copy-start | bytes 24580

commit v4 on v3

v4 whole, which is shorter than its diff:
```python
import jax
import jax.numpy as jnp
from jax import lax
from jax.experimental import pallas as pl
from jax.experimental.pallas import tpu as pltpu
from jax.sharding import PartitionSpec as P

X_BIT, Y_BIT, CORE_BIT = 2, 4, 1
PLANE = (0, X_BIT, Y_BIT, X_BIT | Y_BIT)
TAIL = 16
F32, BF16 = jnp.float32, jnp.bfloat16
HIGHEST = lax.Precision.HIGHEST


def params(mebibytes):
    return pltpu.CompilerParams(vmem_limit_bytes=mebibytes * 1024 * 1024)


def cost(flops, moved):
    return pl.CostEstimate(flops=flops, bytes_accessed=moved, transcendentals=0)


def swap(value, bit):
    count = lax.axis_size("expert")
    return lax.ppermute(value, "expert", [(j, j ^ bit) for j in range(count)])


def number(shape, dim):
    return lax.broadcasted_iota(jnp.int32, shape, dim)


def ones_where(condition):
    return condition.astype(F32).astype(BF16)


def dot(a, b):
    return jnp.dot(a, b, preferred_element_type=F32)


def transposed_dot(a, b):
    return lax.dot_general(a, b, (((1,), (1,)), ((), ())), preferred_element_type=F32)


VMEM = pl.BlockSpec(memory_space=pltpu.VMEM)
ANY = pl.BlockSpec(memory_space=pl.ANY)
HBM = pl.BlockSpec(memory_space=pltpu.HBM)
SMEM = pl.BlockSpec(memory_space=pltpu.SMEM)


def spread_line(tokens, rows):
    shift = (rows // tokens).bit_length() - 1
    return ones_where((number((tokens, rows), 1) >> shift) == number((tokens, rows), 0))


def column_of(values, rows):
    top, tokens = values.shape
    shift = top.bit_length() - 1
    high = values.astype(BF16)
    rest = values - high.astype(F32)
    middle = rest.astype(BF16)
    low = (rest - middle.astype(F32)).astype(BF16)
    token_of = ones_where((number((rows, tokens), 0) >> shift) == number((rows, tokens), 1))
    wide = transposed_dot(token_of, jnp.concatenate([high, middle, low], 0))
    wide = wide[:, :top] + (wide[:, top : 2 * top] + wide[:, 2 * top :])
    mine = (number((rows, top), 0) & (top - 1)) == number((rows, top), 1)
    return jnp.sum(jnp.where(mine, wide, 0.0), 1, keepdims=True)


def pack_kernel(cap, ids_ref, gates_ref, pre_hbm, out_ref, place_ref, pre, picks_ref, sem):
    copy = pltpu.make_async_copy(pre_hbm, pre, sem)
    copy.start()
    members = out_ref.shape[0]
    rows, both = pre.shape
    width = both // 2
    top, tokens = gates_ref.shape
    ids = ids_ref[...]
    member = (ids >> 3) * 2 + (ids & 1)
    hits = jnp.concatenate([(member == q).astype(F32) for q in range(members)], 0)
    size = members * top
    shift = top.bit_length() - 1
    row, col = number((size, size), 0), number((size, size), 1)
    same = (row >> shift) == (col >> shift)
    earlier = dot(ones_where(same & (col < row)), hits.astype(BF16))
    total = dot(ones_where(same), hits.astype(BF16))
    before = ones_where(number((tokens, tokens), 0) < number((tokens, tokens), 1))
    ranks = hits * (dot(total.astype(BF16), before) + earlier)
    slot = ranks[:top]
    for q in range(1, members):
        slot = slot + ranks[q * top : (q + 1) * top]
    place = member.astype(F32) * cap + slot

    gate_column = column_of(gates_ref[...], rows)
    wide = dot(jnp.concatenate([slot, member.astype(F32)], 0).astype(BF16), spread_line(tokens, rows))
    mine = (number((top, rows), 1) & (top - 1)) == number((top, rows), 0)
    slot_line = jnp.sum(jnp.where(mine, wide[:top], 0.0), 0, keepdims=True)
    member_line = jnp.sum(jnp.where(mine, wide[top:], 0.0), 0, keepdims=True)
    place_line = (member_line * cap + slot_line).astype(jnp.int32)
    for q in range(members):
        picks_ref[q * cap : (q + 1) * cap] = ones_where(
            number((cap, rows), 0) == place_line - q * cap
        )
    place_ref[...] = jnp.concatenate([slot, member.astype(F32)], 0)

    copy.wait()
    gate_pre = pre[:, :width].astype(F32)
    up_pre = pre[:, width:].astype(F32)
    hidden = (gate_pre * jax.nn.sigmoid(gate_pre) * up_pre * gate_column).astype(BF16)
    every = dot(picks_ref[...], hidden)
    tail = number((TAIL, width), 0)
    for q in range(members):
        packed = every[q * cap : (q + 1) * cap]
        first = (q >> 1) * 8 + (q & 1)
        table = [
            jnp.sum(jnp.where(ids == first + mask, slot + 1.0, 0.0), 0, keepdims=True)
            for mask in PLANE
        ]
        rest = jnp.zeros((1, width - tokens), F32)
        upper, lower = jnp.concatenate(table[:3], 1), jnp.concatenate([table[3], rest], 1)
        block = jnp.where(tail == TAIL - 2, upper, jnp.where(tail == TAIL - 1, lower, 0.0))
        out_ref[q, : cap - TAIL] = packed[: cap - TAIL].astype(BF16)
        out_ref[q, cap - TAIL :] = (packed[cap - TAIL :] + block).astype(BF16)


def pack_hidden(ids, gates, flat_pre, members, cap):
    rows, both = flat_pre.shape
    width = both // 2
    return pl.pallas_call(
        lambda *refs: pack_kernel(cap, *refs),
        in_specs=[VMEM, VMEM, HBM],
        out_specs=[VMEM] * 2,
        out_shape=[
            jax.ShapeDtypeStruct((members, cap, width), BF16),
            jax.ShapeDtypeStruct((2 * gates.shape[1], gates.shape[0]), F32),
        ],
        scratch_shapes=[
            pltpu.VMEM((rows, both), BF16),
            pltpu.VMEM((members * cap, rows), BF16),
            pltpu.SemaphoreType.DMA,
        ],
        compiler_params=params(60),
        cost_estimate=cost(2 * members * cap * rows * width, 2 * rows * both),
        name="pack_hidden",
    )(ids.T, gates.T, flat_pre)


def columns_kernel(cap, place_ref, gates_ref, out_ref):
    top = gates_ref.shape[0]
    rows = out_ref.shape[0]
    place = place_ref[top:] * cap + place_ref[:top]
    out_ref[...] = jnp.concatenate(
        [column_of(gates_ref[...], rows), column_of(place, rows)], 1
    )


def columns(place, gates, cap):
    return pl.pallas_call(
        lambda *refs: columns_kernel(cap, *refs),
        in_specs=[VMEM] * 2,
        out_specs=VMEM,
        out_shape=jax.ShapeDtypeStruct((gates.size, 2), F32),
        compiler_params=params(16),
        name="columns",
    )(place, gates.T)


def picks(chunk, cap, tokens):
    table = chunk[chunk.shape[0] - TAIL :].astype(F32)
    upper, lower = table[TAIL - 2 : TAIL - 1], table[TAIL - 1 :]
    row = (number((cap, tokens), 0) + 1).astype(F32)
    slots = [upper[:, e * tokens : (e + 1) * tokens] for e in range(3)] + [lower[:, :tokens]]
    return slots, row


def pick_for(chunk, me, cap, tokens):
    slots, row = picks(chunk, cap, tokens)
    parts = []
    for mask in PLANE:
        index = ((me ^ mask) >> 1) & 3
        slot = slots[0]
        for e in range(1, 4):
            slot = jnp.where(index == e, slots[e], slot)
        parts.append(ones_where(row == slot))
    return jnp.concatenate(parts, 1)


def gather_copies(sources, target, sem):
    tokens = sources[0].shape[0]
    return [
        pltpu.make_async_copy(ref, target.at[pl.ds(at * tokens, tokens), :], sem.at[at])
        for at, ref in enumerate(sources)
    ]


def place_of(info, at, blocks):
    core = info[0] & 1
    return info[1 + at % blocks] * 2 + (core if at < blocks else 1 - core)


def middle_kernel(cap, count, info, *refs):
    sources, w, refs = refs[:count], refs[count : count + 7], refs[count + 7 :]
    hidden, out_ref, x_diag, y_diag, x_own, y_own, rest, *refs = refs
    grads, weights, rows, spread, pick, slopes, packed, result, sem, wsem, hsem, osem, psem = refs
    me = info[0]
    tokens = sources[0].shape[0]
    width = rows.shape[2]
    half = width // 2
    hidden_copy = pltpu.make_async_copy(hidden, rows, hsem)
    token_copies = gather_copies(sources, grads, sem)
    starts = (0,) + tuple(width + half * i for i in range(6))
    weight_copies = [
        pltpu.make_async_copy(ref, weights.at[pl.ds(at, ref.shape[0]), :], wsem.at[i])
        for i, (ref, at) in enumerate(zip(w, starts))
    ]
    for copy in [hidden_copy] + token_copies + weight_copies:
        copy.start()
    hidden_copy.wait()
    layout = (
        (2 * width, 2 * width + half),
        (width, 3 * width),
        (3 * width + half, width + half),
        (0, half),
    )
    places = [place_of(info, at, count // 2) for at in range(count)]
    for at in range(count):
        chunk = rows[places[at]]
        pick[at] = pick_for(chunk, me, cap, tokens)
        wide = dot(chunk.astype(F32).T.astype(BF16), pick[at]).astype(BF16)
        for e in range(4):
            for h in range(2):
                spread[pl.ds(layout[e][h], half), at * tokens : (at + 1) * tokens] = wide[
                    h * half : (h + 1) * half, e * tokens : (e + 1) * tokens
                ]
    copies = [pltpu.make_async_copy(spread.at[pl.ds(2 * width, 2 * width), :], rest, osem.at[4])]
    copies[0].start()
    for copy in token_copies:
        copy.wait()
    result[...] = dot(spread[: 2 * width], grads[...]).astype(BF16)
    for i, target in enumerate((x_diag, y_diag, x_own, y_own)):
        copy = pltpu.make_async_copy(result.at[pl.ds(i * half, half), :], target, osem.at[i])
        copy.start()
        copies.append(copy)
    for copy in weight_copies:
        copy.wait()
    for first in range(0, count, 2):
        both = transposed_dot(
            grads[first * tokens : (first + 2) * tokens], weights[...]
        ).astype(BF16)
        for at in (first, first + 1):
            side = both[(at - first) * tokens : (at - first + 1) * tokens]
            for e in range(4):
                slopes[at, e * tokens : (e + 1) * tokens] = side[:, e * width : (e + 1) * width]
            packed[at] = dot(pick[at], slopes[at]).astype(BF16)
            copy = pltpu.make_async_copy(packed.at[at], out_ref.at[places[at]], psem.at[at])
            copy.start()
            copies.append(copy)
    for copy in copies:
        copy.wait()


def middle(info, sources, weights, hidden):
    count = len(sources)
    tokens, model = sources[0].shape
    _, cap, width = hidden.shape
    every = count * tokens
    return pl.pallas_call(
        lambda *refs: middle_kernel(cap, count, *refs),
        in_specs=[SMEM] + [ANY] * (count + 8),
        out_specs=[ANY] * 6,
        out_shape=[jax.ShapeDtypeStruct(hidden.shape, BF16)]
        + [jax.ShapeDtypeStruct((width // 2, model), BF16)] * 4
        + [jax.ShapeDtypeStruct((2 * width, every), BF16)],
        scratch_shapes=[
            pltpu.VMEM((every, model), BF16),
            pltpu.VMEM((4 * width, model), BF16),
            pltpu.VMEM(hidden.shape, BF16),
            pltpu.VMEM((4 * width, every), BF16),
            pltpu.VMEM((count, cap, 4 * tokens), BF16),
            pltpu.VMEM((count, 4 * tokens, width), BF16),
            pltpu.VMEM(hidden.shape, BF16),
            pltpu.VMEM((2 * width, model), BF16),
            pltpu.SemaphoreType.DMA((count,)),
            pltpu.SemaphoreType.DMA((7,)),
            pltpu.SemaphoreType.DMA,
            pltpu.SemaphoreType.DMA((5,)),
            pltpu.SemaphoreType.DMA((count,)),
        ],
        compiler_params=params(52),
        cost_estimate=cost(2 * every * model * 6 * width, 4 * every * model),
        name="middle",
    )(info, *sources, *weights, hidden)


def keep_kernel(count, *refs):
    sources, refs = refs[:count], refs[count:]
    rest, own, keep, spread, grads, result, kept, sem, rsem, osem = refs
    width = kept.shape[0]
    rest_copy = pltpu.make_async_copy(rest, spread, rsem)
    copies = [rest_copy] + gather_copies(sources, grads, sem)
    for copy in copies:
        copy.start()
    for copy in copies:
        copy.wait()
    result[...] = dot(spread[width:], grads[...]).astype(BF16)
    keep_copy = pltpu.make_async_copy(result, keep, osem.at[0])
    keep_copy.start()
    kept[...] = dot(spread[:width], grads[...])
    own_copy = pltpu.make_async_copy(kept, own, osem.at[1])
    own_copy.start()
    keep_copy.wait()
    own_copy.wait()


def keep_partials(sources, rest):
    count = len(sources)
    tokens, model = sources[0].shape
    width, every = rest.shape[0] // 2, count * tokens
    return pl.pallas_call(
        lambda *refs: keep_kernel(count, *refs),
        in_specs=[ANY] * (count + 1),
        out_specs=[ANY] * 2,
        out_shape=[
            jax.ShapeDtypeStruct((width, model), F32),
            jax.ShapeDtypeStruct((width, model), BF16),
        ],
        scratch_shapes=[
            pltpu.VMEM((2 * width, every), BF16),
            pltpu.VMEM((every, model), BF16),
            pltpu.VMEM((width, model), BF16),
            pltpu.VMEM((width, model), F32),
            pltpu.SemaphoreType.DMA((count,)),
            pltpu.SemaphoreType.DMA,
            pltpu.SemaphoreType.DMA((2,)),
        ],
        compiler_params=params(52),
        cost_estimate=cost(2 * every * model * 2 * width, 4 * every * model),
        name="keep_partials",
    )(*sources, rest)


def finish_kernel(column_ref, pre_ref, back_ref, out_ref):
    rows, both = pre_ref.shape
    width = both // 2
    slots = back_ref.shape[0]
    place = column_ref[:, 1:2].astype(jnp.int32)
    pick = ones_where(number((rows, slots), 1) == place)
    slope = dot(pick, back_ref[...]) * column_ref[:, 0:1]
    gate_pre = pre_ref[:, :width].astype(F32)
    up_pre = pre_ref[:, width:].astype(F32)
    sigma = jax.nn.sigmoid(gate_pre)
    out_ref[:, :width] = (
        slope * up_pre * (sigma * (1.0 + gate_pre * (1.0 - sigma)))
    ).astype(BF16)
    out_ref[:, width:] = (slope * (gate_pre * sigma)).astype(BF16)


def finish(column, flat_pre, back):
    rows, both = flat_pre.shape
    tile = rows // 4
    return pl.pallas_call(
        finish_kernel,
        grid=(4,),
        in_specs=[
            pl.BlockSpec((tile, 2), lambda i: (i, 0)),
            pl.BlockSpec((tile, both), lambda i: (i, 0)),
            pl.BlockSpec(back.shape, lambda i: (0, 0)),
        ],
        out_specs=pl.BlockSpec((tile, both), lambda i: (i, 0)),
        out_shape=jax.ShapeDtypeStruct((rows, both), BF16),
        compiler_params=params(32),
        cost_estimate=cost(rows * both, 4 * rows * both),
        name="finish",
    )(column, flat_pre, back)


def per_device(grad_out, gates, expert_ids, pre_acts, w2):
    count = lax.axis_size("expert")
    me = lax.axis_index("expert")
    tokens, top = expert_ids.shape
    width = w2.shape[1]
    half = width // 2
    rows = tokens * top
    members = count // 4
    hot = 2 * rows // count
    cold = (rows - 2 * hot) // (count - 2) + 2
    cap = -(-(2 * hot + 2 * cold) // 16) * 16
    groups = [[j for j in range(count) if j & 6 == mask] for mask in PLANE]

    def exchange(chunks):
        return lax.all_to_all(
            chunks, "expert", split_axis=0, concat_axis=0, tiled=True, axis_index_groups=groups
        )

    flat_pre = pre_acts.reshape(rows, 2 * width)
    bits = [1 << b for b in reversed(range(3, count.bit_length() - 1))]
    first = [grad_out] + [swap(grad_out, bit) for bit in bits]

    own_w = lax.all_gather(w2, "dp", axis=2, tiled=True)[0]
    upper, lower = own_w[:half], own_w[half:]
    x_a, y_b = swap(upper, X_BIT), swap(lower, Y_BIT)
    diag_a, diag_b = swap(x_a, Y_BIT), swap(y_b, X_BIT)
    x_b, y_a = swap(lower, X_BIT), swap(upper, Y_BIT)

    packed, place = pack_hidden(expert_ids, gates, flat_pre, members, cap)
    masks, path = [0] + bits, {}
    for bit in bits:
        for mask in [m for m in masks if m > bit and not m & bit and m | bit not in masks]:
            masks.append(mask | bit)
            path[mask | bit] = (mask, bit)
    info = jnp.stack([me] + [(me ^ mask) >> 3 for mask in masks]).astype(jnp.int32)

    *first, packed, info = lax.optimization_barrier((*first, packed, info))
    arrived = exchange(packed)
    blocks = dict(zip([0] + bits, first))
    for mask, (known, bit) in path.items():
        blocks[mask] = swap(blocks[known], bit)
    near = list(blocks.values())
    near[-1], x_b, y_a, diag_a, diag_b = lax.optimization_barrier((near[-1], x_b, y_a, diag_a, diag_b))
    sources = near + [swap(block, CORE_BIT) for block in near]

    slopes, x_diag, y_diag, x_own, y_own, rest = middle(
        info, sources, (own_w, x_a, x_b, y_a, y_b, diag_a, diag_b), arrived
    )
    back = exchange(slopes).reshape(members * cap, width)
    own, keep = keep_partials(sources, rest)

    from_x, from_y = swap(x_diag, X_BIT), swap(y_diag, Y_BIT)
    mine_x, mine_y = swap(x_own, X_BIT), swap(y_own, Y_BIT)
    mine_x, mine_y = lax.optimization_barrier((mine_x, mine_y))
    from_x, from_y = lax.optimization_barrier((from_x, from_y))
    to_y = (keep[half:].astype(F32) + from_x.astype(F32)).astype(BF16)
    to_x = (keep[:half].astype(F32) + from_y.astype(F32)).astype(BF16)
    last_y, last_x = swap(to_y, Y_BIT), swap(to_x, X_BIT)
    total = own + jnp.concatenate(
        [
            mine_x.astype(F32) + last_y.astype(F32),
            mine_y.astype(F32) + last_x.astype(F32),
        ],
        0,
    )
    total = lax.psum_scatter(total, "dp", scatter_dimension=1, tiled=True)

    column = columns(place, gates, cap)
    pre_grad = finish(column, flat_pre, back)
    return pre_grad.reshape(tokens, top, 2 * width), total[None].astype(BF16)


def solution(mesh):
    in_specs = (
        P(("groups", "expert", "dp"), None),
        P(("groups", "expert", "dp"), None),
        P(("groups", "expert", "dp"), None),
        P(("groups", "expert", "dp"), None, None),
        P("expert", None, "dp"),
    )
    out_specs = (P(("groups", "expert", "dp"), None, None), P("expert", "groups", "dp"))
    return jax.shard_map(
        per_device, mesh=mesh, in_specs=in_specs, out_specs=out_specs, check_vma=False
    )
```

time: 112 us -> 104 us (0.929)
  waiting for transfers between devices: 48.2 us -> 41 us
  Pallas kernels: 28.8 us -> 25.3 us
  starting transfers between devices: 29.1 us -> 31.6 us
    all_to_all x2, waiting for transfers between devices: 14.7 us -> 0.01 us  [exchange(): lax.all_to_all(chunks, 'expert', split_axis=0, concat_axis=0, tiled=True,...]
    ppermute x17 -> x19, waiting for transfers between devices: 33.5 us -> 40.9 us  [swap(): return lax.ppermute(value, 'expert', [(j, j ^ bit) for j in range(count)])]
    ppermute x17 -> x19, starting transfers between devices: 19.2 us -> 22.1 us  [swap(): return lax.ppermute(value, 'expert', [(j, j ^ bit) for j in range(count)])]
    pallas_call x1, Pallas kernels: 7.13 us -> 5.35 us  [pack_hidden(): pl.pallas_call(lambda *refs: pack_kernel(cap, *refs), in_specs=[VMEM, VME...]
    pallas_call x2 -> x3, Pallas kernels: 18 us -> 16.3 us  [the longest x1 10.5 us: middle(): pl.pallas_call(lambda *refs: middle_kernel(cap, count, *refs), in_specs=[...]
    unnamed x30 -> x26, local copies, waits for them, and re-layouts: 2.49 us -> 2.1 us
  transfers between devices with their start and end apart: 19 -> 21, of which waited for: 10 -> 13; matrix products, arithmetic and copies ran while one was open for 2% -> 3% of each run, Pallas kernels for 22% -> 11%
where the time goes in v4:
time: 104 us
  waiting for transfers between devices  41 us (39%)
  starting transfers between devices  31.6 us (30%)
  Pallas kernels  25.3 us (24%)
  other arithmetic  2.72 us (3%)
  local copies, waits for them, and re-layouts  2.24 us (2%)
    ppermute x19, waiting for transfers between devices, swap(): return lax.ppermute(value, 'expert', [(j, j ^ bit) for j in range(count)])  40.9 us
    ppermute x19, starting transfers between devices, swap(): return lax.ppermute(value, 'expert', [(j, j ^ bit) for j in range(count)])  22.1 us
    pallas_call x1, Pallas kernels, middle(): pl.pallas_call(lambda *refs: middle_kernel(cap, count, *refs), in_specs=[...  10.5 us
    all_to_all x2, starting transfers between devices, exchange(): lax.all_to_all(chunks, 'expert', split_axis=0, concat_axis=0, tiled=True,...  9.54 us
    pallas_call x1, Pallas kernels, pack_hidden(): pl.pallas_call(lambda *refs: pack_kernel(cap, *refs), in_specs=[VMEM, VME...  5.35 us
    pallas_call x1, Pallas kernels, keep_partials(): pl.pallas_call(lambda *refs: keep_kernel(count, *refs), in_specs=[ANY] *...  4.51 us
    pallas_call x1, Pallas kernels, finish(): pl.pallas_call(finish_kernel, grid=(4,), in_specs=[pl.BlockSpec((tile, 2)...  3.65 us
    unnamed x26, local copies, waits for them, and re-layouts  2.1 us
  transfers between devices with their start and end apart: 21, of which 13 were waited for; matrix products, arithmetic and copies ran while one was open for 3% of the time, Pallas kernels for 11%

profile of v4, /device:TPU:0, one launch (start us, length us, event | category | flops | bytes accessed | tf_op | source)
XLA Modules:
  0.0 103.7 jit_solution(8256853373761733897)
XLA Ops:
  0.6 4.1 %collective-permute-start = (bf16[128,1024]{1,0:T(8,128)(2,1)}, bf16[128,1024]{1,0:T(8,128)(2,1)S(1)}, u32[]{:S(2)}, u32[]{:S(2)}) collective-permute-start(bf16[128,1024]{1,0:T(8,128)(2,1)} %refs_0_), channel_id=1, source_target_pairs={{0,16},{1,17},{2,18},{3,19},{4,20},{5,21},{6,22},{7,23},{8,24},{9,... | collective-permute-start | bytes 786440 | tf_op jit(solution)/shard_map/ppermute | solution.py:25
  4.7 1.6 %collective-permute-start.1 = (bf16[128,1024]{1,0:T(8,128)(2,1)}, bf16[128,1024]{1,0:T(8,128)(2,1)S(1)}, u32[]{:S(2)}, u32[]{:S(2)}) collective-permute-start(bf16[128,1024]{1,0:T(8,128)(2,1)} %refs_0_), channel_id=1, source_target_pairs={{0,8},{1,9},{2,10},{3,11},{4,12},{5,13},{6,14},{7,15},{8,0},{9,1},... | collective-permute-start | bytes 786440 | tf_op jit(solution)/shard_map/ppermute | solution.py:25
  6.3 0.1 stack.23.refs_0_
  6.4 5.3 %pack_hidden.1 = (bf16[8,192,384]{2,1,0:T(8,128)(2,1)}, f32[16,128]{1,0:T(8,128)}) custom-call(s32[8,128]{1,0:T(8,128)} %bitcast.24, f32[8,128]{1,0:T(8,128)} %bitcast.20, bf16[1024,768]{1,0:T(8,128)(2,1)} %bitcast.18), custom_call_target="tpu_custom_call" | custom-call | flops 1207959552 | bytes 1572864 | tf_op jit(solution)/shard_map/pack_hidden/pallas_call | solution.py:127
  11.7 0.0 copy-start.5
  11.8 5.2 %collective-permute-done.refs_2_.refs_1_ = bf16[128,1024]{1,0:T(8,128)(2,1)S(1)} collective-permute-done((bf16[128,1024]{1,0:T(8,128)(2,1)}, bf16[128,1024]{1,0:T(8,128)(2,1)S(1)}, u32[]{:S(2)}, u32[]{:S(2)}) %collective-permute-start) | collective-permute-done | bytes 262176 | tf_op jit(solution)/shard_map/ppermute | solution.py:25
  17.0 0.2 collective-permute-done.1.refs_3_.refs_2_
  17.2 4.7 %all-to-all-start = ((bf16[8,192,384]{2,1,0:T(8,128)(2,1)}), bf16[8,192,384]{2,1,0:T(8,128)(2,1)}, u32[]{:S(2)}, u32[]{:S(2)}) async-start(bf16[8,192,384]{2,1,0:T(8,128)(2,1)} %get-tuple-element.37), calls=%async_computation | async-start | bytes 2359296 | tf_op jit(solution)/shard_map/all_to_all | solution.py:389
  21.8 0.0 copy-done.5
  21.8 0.1 slice_bitcast_fusion
  21.9 1.6 %collective-permute-start.5 = (bf16[192,1024]{1,0:T(8,128)(2,1)S(1)}, bf16[192,1024]{1,0:T(8,128)(2,1)S(1)}, u32[]{:S(2)}, u32[]{:S(2)}) collective-permute-start(bf16[192,1024]{1,0:T(8,128)(2,1)S(1)} %get-tuple-element.52), channel_id=1, source_target_pairs={{0,2},{1,3},{2,0},{3,1},{4,6},{5,7},{6,4},{7,5},{8,10},{9,11},{10,... | collective-permute-start | bytes 1179656 | tf_op jit(solution)/shard_map/ppermute | solution.py:25
  23.4 1.5 %collective-permute-start.7 = (bf16[192,1024]{1,0:T(8,128)(2,1)S(1)}, bf16[192,1024]{1,0:T(8,128)(2,1)S(1)}, u32[]{:S(2)}, u32[]{:S(2)}) collective-permute-start(bf16[192,1024]{1,0:T(8,128)(2,1)S(1)} %get-tuple-element.53), channel_id=1, source_target_pairs={{0,4},{1,5},{2,6},{3,7},{4,0},{5,1},{6,2},{7,3},{8,12},{9,13},{10,... | collective-permute-start | bytes 1179656 | tf_op jit(solution)/shard_map/ppermute | solution.py:25
  25.0 0.5 collective-permute-start.3
  25.5 0.5 collective-permute-start.4
  26.0 7.9 %collective-permute-done.5.refs_10_ = bf16[192,1024]{1,0:T(8,128)(2,1)S(1)} collective-permute-done((bf16[192,1024]{1,0:T(8,128)(2,1)S(1)}, bf16[192,1024]{1,0:T(8,128)(2,1)S(1)}, u32[]{:S(2)}, u32[]{:S(2)}) %collective-permute-start.5) | collective-permute-done | bytes 393248 | tf_op jit(solution)/shard_map/ppermute | solution.py:25
  33.9 1.5 %collective-permute-start.6 = (bf16[192,1024]{1,0:T(8,128)(2,1)S(1)}, bf16[192,1024]{1,0:T(8,128)(2,1)S(1)}, u32[]{:S(2)}, u32[]{:S(2)}) collective-permute-start(bf16[192,1024]{1,0:T(8,128)(2,1)S(1)} %collective-permute-done.5.refs_10_), channel_id=1, source_target_pairs={{0,4},{1,5},{2,6},{3,7},{4,0},{5,1},{6,2},{7,3},{8,12},{9,13},{10,... | collective-permute-start | bytes 1179656 | tf_op jit(solution)/shard_map/ppermute | solution.py:25
  35.4 0.0 collective-permute-done.7.refs_13_
  35.4 1.5 %collective-permute-start.8 = (bf16[192,1024]{1,0:T(8,128)(2,1)S(1)}, bf16[192,1024]{1,0:T(8,128)(2,1)S(1)}, u32[]{:S(2)}, u32[]{:S(2)}) collective-permute-start(bf16[192,1024]{1,0:T(8,128)(2,1)S(1)} %collective-permute-done.7.refs_13_), channel_id=1, source_target_pairs={{0,2},{1,3},{2,0},{3,1},{4,6},{5,7},{6,4},{7,5},{8,10},{9,11},{10,... | collective-permute-start | bytes 1179656 | tf_op jit(solution)/shard_map/ppermute | solution.py:25
  36.9 2.1 %collective-permute-start.2 = (bf16[128,1024]{1,0:T(8,128)(2,1)S(1)}, bf16[128,1024]{1,0:T(8,128)(2,1)S(1)}, u32[]{:S(2)}, u32[]{:S(2)}) collective-permute-start(bf16[128,1024]{1,0:T(8,128)(2,1)S(1)} %collective-permute-done.refs_2_.refs_1_), channel_id=1, source_target_pairs={{0,8},{1,9},{2,10},{3,11},{4,12},{5,13},{6,14},{7,15},{8,0},{9,1},... | collective-permute-start | bytes 786440 | tf_op jit(solution)/shard_map/ppermute | solution.py:25
  38.9 3.3 %collective-permute-done.3.refs_11_ = bf16[192,1024]{1,0:T(8,128)(2,1)S(1)} collective-permute-done((bf16[192,1024]{1,0:T(8,128)(2,1)S(1)}, bf16[192,1024]{1,0:T(8,128)(2,1)S(1)}, u32[]{:S(2)}, u32[]{:S(2)}) %collective-permute-start.3) | collective-permute-done | bytes 393248 | tf_op jit(solution)/shard_map/ppermute | solution.py:25
  42.3 0.0 collective-permute-start.10
  42.3 1.6 %collective-permute-done.4.refs_12_ = bf16[192,1024]{1,0:T(8,128)(2,1)} collective-permute-done((bf16[192,1024]{1,0:T(8,128)(2,1)S(1)}, bf16[192,1024]{1,0:T(8,128)(2,1)}, u32[]{:S(2)}, u32[]{:S(2)}) %collective-permute-start.4) | collective-permute-done | bytes 393248 | tf_op jit(solution)/shard_map/ppermute | solution.py:25
  43.9 0.0 collective-permute-start.11
  43.9 3.6 %collective-permute-done.2.refs_4_.refs_3_ = bf16[128,1024]{1,0:T(8,128)(2,1)S(1)} collective-permute-done((bf16[128,1024]{1,0:T(8,128)(2,1)S(1)}, bf16[128,1024]{1,0:T(8,128)(2,1)S(1)}, u32[]{:S(2)}, u32[]{:S(2)}) %collective-permute-start.2) | collective-permute-done | bytes 262176 | tf_op jit(solution)/shard_map/ppermute | solution.py:25
  47.5 0.0 copy-done.3
  47.5 0.0 collective-permute-start.9
  47.5 4.0 %collective-permute-done.6.refs_14_ = bf16[192,1024]{1,0:T(8,128)(2,1)S(1)} collective-permute-done((bf16[192,1024]{1,0:T(8,128)(2,1)S(1)}, bf16[192,1024]{1,0:T(8,128)(2,1)S(1)}, u32[]{:S(2)}, u32[]{:S(2)}) %collective-permute-start.6) | collective-permute-done | bytes 393248 | tf_op jit(solution)/shard_map/ppermute | solution.py:25
  51.5 0.0 collective-permute-done.8.refs_15_
  51.5 0.1 collective-permute-start.12
  51.6 0.0 collective-permute-done.10.refs_6_.refs_5_
  51.6 0.0 collective-permute-done.11.refs_7_.refs_6_
  51.6 0.0 collective-permute-done.9.refs_5_.refs_4_
  51.6 0.6 copy-done.9
  52.3 0.2 copy-done.11
  52.5 0.7 collective-permute-done.12.refs_8_.refs_7_
  53.1 0.0 all-to-all-done.refs_16_
  53.2 0.7 copy-done.12
  53.8 10.5 %middle.1 = (bf16[8,192,384]{2,1,0:T(8,128)(2,1)}, bf16[192,1024]{1,0:T(8,128)(2,1)}, bf16[192,1024]{1,0:T(8,128)(2,1)}, bf16[192,1024]{1,0:T(8,128)(2,1)}, bf16...) custom-call(s32[5]{0:T(128)S(1)} %stack.23.refs_0_, bf16[128,1024]{1,0:T(8,128)(2,1)S(1)} %copy-done.3, ...), custom_call_target="tpu_custom_call" | custom-call | flops 4831838208 | bytes 4194304 | tf_op jit(solution)/shard_map/middle/pallas_call | solution.py:265
  64.3 4.9 %all-to-all-start.1 = ((bf16[8,192,384]{2,1,0:T(8,128)(2,1)}), bf16[8,192,384]{2,1,0:T(8,128)(2,1)S(1)}, u32[]{:S(2)}, u32[]{:S(2)}) async-start(bf16[8,192,384]{2,1,0:T(8,128)(2,1)} %get-tuple-element.38), calls=%async_computation.1 | async-start | bytes 2359296 | tf_op jit(solution)/shard_map/all_to_all | solution.py:389
  69.2 0.5 collective-permute-start.15
  69.8 1.5 %collective-permute-start.16 = (bf16[192,1024]{1,0:T(8,128)(2,1)}, bf16[192,1024]{1,0:T(8,128)(2,1)S(1)}, u32[]{:S(2)}, u32[]{:S(2)}) collective-permute-start(bf16[192,1024]{1,0:T(8,128)(2,1)} %get-tuple-element.46), channel_id=1, source_target_pairs={{0,4},{1,5},{2,6},{3,7},{4,0},{5,1},{6,2},{7,3},{8,12},{9,13},{10,... | collective-permute-start | bytes 1179656 | tf_op jit(solution)/shard_map/ppermute | solution.py:25
  71.3 1.5 %collective-permute-start.13 = (bf16[192,1024]{1,0:T(8,128)(2,1)}, bf16[192,1024]{1,0:T(8,128)(2,1)S(1)}, u32[]{:S(2)}, u32[]{:S(2)}) collective-permute-start(bf16[192,1024]{1,0:T(8,128)(2,1)} %get-tuple-element.41), channel_id=1, source_target_pairs={{0,2},{1,3},{2,0},{3,1},{4,6},{5,7},{6,4},{7,5},{8,10},{9,11},{10,... | collective-permute-start | bytes 1179656 | tf_op jit(solution)/shard_map/ppermute | solution.py:25
  72.8 0.5 collective-permute-start.14
  73.3 4.5 %keep_partials.1 = (f32[384,1024]{1,0:T(8,128)}, bf16[384,1024]{1,0:T(8,128)(2,1)}) custom-call(bf16[128,1024]{1,0:T(8,128)(2,1)S(1)} %copy-done.3, bf16[128,1024]{1,0:T(8,128)(2,1)S(1)} %collective-permute-done.refs_2_.refs_1_, bf16[128,1024]{1,0:T(8,128)(2,1)S(1)} %collective-permute-done.1.refs_3_.refs_2_, ...), custom_call_target="tpu_custom_call" | custom-call | flops 1610612736 | bytes 4194304 | tf_op jit(solution)/shard_map/keep_partials/pallas_call | solution.py:317
  77.8 0.0 copy-start.1
  77.8 0.0 copy-start.2
  77.8 3.5 %collective-permute-done.15 = bf16[192,1024]{1,0:T(8,128)(2,1)S(1)} collective-permute-done((bf16[192,1024]{1,0:T(8,128)(2,1)}, bf16[192,1024]{1,0:T(8,128)(2,1)S(1)}, u32[]{:S(2)}, u32[]{:S(2)}) %collective-permute-start.15) | collective-permute-done | bytes 393248 | tf_op jit(solution)/shard_map/ppermute | solution.py:25
  81.3 0.6 collective-permute-done.16
  81.9 1.4 %add_convert_fusion.1 = (bf16[192,1024]{1,0:T(8,128)(2,1)S(1)}, bf16[192,1024]{1,0:T(8,128)(2,1)S(1)}) fusion(bf16[192,1024]{1,0:T(8,128)(2,1)S(1)} %collective-permute-done.15, bf16[384,1024]{1,0:T(8,128)(2,1)} %get-tuple-element.44, bf16[192,1024]{1,0:T(8,128)(2,1)S(1)} %collective-permute-done.16), kind=kLoop, calls=%fused_computation.6 | loop fusion | flops 1572864 | bytes 2359296 | tf_op jit(solution)/shard_map/convert_element_type | solution.py:430
  83.3 1.6 %collective-permute-start.17 = (bf16[192,1024]{1,0:T(8,128)(2,1)S(1)}, bf16[192,1024]{1,0:T(8,128)(2,1)S(1)}, u32[]{:S(2)}, u32[]{:S(2)}) collective-permute-start(bf16[192,1024]{1,0:T(8,128)(2,1)S(1)} %get-tuple-element.50), channel_id=1, source_target_pairs={{0,4},{1,5},{2,6},{3,7},{4,0},{5,1},{6,2},{7,3},{8,12},{9,13},{10,... | collective-permute-start | bytes 1179656 | tf_op jit(solution)/shard_map/ppermute | solution.py:25
  84.9 1.5 %collective-permute-start.18 = (bf16[192,1024]{1,0:T(8,128)(2,1)S(1)}, bf16[192,1024]{1,0:T(8,128)(2,1)S(1)}, u32[]{:S(2)}, u32[]{:S(2)}) collective-permute-start(bf16[192,1024]{1,0:T(8,128)(2,1)S(1)} %get-tuple-element.51), channel_id=1, source_target_pairs={{0,2},{1,3},{2,0},{3,1},{4,6},{5,7},{6,4},{7,5},{8,10},{9,11},{10,... | collective-permute-start | bytes 1179656 | tf_op jit(solution)/shard_map/ppermute | solution.py:25
  86.4 1.3 %columns.1.column_ref = f32[1024,2]{1,0:T(8,128)S(1)} custom-call(f32[16,128]{1,0:T(8,128)S(1)} %copy-done.1, f32[8,128]{1,0:T(8,128)S(1)} %bitcast.21), custom_call_target="tpu_custom_call" | custom-call | tf_op jit(solution)/shard_map/columns/pallas_call | solution.py:156
  87.7 0.0 copy-start.4
  87.8 2.0 %collective-permute-done.13 = bf16[192,1024]{1,0:T(8,128)(2,1)S(1)} collective-permute-done((bf16[192,1024]{1,0:T(8,128)(2,1)}, bf16[192,1024]{1,0:T(8,128)(2,1)S(1)}, u32[]{:S(2)}, u32[]{:S(2)}) %collective-permute-start.13) | collective-permute-done | bytes 393248 | tf_op jit(solution)/shard_map/ppermute | solution.py:25
  89.8 0.6 collective-permute-done.14
  90.3 7.7 %collective-permute-done.17 = bf16[192,1024]{1,0:T(8,128)(2,1)S(1)} collective-permute-done((bf16[192,1024]{1,0:T(8,128)(2,1)S(1)}, bf16[192,1024]{1,0:T(8,128)(2,1)S(1)}, u32[]{:S(2)}, u32[]{:S(2)}) %collective-permute-start.17) | collective-permute-done | bytes 393248 | tf_op jit(solution)/shard_map/ppermute | solution.py:25
  98.1 0.1 convert_add_fusion.1
  98.2 0.0 collective-permute-done.18
  98.2 0.1 convert_add_fusion
  98.3 0.0 copy-start
  98.3 1.1 %fusion.1 = bf16[1,384,1024]{2,1,0:T(8,128)(2,1)} fusion(f32[384,1024]{1,0:T(8,128)S(1)} %copy-done.4, f32[192,1024]{1,0:T(8,128)S(1)} %convert_add_fusion, f32[192,1024]{1,0:T(8,128)S(1)} %convert_add_fusion.1), kind=kLoop, calls=%fused_computation.2 | loop fusion | flops 1179648 | bytes 3932160 | tf_op jit(solution)/shard_map/convert_element_type | solution.py:444
  99.4 0.0 all-to-all-done.1
  99.4 0.6 copy-done
  100.0 3.6 %finish.1 = bf16[1024,768]{1,0:T(8,128)(2,1)} custom-call(f32[1024,2]{1,0:T(8,128)S(1)} %columns.1.column_ref, bf16[1024,768]{1,0:T(8,128)(2,1)S(1)} %bitcast.19, bf16[1536,384]{1,0:T(8,128)(2,1)S(1)} %bitcast.17), custom_call_target="tpu_custom_call" | custom-call | flops 786432 | bytes 3145728 | tf_op jit(solution)/shard_map/finish/pallas_call | solution.py:359
  (15 shorter events, 0.0 us)
Async XLA Ops:
  0.6 16.3 %collective-permute-start = (bf16[128,1024]{1,0:T(8,128)(2,1)}, bf16[128,1024]{1,0:T(8,128)(2,1)S(1)}, u32[]{:S(2)}, u32[]{:S(2)}) collective-permute-start(bf16[128,1024]{1,0:T(8,128)(2,1)} %refs_0_), channel_id=1, source_target_pairs={{0,16},{1,17},{2,18},{3,19},{4,20},{5,21},{6,22},{7,23},{8,24},{9,... | collective-permute-start | bytes 786440 | tf_op jit(solution)/shard_map/ppermute | solution.py:25
  4.7 12.4 %collective-permute-start.1 = (bf16[128,1024]{1,0:T(8,128)(2,1)}, bf16[128,1024]{1,0:T(8,128)(2,1)S(1)}, u32[]{:S(2)}, u32[]{:S(2)}) collective-permute-start(bf16[128,1024]{1,0:T(8,128)(2,1)} %refs_0_), channel_id=1, source_target_pairs={{0,8},{1,9},{2,10},{3,11},{4,12},{5,13},{6,14},{7,15},{8,0},{9,1},... | collective-permute-start | bytes 786440 | tf_op jit(solution)/shard_map/ppermute | solution.py:25
  11.7 10.1 %copy-start.5 = (bf16[1,384,1024]{2,1,0:T(8,128)(2,1)S(1)}, bf16[1,384,1024]{2,1,0:T(8,128)(2,1)}, u32[]{:S(2)}) copy-start(bf16[1,384,1024]{2,1,0:T(8,128)(2,1)} %param.9) | copy-start | bytes 2359300
  17.2 30.4 %copy-start.3 = (bf16[128,1024]{1,0:T(8,128)(2,1)S(1)}, bf16[128,1024]{1,0:T(8,128)(2,1)}, u32[]{:S(2)}) copy-start(bf16[128,1024]{1,0:T(8,128)(2,1)} %refs_0_) | copy-start | bytes 786436
  17.2 36.0 %all-to-all-start = ((bf16[8,192,384]{2,1,0:T(8,128)(2,1)}), bf16[8,192,384]{2,1,0:T(8,128)(2,1)}, u32[]{:S(2)}, u32[]{:S(2)}) async-start(bf16[8,192,384]{2,1,0:T(8,128)(2,1)} %get-tuple-element.37), calls=%async_computation | async-start | bytes 2359296 | tf_op jit(solution)/shard_map/all_to_all | solution.py:389
  21.9 12.0 %collective-permute-start.5 = (bf16[192,1024]{1,0:T(8,128)(2,1)S(1)}, bf16[192,1024]{1,0:T(8,128)(2,1)S(1)}, u32[]{:S(2)}, u32[]{:S(2)}) collective-permute-start(bf16[192,1024]{1,0:T(8,128)(2,1)S(1)} %get-tuple-element.52), channel_id=1, source_target_pairs={{0,2},{1,3},{2,0},{3,1},{4,6},{5,7},{6,4},{7,5},{8,10},{9,11},{10,... | collective-permute-start | bytes 1179656 | tf_op jit(solution)/shard_map/ppermute | solution.py:25
  23.4 11.9 %collective-permute-start.7 = (bf16[192,1024]{1,0:T(8,128)(2,1)S(1)}, bf16[192,1024]{1,0:T(8,128)(2,1)S(1)}, u32[]{:S(2)}, u32[]{:S(2)}) collective-permute-start(bf16[192,1024]{1,0:T(8,128)(2,1)S(1)} %get-tuple-element.53), channel_id=1, source_target_pairs={{0,4},{1,5},{2,6},{3,7},{4,0},{5,1},{6,2},{7,3},{8,12},{9,13},{10,... | collective-permute-start | bytes 1179656 | tf_op jit(solution)/shard_map/ppermute | solution.py:25
  25.0 17.3 %collective-permute-start.3 = (bf16[192,1024]{1,0:T(8,128)(2,1)S(1)}, bf16[192,1024]{1,0:T(8,128)(2,1)S(1)}, u32[]{:S(2)}, u32[]{:S(2)}) collective-permute-start(bf16[192,1024]{1,0:T(8,128)(2,1)S(1)} %get-tuple-element.53), channel_id=1, source_target_pairs={{0,2},{1,3},{2,0},{3,1},{4,6},{5,7},{6,4},{7,5},{8,10},{9,11},{10,... | collective-permute-start | bytes 1179656 | tf_op jit(solution)/shard_map/ppermute | solution.py:25
  25.5 18.4 %collective-permute-start.4 = (bf16[192,1024]{1,0:T(8,128)(2,1)S(1)}, bf16[192,1024]{1,0:T(8,128)(2,1)}, u32[]{:S(2)}, u32[]{:S(2)}) collective-permute-start(bf16[192,1024]{1,0:T(8,128)(2,1)S(1)} %get-tuple-element.52), channel_id=1, source_target_pairs={{0,4},{1,5},{2,6},{3,7},{4,0},{5,1},{6,2},{7,3},{8,12},{9,13},{10,... | collective-permute-start | bytes 1179656 | tf_op jit(solution)/shard_map/ppermute | solution.py:25
  33.9 19.3 %copy-start.6 = (bf16[192,1024]{1,0:T(8,128)(2,1)}, bf16[192,1024]{1,0:T(8,128)(2,1)S(1)}, u32[]{:S(2)}) copy-start(bf16[192,1024]{1,0:T(8,128)(2,1)S(1)} %collective-permute-done.5.refs_10_) | copy-start | bytes 1179652
  33.9 17.7 %collective-permute-start.6 = (bf16[192,1024]{1,0:T(8,128)(2,1)S(1)}, bf16[192,1024]{1,0:T(8,128)(2,1)S(1)}, u32[]{:S(2)}, u32[]{:S(2)}) collective-permute-start(bf16[192,1024]{1,0:T(8,128)(2,1)S(1)} %collective-permute-done.5.refs_10_), channel_id=1, source_target_pairs={{0,4},{1,5},{2,6},{3,7},{4,0},{5,1},{6,2},{7,3},{8,12},{9,13},{10,... | collective-permute-start | bytes 1179656 | tf_op jit(solution)/shard_map/ppermute | solution.py:25
  35.4 17.8 %copy-start.7 = (bf16[192,1024]{1,0:T(8,128)(2,1)}, bf16[192,1024]{1,0:T(8,128)(2,1)S(1)}, u32[]{:S(2)}) copy-start(bf16[192,1024]{1,0:T(8,128)(2,1)S(1)} %collective-permute-done.7.refs_13_) | copy-start | bytes 1179652
  35.4 16.1 %collective-permute-start.8 = (bf16[192,1024]{1,0:T(8,128)(2,1)S(1)}, bf16[192,1024]{1,0:T(8,128)(2,1)S(1)}, u32[]{:S(2)}, u32[]{:S(2)}) collective-permute-start(bf16[192,1024]{1,0:T(8,128)(2,1)S(1)} %collective-permute-done.7.refs_13_), channel_id=1, source_target_pairs={{0,2},{1,3},{2,0},{3,1},{4,6},{5,7},{6,4},{7,5},{8,10},{9,11},{10,... | collective-permute-start | bytes 1179656 | tf_op jit(solution)/shard_map/ppermute | solution.py:25
  36.9 10.7 %collective-permute-start.2 = (bf16[128,1024]{1,0:T(8,128)(2,1)S(1)}, bf16[128,1024]{1,0:T(8,128)(2,1)S(1)}, u32[]{:S(2)}, u32[]{:S(2)}) collective-permute-start(bf16[128,1024]{1,0:T(8,128)(2,1)S(1)} %collective-permute-done.refs_2_.refs_1_), channel_id=1, source_target_pairs={{0,8},{1,9},{2,10},{3,11},{4,12},{5,13},{6,14},{7,15},{8,0},{9,1},... | collective-permute-start | bytes 786440 | tf_op jit(solution)/shard_map/ppermute | solution.py:25
  42.3 10.9 %copy-start.8 = (bf16[192,1024]{1,0:T(8,128)(2,1)}, bf16[192,1024]{1,0:T(8,128)(2,1)S(1)}, u32[]{:S(2)}) copy-start(bf16[192,1024]{1,0:T(8,128)(2,1)S(1)} %collective-permute-done.3.refs_11_) | copy-start | bytes 1179652
  42.3 9.3 %collective-permute-start.10 = (bf16[128,1024]{1,0:T(8,128)(2,1)S(1)}, bf16[128,1024]{1,0:T(8,128)(2,1)S(1)}, u32[]{:S(2)}, u32[]{:S(2)}) collective-permute-start(bf16[128,1024]{1,0:T(8,128)(2,1)S(1)} %collective-permute-done.refs_2_.refs_1_), channel_id=1, source_target_pairs={{0,1},{1,0},{2,3},{3,2},{4,5},{5,4},{6,7},{7,6},{8,9},{9,8},{10,11... | collective-permute-start | bytes 786440 | tf_op jit(solution)/shard_map/ppermute | solution.py:25
  43.9 7.7 %collective-permute-start.11 = (bf16[128,1024]{1,0:T(8,128)(2,1)S(1)}, bf16[128,1024]{1,0:T(8,128)(2,1)S(1)}, u32[]{:S(2)}, u32[]{:S(2)}) collective-permute-start(bf16[128,1024]{1,0:T(8,128)(2,1)S(1)} %collective-permute-done.1.refs_3_.refs_2_), channel_id=1, source_target_pairs={{0,1},{1,0},{2,3},{3,2},{4,5},{5,4},{6,7},{7,6},{8,9},{9,8},{10,11... | collective-permute-start | bytes 786440 | tf_op jit(solution)/shard_map/ppermute | solution.py:25
  47.5 4.1 %collective-permute-start.9 = (bf16[128,1024]{1,0:T(8,128)(2,1)S(1)}, bf16[128,1024]{1,0:T(8,128)(2,1)S(1)}, u32[]{:S(2)}, u32[]{:S(2)}) collective-permute-start(bf16[128,1024]{1,0:T(8,128)(2,1)S(1)} %copy-done.3), channel_id=1, source_target_pairs={{0,1},{1,0},{2,3},{3,2},{4,5},{5,4},{6,7},{7,6},{8,9},{9,8},{10,11... | collective-permute-start | bytes 786440 | tf_op jit(solution)/shard_map/ppermute | solution.py:25
  51.5 0.8 copy-start.9
  51.5 0.9 copy-start.11
  51.5 1.6 %collective-permute-start.12 = (bf16[128,1024]{1,0:T(8,128)(2,1)S(1)}, bf16[128,1024]{1,0:T(8,128)(2,1)S(1)}, u32[]{:S(2)}, u32[]{:S(2)}) collective-permute-start(bf16[128,1024]{1,0:T(8,128)(2,1)S(1)} %collective-permute-done.2.refs_4_.refs_3_), channel_id=1, source_target_pairs={{0,1},{1,0},{2,3},{3,2},{4,5},{5,4},{6,7},{7,6},{8,9},{9,8},{10,11... | collective-permute-start | bytes 786440 | tf_op jit(solution)/shard_map/ppermute | solution.py:25
  53.1 0.7 copy-start.12
  64.3 8.5 %copy-start.10 = (bf16[192,1024]{1,0:T(8,128)(2,1)S(1)}, bf16[192,1024]{1,0:T(8,128)(2,1)}, u32[]{:S(2)}) copy-start(bf16[192,1024]{1,0:T(8,128)(2,1)} %get-tuple-element.42) | copy-start | bytes 1179652
  64.3 35.1 %all-to-all-start.1 = ((bf16[8,192,384]{2,1,0:T(8,128)(2,1)}), bf16[8,192,384]{2,1,0:T(8,128)(2,1)S(1)}, u32[]{:S(2)}, u32[]{:S(2)}) async-start(bf16[8,192,384]{2,1,0:T(8,128)(2,1)} %get-tuple-element.38), calls=%async_computation.1 | async-start | bytes 2359296 | tf_op jit(solution)/shard_map/all_to_all | solution.py:389
  69.2 12.1 %collective-permute-start.15 = (bf16[192,1024]{1,0:T(8,128)(2,1)}, bf16[192,1024]{1,0:T(8,128)(2,1)S(1)}, u32[]{:S(2)}, u32[]{:S(2)}) collective-permute-start(bf16[192,1024]{1,0:T(8,128)(2,1)} %get-tuple-element.45), channel_id=1, source_target_pairs={{0,2},{1,3},{2,0},{3,1},{4,6},{5,7},{6,4},{7,5},{8,10},{9,11},{10,... | collective-permute-start | bytes 1179656 | tf_op jit(solution)/shard_map/ppermute | solution.py:25
  69.8 12.2 %collective-permute-start.16 = (bf16[192,1024]{1,0:T(8,128)(2,1)}, bf16[192,1024]{1,0:T(8,128)(2,1)S(1)}, u32[]{:S(2)}, u32[]{:S(2)}) collective-permute-start(bf16[192,1024]{1,0:T(8,128)(2,1)} %get-tuple-element.46), channel_id=1, source_target_pairs={{0,4},{1,5},{2,6},{3,7},{4,0},{5,1},{6,2},{7,3},{8,12},{9,13},{10,... | collective-permute-start | bytes 1179656 | tf_op jit(solution)/shard_map/ppermute | solution.py:25
  71.3 18.5 %collective-permute-start.13 = (bf16[192,1024]{1,0:T(8,128)(2,1)}, bf16[192,1024]{1,0:T(8,128)(2,1)S(1)}, u32[]{:S(2)}, u32[]{:S(2)}) collective-permute-start(bf16[192,1024]{1,0:T(8,128)(2,1)} %get-tuple-element.41), channel_id=1, source_target_pairs={{0,2},{1,3},{2,0},{3,1},{4,6},{5,7},{6,4},{7,5},{8,10},{9,11},{10,... | collective-permute-start | bytes 1179656 | tf_op jit(solution)/shard_map/ppermute | solution.py:25
  72.8 17.6 %collective-permute-start.14 = (bf16[192,1024]{1,0:T(8,128)(2,1)S(1)}, bf16[192,1024]{1,0:T(8,128)(2,1)S(1)}, u32[]{:S(2)}, u32[]{:S(2)}) collective-permute-start(bf16[192,1024]{1,0:T(8,128)(2,1)S(1)} %copy-done.10), channel_id=1, source_target_pairs={{0,4},{1,5},{2,6},{3,7},{4,0},{5,1},{6,2},{7,3},{8,12},{9,13},{10,... | collective-permute-start | bytes 1179656 | tf_op jit(solution)/shard_map/ppermute | solution.py:25
  77.8 8.6 %copy-start.1 = (f32[16,128]{1,0:T(8,128)S(1)}, f32[16,128]{1,0:T(8,128)}, u32[]{:S(2)}) copy-start(f32[16,128]{1,0:T(8,128)} %get-tuple-element.26.refs_0_) | copy-start | bytes 24580
  77.8 8.6 %copy-start.2 = (f32[128,8]{0,1:T(8,128)S(1)}, f32[128,8]{0,1:T(8,128)}, u32[]{:S(2)}) copy-start(f32[128,8]{0,1:T(8,128)} %param.6) | copy-start | bytes 12292
  83.3 14.7 %collective-permute-start.17 = (bf16[192,1024]{1,0:T(8,128)(2,1)S(1)}, bf16[192,1024]{1,0:T(8,128)(2,1)S(1)}, u32[]{:S(2)}, u32[]{:S(2)}) collective-permute-start(bf16[192,1024]{1,0:T(8,128)(2,1)S(1)} %get-tuple-element.50), channel_id=1, source_target_pairs={{0,4},{1,5},{2,6},{3,7},{4,0},{5,1},{6,2},{7,3},{8,12},{9,13},{10,... | collective-permute-start | bytes 1179656 | tf_op jit(solution)/shard_map/ppermute | solution.py:25
  84.9 13.3 %collective-permute-start.18 = (bf16[192,1024]{1,0:T(8,128)(2,1)S(1)}, bf16[192,1024]{1,0:T(8,128)(2,1)S(1)}, u32[]{:S(2)}, u32[]{:S(2)}) collective-permute-start(bf16[192,1024]{1,0:T(8,128)(2,1)S(1)} %get-tuple-element.51), channel_id=1, source_target_pairs={{0,2},{1,3},{2,0},{3,1},{4,6},{5,7},{6,4},{7,5},{8,10},{9,11},{10,... | collective-permute-start | bytes 1179656 | tf_op jit(solution)/shard_map/ppermute | solution.py:25
  87.7 10.6 %copy-start.4 = (f32[384,1024]{1,0:T(8,128)S(1)}, f32[384,1024]{1,0:T(8,128)}, u32[]{:S(2)}) copy-start(f32[384,1024]{1,0:T(8,128)} %get-tuple-element.40) | copy-start | bytes 4718596
  98.3 1.7 %copy-start = (bf16[128,8,768]{2,1,0:T(8,128)(2,1)S(1)}, bf16[128,8,768]{2,1,0:T(8,128)(2,1)}, u32[]{:S(2)}) copy-start(bf16[128,8,768]{2,1,0:T(8,128)(2,1)} %param.8) | copy-start | bytes 4718596

commit v5 on v4

--- a/solution.py
+++ b/solution.py
@@ -143,24 +143,46 @@
     )(ids.T, gates.T, flat_pre)
 
 
-def columns_kernel(cap, place_ref, gates_ref, out_ref):
+def factors_kernel(cap, place_ref, gates_ref, pre_ref, out_ref, column_ref, gate):
     top = gates_ref.shape[0]
-    rows = out_ref.shape[0]
-    place = place_ref[top:] * cap + place_ref[:top]
-    out_ref[...] = jnp.concatenate(
-        [column_of(gates_ref[...], rows), column_of(place, rows)], 1
-    )
-
-
-def columns(place, gates, cap):
+    rows = gate.shape[0]
+    tile, both = pre_ref.shape
+    width = both // 2
+    step = pl.program_id(0)
+
+    @pl.when(step == 0)
+    def _():
+        gate[...] = column_of(gates_ref[...], rows)
+        column_ref[...] = column_of(place_ref[top:] * cap + place_ref[:top], rows).astype(jnp.int32)
+
+    gate_pre = pre_ref[:, :width].astype(F32)
+    up_pre = pre_ref[:, width:].astype(F32)
+    sigma = jax.nn.sigmoid(gate_pre)
+    own = gate[pl.ds(pl.multiple_of(step * tile, tile), tile), :]
+    out_ref[:, :width] = (own * up_pre * (sigma * (1.0 + gate_pre * (1.0 - sigma)))).astype(BF16)
+    out_ref[:, width:] = (own * (gate_pre * sigma)).astype(BF16)
+
+
+def factors(place, gates, flat_pre, cap):
+    rows, both = flat_pre.shape
+    tile = rows // 4
+    whole = lambda a: pl.BlockSpec(a.shape, lambda i: (0, 0))
     return pl.pallas_call(
-        lambda *refs: columns_kernel(cap, *refs),
-        in_specs=[VMEM] * 2,
-        out_specs=VMEM,
-        out_shape=jax.ShapeDtypeStruct((gates.size, 2), F32),
+        lambda *refs: factors_kernel(cap, *refs),
+        grid=(4,),
+        in_specs=[whole(place), whole(gates.T), pl.BlockSpec((tile, both), lambda i: (i, 0))],
+        out_specs=[
+            pl.BlockSpec((tile, both), lambda i: (i, 0)),
+            pl.BlockSpec((rows, 1), lambda i: (0, 0)),
+        ],
+        out_shape=[
+            jax.ShapeDtypeStruct((rows, both), BF16),
+            jax.ShapeDtypeStruct((rows, 1), jnp.int32),
+        ],
+        scratch_shapes=[pltpu.VMEM((rows, 1), F32)],
         compiler_params=params(16),
-        name="columns",
-    )(place, gates.T)
+        name="factors",
+    )(place, gates.T, flat_pre)
 
 
 def picks(chunk, cap, tokens):
@@ -284,7 +306,7 @@
             pltpu.SemaphoreType.DMA((5,)),
             pltpu.SemaphoreType.DMA((count,)),
         ],
-        compiler_params=params(52),
+        compiler_params=params(53),
         cost_estimate=cost(2 * every * model * 6 * width, 4 * every * model),
         name="middle",
     )(info, *sources, *weights, hidden)
@@ -337,30 +359,24 @@
     )(*sources, rest)
 
 
-def finish_kernel(column_ref, pre_ref, back_ref, out_ref):
-    rows, both = pre_ref.shape
+def finish_kernel(column_ref, factors_ref, back_ref, out_ref):
+    rows, both = factors_ref.shape
     width = both // 2
     slots = back_ref.shape[0]
-    place = column_ref[:, 1:2].astype(jnp.int32)
-    pick = ones_where(number((rows, slots), 1) == place)
-    slope = dot(pick, back_ref[...]) * column_ref[:, 0:1]
-    gate_pre = pre_ref[:, :width].astype(F32)
-    up_pre = pre_ref[:, width:].astype(F32)
-    sigma = jax.nn.sigmoid(gate_pre)
-    out_ref[:, :width] = (
-        slope * up_pre * (sigma * (1.0 + gate_pre * (1.0 - sigma)))
-    ).astype(BF16)
-    out_ref[:, width:] = (slope * (gate_pre * sigma)).astype(BF16)
-
-
-def finish(column, flat_pre, back):
-    rows, both = flat_pre.shape
-    tile = rows // 4
+    pick = ones_where(number((rows, slots), 1) == column_ref[...])
+    slope = dot(pick, back_ref[...])
+    out_ref[:, :width] = (slope * factors_ref[:, :width].astype(F32)).astype(BF16)
+    out_ref[:, width:] = (slope * factors_ref[:, width:].astype(F32)).astype(BF16)
+
+
+def finish(column, scale, back):
+    rows, both = scale.shape
+    tile = rows // 2
     return pl.pallas_call(
         finish_kernel,
-        grid=(4,),
+        grid=(2,),
         in_specs=[
-            pl.BlockSpec((tile, 2), lambda i: (i, 0)),
+            pl.BlockSpec((tile, 1), lambda i: (i, 0)),
             pl.BlockSpec((tile, both), lambda i: (i, 0)),
             pl.BlockSpec(back.shape, lambda i: (0, 0)),
         ],
@@ -369,7 +385,7 @@
         compiler_params=params(32),
         cost_estimate=cost(rows * both, 4 * rows * both),
         name="finish",
-    )(column, flat_pre, back)
+    )(column, scale, back)
 
 
 def per_device(grad_out, gates, expert_ids, pre_acts, w2):
@@ -439,8 +455,8 @@
     )
     total = lax.psum_scatter(total, "dp", scatter_dimension=1, tiled=True)
 
-    column = columns(place, gates, cap)
-    pre_grad = finish(column, flat_pre, back)
+    scale, column = factors(place, gates, flat_pre, cap)
+    pre_grad = finish(column, scale, back)
     return pre_grad.reshape(tokens, top, 2 * width), total[None].astype(BF16)
 
 

time: 104 us -> 102 us (0.981)
  waiting for transfers between devices: 41 us -> 39.4 us
  local copies, waits for them, and re-layouts: 2.24 us -> 1.02 us
    ppermute x19, waiting for transfers between devices: 40.9 us -> 39.4 us  [swap(): return lax.ppermute(value, 'expert', [(j, j ^ bit) for j in range(count)])]
    unnamed x26 -> x42, local copies, waits for them, and re-layouts: 2.1 us -> 0.88 us
  transfers between devices with their start and end apart: 21 -> 21, of which waited for: 13 -> 12; matrix products, arithmetic and copies ran while one was open for 3% -> 3% of each run, Pallas kernels for 11% -> 12%
where the time goes in v5:
time: 102 us
  waiting for transfers between devices  39.4 us (39%)
  starting transfers between devices  32.1 us (31%)
  Pallas kernels  25.5 us (25%)
  other arithmetic  2.73 us (3%)
  local copies, waits for them, and re-layouts  1.02 us (1%)
    ppermute x19, waiting for transfers between devices, swap(): return lax.ppermute(value, 'expert', [(j, j ^ bit) for j in range(count)])  39.4 us
    ppermute x19, starting transfers between devices, swap(): return lax.ppermute(value, 'expert', [(j, j ^ bit) for j in range(count)])  22.6 us
    pallas_call x1, Pallas kernels, middle(): pl.pallas_call(lambda *refs: middle_kernel(cap, count, *refs), in_specs=[...  10.5 us
    all_to_all x2, starting transfers between devices, exchange(): lax.all_to_all(chunks, 'expert', split_axis=0, concat_axis=0, tiled=True,...  9.52 us
    pallas_call x1, Pallas kernels, pack_hidden(): pl.pallas_call(lambda *refs: pack_kernel(cap, *refs), in_specs=[VMEM, VME...  5.35 us
    pallas_call x1, Pallas kernels, keep_partials(): pl.pallas_call(lambda *refs: keep_kernel(count, *refs), in_specs=[ANY] *...  4.52 us
    pallas_call x1, Pallas kernels, finish(): pl.pallas_call(finish_kernel, grid=(2,), in_specs=[pl.BlockSpec((tile, 1)...  2.95 us
    pallas_call x1, Pallas kernels, factors(): pl.pallas_call(lambda *refs: factors_kernel(cap, *refs), grid=(4,), in_sp...  2.13 us
  transfers between devices with their start and end apart: 21, of which 12 were waited for; matrix products, arithmetic and copies ran while one was open for 3% of the time, Pallas kernels for 12%

profile of v5, /device:TPU:0, one launch (start us, length us, event | category | flops | bytes accessed | tf_op | source)
XLA Modules:
  0.0 101.7 jit_solution(10703744992998372372)
XLA Ops:
  0.6 4.1 %collective-permute-start = (bf16[128,1024]{1,0:T(8,128)(2,1)}, bf16[128,1024]{1,0:T(8,128)(2,1)S(1)}, u32[]{:S(2)}, u32[]{:S(2)}) collective-permute-start(bf16[128,1024]{1,0:T(8,128)(2,1)} %refs_0_), channel_id=1, source_target_pairs={{0,16},{1,17},{2,18},{3,19},{4,20},{5,21},{6,22},{7,23},{8,24},{9,... | collective-permute-start | bytes 786440 | tf_op jit(solution)/shard_map/ppermute | solution.py:25
  4.7 1.6 %collective-permute-start.1 = (bf16[128,1024]{1,0:T(8,128)(2,1)}, bf16[128,1024]{1,0:T(8,128)(2,1)S(1)}, u32[]{:S(2)}, u32[]{:S(2)}) collective-permute-start(bf16[128,1024]{1,0:T(8,128)(2,1)} %refs_0_), channel_id=1, source_target_pairs={{0,8},{1,9},{2,10},{3,11},{4,12},{5,13},{6,14},{7,15},{8,0},{9,1},... | collective-permute-start | bytes 786440 | tf_op jit(solution)/shard_map/ppermute | solution.py:25
  6.3 0.1 stack.23.refs_0_
  6.4 5.3 %pack_hidden.1 = (bf16[8,192,384]{2,1,0:T(8,128)(2,1)}, f32[16,128]{1,0:T(8,128)}) custom-call(s32[8,128]{1,0:T(8,128)} %bitcast.24, f32[8,128]{1,0:T(8,128)} %bitcast.20, bf16[1024,768]{1,0:T(8,128)(2,1)} %bitcast.18), custom_call_target="tpu_custom_call" | custom-call | flops 1207959552 | bytes 1572864 | tf_op jit(solution)/shard_map/pack_hidden/pallas_call | solution.py:127
  11.7 0.0 copy-start.13
  11.8 5.2 %collective-permute-done.refs_2_.refs_1_ = bf16[128,1024]{1,0:T(8,128)(2,1)S(1)} collective-permute-done((bf16[128,1024]{1,0:T(8,128)(2,1)}, bf16[128,1024]{1,0:T(8,128)(2,1)S(1)}, u32[]{:S(2)}, u32[]{:S(2)}) %collective-permute-start) | collective-permute-done | bytes 262176 | tf_op jit(solution)/shard_map/ppermute | solution.py:25
  17.0 0.2 collective-permute-done.1.refs_3_.refs_2_
  17.2 4.7 %all-to-all-start = ((bf16[8,192,384]{2,1,0:T(8,128)(2,1)}), bf16[8,192,384]{2,1,0:T(8,128)(2,1)}, u32[]{:S(2)}, u32[]{:S(2)}) async-start(bf16[8,192,384]{2,1,0:T(8,128)(2,1)} %get-tuple-element.41), calls=%async_computation | async-start | bytes 2359296 | tf_op jit(solution)/shard_map/all_to_all | solution.py:405
  21.8 0.1 slice_bitcast_fusion
  21.9 1.6 %collective-permute-start.5 = (bf16[192,1024]{1,0:T(8,128)(2,1)S(1)}, bf16[192,1024]{1,0:T(8,128)(2,1)S(1)}, u32[]{:S(2)}, u32[]{:S(2)}) collective-permute-start(bf16[192,1024]{1,0:T(8,128)(2,1)S(1)} %get-tuple-element.56), channel_id=1, source_target_pairs={{0,2},{1,3},{2,0},{3,1},{4,6},{5,7},{6,4},{7,5},{8,10},{9,11},{10,... | collective-permute-start | bytes 1179656 | tf_op jit(solution)/shard_map/ppermute | solution.py:25
  23.4 1.5 %collective-permute-start.7 = (bf16[192,1024]{1,0:T(8,128)(2,1)S(1)}, bf16[192,1024]{1,0:T(8,128)(2,1)S(1)}, u32[]{:S(2)}, u32[]{:S(2)}) collective-permute-start(bf16[192,1024]{1,0:T(8,128)(2,1)S(1)} %get-tuple-element.57), channel_id=1, source_target_pairs={{0,4},{1,5},{2,6},{3,7},{4,0},{5,1},{6,2},{7,3},{8,12},{9,13},{10,... | collective-permute-start | bytes 1179656 | tf_op jit(solution)/shard_map/ppermute | solution.py:25
  25.0 0.5 collective-permute-start.4
  25.5 0.5 collective-permute-start.3
  26.0 7.9 %collective-permute-done.5.refs_10_ = bf16[192,1024]{1,0:T(8,128)(2,1)S(1)} collective-permute-done((bf16[192,1024]{1,0:T(8,128)(2,1)S(1)}, bf16[192,1024]{1,0:T(8,128)(2,1)S(1)}, u32[]{:S(2)}, u32[]{:S(2)}) %collective-permute-start.5) | collective-permute-done | bytes 393248 | tf_op jit(solution)/shard_map/ppermute | solution.py:25
  33.9 1.5 %collective-permute-start.6 = (bf16[192,1024]{1,0:T(8,128)(2,1)S(1)}, bf16[192,1024]{1,0:T(8,128)(2,1)S(1)}, u32[]{:S(2)}, u32[]{:S(2)}) collective-permute-start(bf16[192,1024]{1,0:T(8,128)(2,1)S(1)} %collective-permute-done.5.refs_10_), channel_id=1, source_target_pairs={{0,4},{1,5},{2,6},{3,7},{4,0},{5,1},{6,2},{7,3},{8,12},{9,13},{10,... | collective-permute-start | bytes 1179656 | tf_op jit(solution)/shard_map/ppermute | solution.py:25
  35.4 0.0 collective-permute-done.7.refs_13_
  35.4 1.5 %collective-permute-start.8 = (bf16[192,1024]{1,0:T(8,128)(2,1)S(1)}, bf16[192,1024]{1,0:T(8,128)(2,1)S(1)}, u32[]{:S(2)}, u32[]{:S(2)}) collective-permute-start(bf16[192,1024]{1,0:T(8,128)(2,1)S(1)} %collective-permute-done.7.refs_13_), channel_id=1, source_target_pairs={{0,2},{1,3},{2,0},{3,1},{4,6},{5,7},{6,4},{7,5},{8,10},{9,11},{10,... | collective-permute-start | bytes 1179656 | tf_op jit(solution)/shard_map/ppermute | solution.py:25
  36.9 2.1 %collective-permute-start.2 = (bf16[128,1024]{1,0:T(8,128)(2,1)S(1)}, bf16[128,1024]{1,0:T(8,128)(2,1)S(1)}, u32[]{:S(2)}, u32[]{:S(2)}) collective-permute-start(bf16[128,1024]{1,0:T(8,128)(2,1)S(1)} %collective-permute-done.refs_2_.refs_1_), channel_id=1, source_target_pairs={{0,8},{1,9},{2,10},{3,11},{4,12},{5,13},{6,14},{7,15},{8,0},{9,1},... | collective-permute-start | bytes 786440 | tf_op jit(solution)/shard_map/ppermute | solution.py:25
  38.9 4.9 %collective-permute-done.4.refs_12_ = bf16[192,1024]{1,0:T(8,128)(2,1)S(1)} collective-permute-done((bf16[192,1024]{1,0:T(8,128)(2,1)S(1)}, bf16[192,1024]{1,0:T(8,128)(2,1)S(1)}, u32[]{:S(2)}, u32[]{:S(2)}) %collective-permute-start.4) | collective-permute-done | bytes 393248 | tf_op jit(solution)/shard_map/ppermute | solution.py:25
  43.8 0.0 collective-permute-start.10
  43.8 0.0 collective-permute-done.3.refs_11_
  43.8 0.6 collective-permute-start.9
  44.4 3.1 %collective-permute-done.2.refs_4_.refs_3_ = bf16[128,1024]{1,0:T(8,128)(2,1)S(1)} collective-permute-done((bf16[128,1024]{1,0:T(8,128)(2,1)S(1)}, bf16[128,1024]{1,0:T(8,128)(2,1)S(1)}, u32[]{:S(2)}, u32[]{:S(2)}) %collective-permute-start.2) | collective-permute-done | bytes 262176 | tf_op jit(solution)/shard_map/ppermute | solution.py:25
  47.5 0.0 collective-permute-start.11
  47.5 4.0 %collective-permute-done.6.refs_14_ = bf16[192,1024]{1,0:T(8,128)(2,1)S(1)} collective-permute-done((bf16[192,1024]{1,0:T(8,128)(2,1)S(1)}, bf16[192,1024]{1,0:T(8,128)(2,1)S(1)}, u32[]{:S(2)}, u32[]{:S(2)}) %collective-permute-start.6) | collective-permute-done | bytes 393248 | tf_op jit(solution)/shard_map/ppermute | solution.py:25
  51.5 0.0 collective-permute-done.8.refs_15_
  51.5 0.1 collective-permute-start.12
  51.6 0.0 collective-permute-done.9.refs_5_.refs_4_
  51.6 0.0 collective-permute-done.11.refs_7_.refs_6_
  51.7 0.0 collective-permute-done.10.refs_6_.refs_5_
  51.7 0.6 copy-done.18
  52.3 0.1 copy-done.19
  52.5 0.8 collective-permute-done.12.refs_8_.refs_7_
  53.3 0.0 all-to-all-done.refs_16_
  53.3 0.0 copy-done.15
  53.3 0.0 copy-done.16
  53.3 0.0 copy-done.17
  53.3 0.0 copy-done.4
  53.3 0.0 copy-done.8
  53.3 0.0 copy-done.10
  53.3 10.5 %middle.1 = (bf16[8,192,384]{2,1,0:T(8,128)(2,1)}, bf16[192,1024]{1,0:T(8,128)(2,1)}, bf16[192,1024]{1,0:T(8,128)(2,1)}, bf16[192,1024]{1,0:T(8,128)(2,1)}, bf16...) custom-call(s32[5]{0:T(128)S(1)} %stack.23.refs_0_, bf16[128,1024]{1,0:T(8,128)(2,1)S(1)} %copy-done.3, ...), custom_call_target="tpu_custom_call" | custom-call | flops 4831838208 | bytes 4194304 | tf_op jit(solution)/shard_map/middle/pallas_call | solution.py:287
  63.9 4.9 %all-to-all-start.1 = ((bf16[8,192,384]{2,1,0:T(8,128)(2,1)}), bf16[8,192,384]{2,1,0:T(8,128)(2,1)S(1)}, u32[]{:S(2)}, u32[]{:S(2)}) async-start(bf16[8,192,384]{2,1,0:T(8,128)(2,1)} %get-tuple-element.42), calls=%async_computation.1 | async-start | bytes 2359296 | tf_op jit(solution)/shard_map/all_to_all | solution.py:405
  68.8 0.5 collective-permute-start.15
  69.3 1.5 %collective-permute-start.16 = (bf16[192,1024]{1,0:T(8,128)(2,1)S(1)}, bf16[192,1024]{1,0:T(8,128)(2,1)S(1)}, u32[]{:S(2)}, u32[]{:S(2)}) collective-permute-start(bf16[192,1024]{1,0:T(8,128)(2,1)S(1)} %copy-done.20), channel_id=1, source_target_pairs={{0,4},{1,5},{2,6},{3,7},{4,0},{5,1},{6,2},{7,3},{8,12},{9,13},{10,... | collective-permute-start | bytes 1179656 | tf_op jit(solution)/shard_map/ppermute | solution.py:25
  70.8 1.5 %collective-permute-start.13 = (bf16[192,1024]{1,0:T(8,128)(2,1)}, bf16[192,1024]{1,0:T(8,128)(2,1)S(1)}, u32[]{:S(2)}, u32[]{:S(2)}) collective-permute-start(bf16[192,1024]{1,0:T(8,128)(2,1)} %get-tuple-element.45), channel_id=1, source_target_pairs={{0,2},{1,3},{2,0},{3,1},{4,6},{5,7},{6,4},{7,5},{8,10},{9,11},{10,... | collective-permute-start | bytes 1179656 | tf_op jit(solution)/shard_map/ppermute | solution.py:25
  72.3 0.5 collective-permute-start.14
  72.8 4.5 %keep_partials.1 = (f32[384,1024]{1,0:T(8,128)}, bf16[384,1024]{1,0:T(8,128)(2,1)}) custom-call(bf16[128,1024]{1,0:T(8,128)(2,1)S(1)} %copy-done.3, bf16[128,1024]{1,0:T(8,128)(2,1)S(1)} %collective-permute-done.refs_2_.refs_1_, bf16[128,1024]{1,0:T(8,128)(2,1)S(1)} %collective-permute-done.1.refs_3_.refs_2_, bf16[128,1024]{1,0:T(8,128)(2,1)S(1)} %copy-done.5, ...), custom_call_target="tpu_custom_call" | custom-call | flops 1610612736 | bytes 4194304 | tf_op jit(solution)/shard_map/keep_partials/pallas_call | solution.py:339
  77.4 0.0 copy-start
  77.4 0.0 copy-start.2
  77.4 3.5 %collective-permute-done.15 = bf16[192,1024]{1,0:T(8,128)(2,1)S(1)} collective-permute-done((bf16[192,1024]{1,0:T(8,128)(2,1)}, bf16[192,1024]{1,0:T(8,128)(2,1)S(1)}, u32[]{:S(2)}, u32[]{:S(2)}) %collective-permute-start.15) | collective-permute-done | bytes 393248 | tf_op jit(solution)/shard_map/ppermute | solution.py:25
  80.9 0.4 collective-permute-done.16
  81.3 1.4 %add_convert_fusion.1 = (bf16[192,1024]{1,0:T(8,128)(2,1)S(1)}, bf16[192,1024]{1,0:T(8,128)(2,1)S(1)}) fusion(bf16[192,1024]{1,0:T(8,128)(2,1)S(1)} %collective-permute-done.15, bf16[384,1024]{1,0:T(8,128)(2,1)} %get-tuple-element.48, bf16[192,1024]{1,0:T(8,128)(2,1)S(1)} %collective-permute-done.16), kind=kLoop, calls=%fused_computation.6 | loop fusion | flops 1572864 | bytes 2359296 | tf_op jit(solution)/shard_map/convert_element_type | solution.py:446
  82.7 1.6 %collective-permute-start.17 = (bf16[192,1024]{1,0:T(8,128)(2,1)S(1)}, bf16[192,1024]{1,0:T(8,128)(2,1)S(1)}, u32[]{:S(2)}, u32[]{:S(2)}) collective-permute-start(bf16[192,1024]{1,0:T(8,128)(2,1)S(1)} %get-tuple-element.54), channel_id=1, source_target_pairs={{0,4},{1,5},{2,6},{3,7},{4,0},{5,1},{6,2},{7,3},{8,12},{9,13},{10,... | collective-permute-start | bytes 1179656 | tf_op jit(solution)/shard_map/ppermute | solution.py:25
  84.3 1.5 %collective-permute-start.18 = (bf16[192,1024]{1,0:T(8,128)(2,1)S(1)}, bf16[192,1024]{1,0:T(8,128)(2,1)S(1)}, u32[]{:S(2)}, u32[]{:S(2)}) collective-permute-start(bf16[192,1024]{1,0:T(8,128)(2,1)S(1)} %get-tuple-element.55), channel_id=1, source_target_pairs={{0,2},{1,3},{2,0},{3,1},{4,6},{5,7},{6,4},{7,5},{8,10},{9,11},{10,... | collective-permute-start | bytes 1179656 | tf_op jit(solution)/shard_map/ppermute | solution.py:25
  85.8 2.1 %factors.1 = (bf16[1024,768]{1,0:T(8,128)(2,1)S(1)}, s32[1024,1]{1,0:T(8,128)S(1)}) custom-call(f32[16,128]{1,0:T(8,128)S(1)} %copy-done.1, f32[8,128]{1,0:T(8,128)S(1)} %bitcast.21, bf16[1024,768]{1,0:T(8,128)(2,1)S(1)} %bitcast.19), custom_call_target="tpu_custom_call" | custom-call | tf_op jit(solution)/shard_map/factors/pallas_call | solution.py:170
  87.9 1.4 %collective-permute-done.13 = bf16[192,1024]{1,0:T(8,128)(2,1)S(1)} collective-permute-done((bf16[192,1024]{1,0:T(8,128)(2,1)}, bf16[192,1024]{1,0:T(8,128)(2,1)S(1)}, u32[]{:S(2)}, u32[]{:S(2)}) %collective-permute-start.13) | collective-permute-done | bytes 393248 | tf_op jit(solution)/shard_map/ppermute | solution.py:25
  89.3 0.4 collective-permute-done.14
  89.7 7.7 %collective-permute-done.17 = bf16[192,1024]{1,0:T(8,128)(2,1)S(1)} collective-permute-done((bf16[192,1024]{1,0:T(8,128)(2,1)S(1)}, bf16[192,1024]{1,0:T(8,128)(2,1)S(1)}, u32[]{:S(2)}, u32[]{:S(2)}) %collective-permute-start.17) | collective-permute-done | bytes 393248 | tf_op jit(solution)/shard_map/ppermute | solution.py:25
  97.4 0.1 convert_add_fusion.1
  97.5 0.0 collective-permute-done.18
  97.5 0.1 convert_add_fusion
  97.6 1.1 %fusion.1 = bf16[1,384,1024]{2,1,0:T(8,128)(2,1)} fusion(f32[384,1024]{1,0:T(8,128)S(1)} %copy-done.12, f32[192,1024]{1,0:T(8,128)S(1)} %convert_add_fusion, f32[192,1024]{1,0:T(8,128)S(1)} %convert_add_fusion.1), kind=kLoop, calls=%fused_computation.2 | loop fusion | flops 1179648 | bytes 3932160 | tf_op jit(solution)/shard_map/convert_element_type | solution.py:460
  98.7 0.0 all-to-all-done.1
  98.8 2.9 %finish.1 = bf16[1024,768]{1,0:T(8,128)(2,1)} custom-call(s32[1024,1]{1,0:T(8,128)S(1)} %get-tuple-element.29.column_ref, bf16[1024,768]{1,0:T(8,128)(2,1)S(1)} %get-tuple-element.30.factors_ref, bf16[1536,384]{1,0:T(8,128)(2,1)S(1)} %bitcast.17), custom_call_target="tpu_custom_call" | custom-call | flops 786432 | bytes 3145728 | tf_op jit(solution)/shard_map/finish/pallas_call | solution.py:375
  (31 shorter events, 0.1 us)
Async XLA Ops:
  0.6 16.3 %collective-permute-start = (bf16[128,1024]{1,0:T(8,128)(2,1)}, bf16[128,1024]{1,0:T(8,128)(2,1)S(1)}, u32[]{:S(2)}, u32[]{:S(2)}) collective-permute-start(bf16[128,1024]{1,0:T(8,128)(2,1)} %refs_0_), channel_id=1, source_target_pairs={{0,16},{1,17},{2,18},{3,19},{4,20},{5,21},{6,22},{7,23},{8,24},{9,... | collective-permute-start | bytes 786440 | tf_op jit(solution)/shard_map/ppermute | solution.py:25
  4.7 12.4 %collective-permute-start.1 = (bf16[128,1024]{1,0:T(8,128)(2,1)}, bf16[128,1024]{1,0:T(8,128)(2,1)S(1)}, u32[]{:S(2)}, u32[]{:S(2)}) collective-permute-start(bf16[128,1024]{1,0:T(8,128)(2,1)} %refs_0_), channel_id=1, source_target_pairs={{0,8},{1,9},{2,10},{3,11},{4,12},{5,13},{6,14},{7,15},{8,0},{9,1},... | collective-permute-start | bytes 786440 | tf_op jit(solution)/shard_map/ppermute | solution.py:25
  11.7 10.1 %copy-start.13 = (bf16[1,384,1024]{2,1,0:T(8,128)(2,1)S(1)}, bf16[1,384,1024]{2,1,0:T(8,128)(2,1)}, u32[]{:S(2)}) copy-start(bf16[1,384,1024]{2,1,0:T(8,128)(2,1)} %param.9) | copy-start | bytes 2359300
  17.2 26.7 %copy-start.3 = (bf16[128,1024]{1,0:T(8,128)(2,1)S(1)}, bf16[128,1024]{1,0:T(8,128)(2,1)}, u32[]{:S(2)}) copy-start(bf16[128,1024]{1,0:T(8,128)(2,1)} %refs_0_) | copy-start | bytes 786436
  17.2 36.1 %all-to-all-start = ((bf16[8,192,384]{2,1,0:T(8,128)(2,1)}), bf16[8,192,384]{2,1,0:T(8,128)(2,1)}, u32[]{:S(2)}, u32[]{:S(2)}) async-start(bf16[8,192,384]{2,1,0:T(8,128)(2,1)} %get-tuple-element.41), calls=%async_computation | async-start | bytes 2359296 | tf_op jit(solution)/shard_map/all_to_all | solution.py:405
  21.9 12.0 %collective-permute-start.5 = (bf16[192,1024]{1,0:T(8,128)(2,1)S(1)}, bf16[192,1024]{1,0:T(8,128)(2,1)S(1)}, u32[]{:S(2)}, u32[]{:S(2)}) collective-permute-start(bf16[192,1024]{1,0:T(8,128)(2,1)S(1)} %get-tuple-element.56), channel_id=1, source_target_pairs={{0,2},{1,3},{2,0},{3,1},{4,6},{5,7},{6,4},{7,5},{8,10},{9,11},{10,... | collective-permute-start | bytes 1179656 | tf_op jit(solution)/shard_map/ppermute | solution.py:25
  23.4 11.9 %collective-permute-start.7 = (bf16[192,1024]{1,0:T(8,128)(2,1)S(1)}, bf16[192,1024]{1,0:T(8,128)(2,1)S(1)}, u32[]{:S(2)}, u32[]{:S(2)}) collective-permute-start(bf16[192,1024]{1,0:T(8,128)(2,1)S(1)} %get-tuple-element.57), channel_id=1, source_target_pairs={{0,4},{1,5},{2,6},{3,7},{4,0},{5,1},{6,2},{7,3},{8,12},{9,13},{10,... | collective-permute-start | bytes 1179656 | tf_op jit(solution)/shard_map/ppermute | solution.py:25
  25.0 18.9 %collective-permute-start.4 = (bf16[192,1024]{1,0:T(8,128)(2,1)S(1)}, bf16[192,1024]{1,0:T(8,128)(2,1)S(1)}, u32[]{:S(2)}, u32[]{:S(2)}) collective-permute-start(bf16[192,1024]{1,0:T(8,128)(2,1)S(1)} %get-tuple-element.56), channel_id=1, source_target_pairs={{0,4},{1,5},{2,6},{3,7},{4,0},{5,1},{6,2},{7,3},{8,12},{9,13},{10,... | collective-permute-start | bytes 1179656 | tf_op jit(solution)/shard_map/ppermute | solution.py:25
  25.5 18.4 %collective-permute-start.3 = (bf16[192,1024]{1,0:T(8,128)(2,1)S(1)}, bf16[192,1024]{1,0:T(8,128)(2,1)S(1)}, u32[]{:S(2)}, u32[]{:S(2)}) collective-permute-start(bf16[192,1024]{1,0:T(8,128)(2,1)S(1)} %get-tuple-element.57), channel_id=1, source_target_pairs={{0,2},{1,3},{2,0},{3,1},{4,6},{5,7},{6,4},{7,5},{8,10},{9,11},{10,... | collective-permute-start | bytes 1179656 | tf_op jit(solution)/shard_map/ppermute | solution.py:25
  33.9 19.4 %copy-start.14 = (bf16[192,1024]{1,0:T(8,128)(2,1)}, bf16[192,1024]{1,0:T(8,128)(2,1)S(1)}, u32[]{:S(2)}) copy-start(bf16[192,1024]{1,0:T(8,128)(2,1)S(1)} %collective-permute-done.5.refs_10_) | copy-start | bytes 1179652
  33.9 17.7 %collective-permute-start.6 = (bf16[192,1024]{1,0:T(8,128)(2,1)S(1)}, bf16[192,1024]{1,0:T(8,128)(2,1)S(1)}, u32[]{:S(2)}, u32[]{:S(2)}) collective-permute-start(bf16[192,1024]{1,0:T(8,128)(2,1)S(1)} %collective-permute-done.5.refs_10_), channel_id=1, source_target_pairs={{0,4},{1,5},{2,6},{3,7},{4,0},{5,1},{6,2},{7,3},{8,12},{9,13},{10,... | collective-permute-start | bytes 1179656 | tf_op jit(solution)/shard_map/ppermute | solution.py:25
  35.4 17.9 %copy-start.15 = (bf16[192,1024]{1,0:T(8,128)(2,1)}, bf16[192,1024]{1,0:T(8,128)(2,1)S(1)}, u32[]{:S(2)}) copy-start(bf16[192,1024]{1,0:T(8,128)(2,1)S(1)} %collective-permute-done.7.refs_13_) | copy-start | bytes 1179652
  35.4 16.1 %collective-permute-start.8 = (bf16[192,1024]{1,0:T(8,128)(2,1)S(1)}, bf16[192,1024]{1,0:T(8,128)(2,1)S(1)}, u32[]{:S(2)}, u32[]{:S(2)}) collective-permute-start(bf16[192,1024]{1,0:T(8,128)(2,1)S(1)} %collective-permute-done.7.refs_13_), channel_id=1, source_target_pairs={{0,2},{1,3},{2,0},{3,1},{4,6},{5,7},{6,4},{7,5},{8,10},{9,11},{10,... | collective-permute-start | bytes 1179656 | tf_op jit(solution)/shard_map/ppermute | solution.py:25
  36.9 10.7 %collective-permute-start.2 = (bf16[128,1024]{1,0:T(8,128)(2,1)S(1)}, bf16[128,1024]{1,0:T(8,128)(2,1)S(1)}, u32[]{:S(2)}, u32[]{:S(2)}) collective-permute-start(bf16[128,1024]{1,0:T(8,128)(2,1)S(1)} %collective-permute-done.refs_2_.refs_1_), channel_id=1, source_target_pairs={{0,8},{1,9},{2,10},{3,11},{4,12},{5,13},{6,14},{7,15},{8,0},{9,1},... | collective-permute-start | bytes 786440 | tf_op jit(solution)/shard_map/ppermute | solution.py:25
  43.8 9.5 %copy-start.16 = (bf16[192,1024]{1,0:T(8,128)(2,1)}, bf16[192,1024]{1,0:T(8,128)(2,1)S(1)}, u32[]{:S(2)}) copy-start(bf16[192,1024]{1,0:T(8,128)(2,1)S(1)} %collective-permute-done.4.refs_12_) | copy-start | bytes 1179652
  43.8 7.8 %collective-permute-start.10 = (bf16[128,1024]{1,0:T(8,128)(2,1)S(1)}, bf16[128,1024]{1,0:T(8,128)(2,1)S(1)}, u32[]{:S(2)}, u32[]{:S(2)}) collective-permute-start(bf16[128,1024]{1,0:T(8,128)(2,1)S(1)} %collective-permute-done.refs_2_.refs_1_), channel_id=1, source_target_pairs={{0,1},{1,0},{2,3},{3,2},{4,5},{5,4},{6,7},{7,6},{8,9},{9,8},{10,11... | collective-permute-start | bytes 786440 | tf_op jit(solution)/shard_map/ppermute | solution.py:25
  43.8 9.5 %copy-start.17 = (bf16[192,1024]{1,0:T(8,128)(2,1)}, bf16[192,1024]{1,0:T(8,128)(2,1)S(1)}, u32[]{:S(2)}) copy-start(bf16[192,1024]{1,0:T(8,128)(2,1)S(1)} %collective-permute-done.3.refs_11_) | copy-start | bytes 1179652
  43.8 7.8 %collective-permute-start.9 = (bf16[128,1024]{1,0:T(8,128)(2,1)S(1)}, bf16[128,1024]{1,0:T(8,128)(2,1)S(1)}, u32[]{:S(2)}, u32[]{:S(2)}) collective-permute-start(bf16[128,1024]{1,0:T(8,128)(2,1)S(1)} %copy-done.3), channel_id=1, source_target_pairs={{0,1},{1,0},{2,3},{3,2},{4,5},{5,4},{6,7},{7,6},{8,9},{9,8},{10,11... | collective-permute-start | bytes 786440 | tf_op jit(solution)/shard_map/ppermute | solution.py:25
  47.5 5.8 %copy-start.4 = (bf16[128,1024]{1,0:T(8,128)(2,1)}, bf16[128,1024]{1,0:T(8,128)(2,1)S(1)}, u32[]{:S(2)}) copy-start(bf16[128,1024]{1,0:T(8,128)(2,1)S(1)} %collective-permute-done.2.refs_4_.refs_3_) | copy-start | bytes 786436
  47.5 4.1 %collective-permute-start.11 = (bf16[128,1024]{1,0:T(8,128)(2,1)S(1)}, bf16[128,1024]{1,0:T(8,128)(2,1)S(1)}, u32[]{:S(2)}, u32[]{:S(2)}) collective-permute-start(bf16[128,1024]{1,0:T(8,128)(2,1)S(1)} %collective-permute-done.1.refs_3_.refs_2_), channel_id=1, source_target_pairs={{0,1},{1,0},{2,3},{3,2},{4,5},{5,4},{6,7},{7,6},{8,9},{9,8},{10,11... | collective-permute-start | bytes 786440 | tf_op jit(solution)/shard_map/ppermute | solution.py:25
  51.5 0.8 copy-start.18
  51.5 0.9 copy-start.19
  51.5 1.7 %collective-permute-start.12 = (bf16[128,1024]{1,0:T(8,128)(2,1)S(1)}, bf16[128,1024]{1,0:T(8,128)(2,1)}, u32[]{:S(2)}, u32[]{:S(2)}) collective-permute-start(bf16[128,1024]{1,0:T(8,128)(2,1)S(1)} %collective-permute-done.2.refs_4_.refs_3_), channel_id=1, source_target_pairs={{0,1},{1,0},{2,3},{3,2},{4,5},{5,4},{6,7},{7,6},{8,9},{9,8},{10,11... | collective-permute-start | bytes 786440 | tf_op jit(solution)/shard_map/ppermute | solution.py:25
  51.6 1.7 %copy-start.8 = (bf16[128,1024]{1,0:T(8,128)(2,1)}, bf16[128,1024]{1,0:T(8,128)(2,1)S(1)}, u32[]{:S(2)}) copy-start(bf16[128,1024]{1,0:T(8,128)(2,1)S(1)} %collective-permute-done.9.refs_5_.refs_4_) | copy-start | bytes 786436
  51.6 1.7 %copy-start.10 = (bf16[128,1024]{1,0:T(8,128)(2,1)}, bf16[128,1024]{1,0:T(8,128)(2,1)S(1)}, u32[]{:S(2)}) copy-start(bf16[128,1024]{1,0:T(8,128)(2,1)S(1)} %collective-permute-done.11.refs_7_.refs_6_) | copy-start | bytes 786436
  52.5 0.9 copy-start.6
  63.9 5.4 %copy-start.20 = (bf16[192,1024]{1,0:T(8,128)(2,1)S(1)}, bf16[192,1024]{1,0:T(8,128)(2,1)}, u32[]{:S(2)}) copy-start(bf16[192,1024]{1,0:T(8,128)(2,1)} %get-tuple-element.50) | copy-start | bytes 1179652
  63.9 9.0 %copy-start.5 = (bf16[128,1024]{1,0:T(8,128)(2,1)S(1)}, bf16[128,1024]{1,0:T(8,128)(2,1)}, u32[]{:S(2)}) copy-start(bf16[128,1024]{1,0:T(8,128)(2,1)} %copy-done.4) | copy-start | bytes 786436
  63.9 9.0 %copy-start.7 = (bf16[128,1024]{1,0:T(8,128)(2,1)S(1)}, bf16[128,1024]{1,0:T(8,128)(2,1)}, u32[]{:S(2)}) copy-start(bf16[128,1024]{1,0:T(8,128)(2,1)} %copy-done.6) | copy-start | bytes 786436
  63.9 8.9 %copy-start.9 = (bf16[128,1024]{1,0:T(8,128)(2,1)S(1)}, bf16[128,1024]{1,0:T(8,128)(2,1)}, u32[]{:S(2)}) copy-start(bf16[128,1024]{1,0:T(8,128)(2,1)} %copy-done.8) | copy-start | bytes 786436
  63.9 8.9 %copy-start.11 = (bf16[128,1024]{1,0:T(8,128)(2,1)S(1)}, bf16[128,1024]{1,0:T(8,128)(2,1)}, u32[]{:S(2)}) copy-start(bf16[128,1024]{1,0:T(8,128)(2,1)} %copy-done.10) | copy-start | bytes 786436
  63.9 34.8 %all-to-all-start.1 = ((bf16[8,192,384]{2,1,0:T(8,128)(2,1)}), bf16[8,192,384]{2,1,0:T(8,128)(2,1)S(1)}, u32[]{:S(2)}, u32[]{:S(2)}) async-start(bf16[8,192,384]{2,1,0:T(8,128)(2,1)} %get-tuple-element.42), calls=%async_computation.1 | async-start | bytes 2359296 | tf_op jit(solution)/shard_map/all_to_all | solution.py:405
  68.8 12.1 %collective-permute-start.15 = (bf16[192,1024]{1,0:T(8,128)(2,1)}, bf16[192,1024]{1,0:T(8,128)(2,1)S(1)}, u32[]{:S(2)}, u32[]{:S(2)}) collective-permute-start(bf16[192,1024]{1,0:T(8,128)(2,1)} %get-tuple-element.49), channel_id=1, source_target_pairs={{0,2},{1,3},{2,0},{3,1},{4,6},{5,7},{6,4},{7,5},{8,10},{9,11},{10,... | collective-permute-start | bytes 1179656 | tf_op jit(solution)/shard_map/ppermute | solution.py:25
  69.3 11.9 %collective-permute-start.16 = (bf16[192,1024]{1,0:T(8,128)(2,1)S(1)}, bf16[192,1024]{1,0:T(8,128)(2,1)S(1)}, u32[]{:S(2)}, u32[]{:S(2)}) collective-permute-start(bf16[192,1024]{1,0:T(8,128)(2,1)S(1)} %copy-done.20), channel_id=1, source_target_pairs={{0,4},{1,5},{2,6},{3,7},{4,0},{5,1},{6,2},{7,3},{8,12},{9,13},{10,... | collective-permute-start | bytes 1179656 | tf_op jit(solution)/shard_map/ppermute | solution.py:25
  70.8 18.5 %collective-permute-start.13 = (bf16[192,1024]{1,0:T(8,128)(2,1)}, bf16[192,1024]{1,0:T(8,128)(2,1)S(1)}, u32[]{:S(2)}, u32[]{:S(2)}) collective-permute-start(bf16[192,1024]{1,0:T(8,128)(2,1)} %get-tuple-element.45), channel_id=1, source_target_pairs={{0,2},{1,3},{2,0},{3,1},{4,6},{5,7},{6,4},{7,5},{8,10},{9,11},{10,... | collective-permute-start | bytes 1179656 | tf_op jit(solution)/shard_map/ppermute | solution.py:25
  72.3 17.4 %collective-permute-start.14 = (bf16[192,1024]{1,0:T(8,128)(2,1)}, bf16[192,1024]{1,0:T(8,128)(2,1)S(1)}, u32[]{:S(2)}, u32[]{:S(2)}) collective-permute-start(bf16[192,1024]{1,0:T(8,128)(2,1)} %get-tuple-element.46), channel_id=1, source_target_pairs={{0,4},{1,5},{2,6},{3,7},{4,0},{5,1},{6,2},{7,3},{8,12},{9,13},{10,... | collective-permute-start | bytes 1179656 | tf_op jit(solution)/shard_map/ppermute | solution.py:25
  77.4 8.4 %copy-start = (bf16[128,8,768]{2,1,0:T(8,128)(2,1)S(1)}, bf16[128,8,768]{2,1,0:T(8,128)(2,1)}, u32[]{:S(2)}) copy-start(bf16[128,8,768]{2,1,0:T(8,128)(2,1)} %param.8) | copy-start | bytes 4718596
  77.4 8.4 %copy-start.1 = (f32[16,128]{1,0:T(8,128)S(1)}, f32[16,128]{1,0:T(8,128)}, u32[]{:S(2)}) copy-start(f32[16,128]{1,0:T(8,128)} %get-tuple-element.28.refs_0_) | copy-start | bytes 24580
  77.4 8.4 %copy-start.2 = (f32[128,8]{0,1:T(8,128)S(1)}, f32[128,8]{0,1:T(8,128)}, u32[]{:S(2)}) copy-start(f32[128,8]{0,1:T(8,128)} %param.6) | copy-start | bytes 12292
  82.7 14.7 %collective-permute-start.17 = (bf16[192,1024]{1,0:T(8,128)(2,1)S(1)}, bf16[192,1024]{1,0:T(8,128)(2,1)S(1)}, u32[]{:S(2)}, u32[]{:S(2)}) collective-permute-start(bf16[192,1024]{1,0:T(8,128)(2,1)S(1)} %get-tuple-element.54), channel_id=1, source_target_pairs={{0,4},{1,5},{2,6},{3,7},{4,0},{5,1},{6,2},{7,3},{8,12},{9,13},{10,... | collective-permute-start | bytes 1179656 | tf_op jit(solution)/shard_map/ppermute | solution.py:25
  84.3 13.3 %collective-permute-start.18 = (bf16[192,1024]{1,0:T(8,128)(2,1)S(1)}, bf16[192,1024]{1,0:T(8,128)(2,1)S(1)}, u32[]{:S(2)}, u32[]{:S(2)}) collective-permute-start(bf16[192,1024]{1,0:T(8,128)(2,1)S(1)} %get-tuple-element.55), channel_id=1, source_target_pairs={{0,2},{1,3},{2,0},{3,1},{4,6},{5,7},{6,4},{7,5},{8,10},{9,11},{10,... | collective-permute-start | bytes 1179656 | tf_op jit(solution)/shard_map/ppermute | solution.py:25
  87.9 9.7 %copy-start.12 = (f32[384,1024]{1,0:T(8,128)S(1)}, f32[384,1024]{1,0:T(8,128)}, u32[]{:S(2)}) copy-start(f32[384,1024]{1,0:T(8,128)} %get-tuple-element.44) | copy-start | bytes 4718596

commit v6 on v5

--- a/solution.py
+++ b/solution.py
@@ -219,7 +219,7 @@
 
 
 def middle_kernel(cap, count, info, *refs):
-    sources, w, refs = refs[:count], refs[count : count + 7], refs[count + 7 :]
+    sources, w, refs = refs[:count], refs[count:-20], refs[-20:]
     hidden, out_ref, x_diag, y_diag, x_own, y_own, rest, *refs = refs
     grads, weights, rows, spread, pick, slopes, packed, result, sem, wsem, hsem, osem, psem = refs
     me = info[0]
@@ -228,11 +228,12 @@
     half = width // 2
     hidden_copy = pltpu.make_async_copy(hidden, rows, hsem)
     token_copies = gather_copies(sources, grads, sem)
-    starts = (0,) + tuple(width + half * i for i in range(6))
-    weight_copies = [
-        pltpu.make_async_copy(ref, weights.at[pl.ds(at, ref.shape[0]), :], wsem.at[i])
-        for i, (ref, at) in enumerate(zip(w, starts))
-    ]
+    weight_copies, start = [], 0
+    for i, ref in enumerate(w):
+        weight_copies.append(
+            pltpu.make_async_copy(ref, weights.at[pl.ds(start, ref.shape[0]), :], wsem.at[i])
+        )
+        start += ref.shape[0]
     for copy in [hidden_copy] + token_copies + weight_copies:
         copy.start()
     hidden_copy.wait()
@@ -286,7 +287,7 @@
     every = count * tokens
     return pl.pallas_call(
         lambda *refs: middle_kernel(cap, count, *refs),
-        in_specs=[SMEM] + [ANY] * (count + 8),
+        in_specs=[SMEM] + [ANY] * (count + len(weights) + 1),
         out_specs=[ANY] * 6,
         out_shape=[jax.ShapeDtypeStruct(hidden.shape, BF16)]
         + [jax.ShapeDtypeStruct((width // 2, model), BF16)] * 4
@@ -301,12 +302,12 @@
             pltpu.VMEM(hidden.shape, BF16),
             pltpu.VMEM((2 * width, model), BF16),
             pltpu.SemaphoreType.DMA((count,)),
-            pltpu.SemaphoreType.DMA((7,)),
+            pltpu.SemaphoreType.DMA((len(weights),)),
             pltpu.SemaphoreType.DMA,
             pltpu.SemaphoreType.DMA((5,)),
             pltpu.SemaphoreType.DMA((count,)),
         ],
-        compiler_params=params(53),
+        compiler_params=params(52),
         cost_estimate=cost(2 * every * model * 6 * width, 4 * every * model),
         name="middle",
     )(info, *sources, *weights, hidden)
@@ -411,10 +412,14 @@
     first = [grad_out] + [swap(grad_out, bit) for bit in bits]
 
     own_w = lax.all_gather(w2, "dp", axis=2, tiled=True)[0]
-    upper, lower = own_w[:half], own_w[half:]
-    x_a, y_b = swap(upper, X_BIT), swap(lower, Y_BIT)
-    diag_a, diag_b = swap(x_a, Y_BIT), swap(y_b, X_BIT)
-    x_b, y_a = swap(lower, X_BIT), swap(upper, Y_BIT)
+    quarter = half // 2
+    x_a1, y_b1 = swap(own_w[:quarter], X_BIT), swap(own_w[half : half + quarter], Y_BIT)
+    x_a2, y_b2 = swap(own_w[quarter:half], X_BIT), swap(own_w[half + quarter :], Y_BIT)
+    diag = [
+        swap(jnp.concatenate([x_a1, x_a2], 0), Y_BIT),
+        swap(jnp.concatenate([y_b1, y_b2], 0), X_BIT),
+    ]
+    x_b, y_a = swap(own_w[half:], X_BIT), swap(own_w[:half], Y_BIT)
 
     packed, place = pack_hidden(expert_ids, gates, flat_pre, members, cap)
     masks, path = [0] + bits, {}
@@ -424,17 +429,17 @@
             path[mask | bit] = (mask, bit)
     info = jnp.stack([me] + [(me ^ mask) >> 3 for mask in masks]).astype(jnp.int32)
 
-    *first, packed, info = lax.optimization_barrier((*first, packed, info))
+    *first, x_a1, y_b1, packed, info = lax.optimization_barrier((*first, x_a1, y_b1, packed, info))
     arrived = exchange(packed)
     blocks = dict(zip([0] + bits, first))
     for mask, (known, bit) in path.items():
         blocks[mask] = swap(blocks[known], bit)
     near = list(blocks.values())
-    near[-1], x_b, y_a, diag_a, diag_b = lax.optimization_barrier((near[-1], x_b, y_a, diag_a, diag_b))
+    near[-1], x_b, y_a, *diag = lax.optimization_barrier((near[-1], x_b, y_a, *diag))
     sources = near + [swap(block, CORE_BIT) for block in near]
 
     slopes, x_diag, y_diag, x_own, y_own, rest = middle(
-        info, sources, (own_w, x_a, x_b, y_a, y_b, diag_a, diag_b), arrived
+        info, sources, (own_w, x_a1, x_a2, x_b, y_a, y_b1, y_b2, *diag), arrived
     )
     back = exchange(slopes).reshape(members * cap, width)
     own, keep = keep_partials(sources, rest)

time: 102 us -> 101 us (level)
  waiting for transfers between devices: 39.4 us -> 35.7 us
  starting transfers between devices: 32.1 us -> 34.1 us
    ppermute x19 -> x21, waiting for transfers between devices: 39.4 us -> 33.8 us  [swap(): return lax.ppermute(value, 'expert', [(j, j ^ bit) for j in range(count)])]
    ppermute x19 -> x21, starting transfers between devices: 22.6 us -> 24.8 us  [swap(): return lax.ppermute(value, 'expert', [(j, j ^ bit) for j in range(count)])]
    all_to_all x2, waiting for transfers between devices: 0.01 us -> 1.87 us  [exchange(): lax.all_to_all(chunks, 'expert', split_axis=0, concat_axis=0, tiled=True,...]
    slice x1 -> x2, local copies, waits for them, and re-layouts: 0.05 us -> 1.32 us  [the longest x1 1.27 us: per_device(): own_w[half + quarter:]]
  transfers between devices with their start and end apart: 21 -> 23, of which waited for: 12 -> 14; matrix products, arithmetic and copies ran while one was open for 3% -> 4% of each run, Pallas kernels for 12% -> 12%
where the time goes in v6:
time: 101 us; the launch traced here: 100 us
  waiting for transfers between devices  35.7 us (35%)
  starting transfers between devices  34.1 us (34%)
  Pallas kernels  25.5 us (25%)
  other arithmetic  2.78 us (3%)
  local copies, waits for them, and re-layouts  1.48 us (1%)
    ppermute x21, waiting for transfers between devices, swap(): return lax.ppermute(value, 'expert', [(j, j ^ bit) for j in range(count)])  33.8 us
    ppermute x21, starting transfers between devices, swap(): return lax.ppermute(value, 'expert', [(j, j ^ bit) for j in range(count)])  24.8 us
    pallas_call x1, Pallas kernels, middle(): pl.pallas_call(lambda *refs: middle_kernel(cap, count, *refs), in_specs=[...  10.5 us
    all_to_all x2, starting transfers between devices, exchange(): lax.all_to_all(chunks, 'expert', split_axis=0, concat_axis=0, tiled=True,...  9.23 us
    pallas_call x1, Pallas kernels, pack_hidden(): pl.pallas_call(lambda *refs: pack_kernel(cap, *refs), in_specs=[VMEM, VME...  5.34 us
    pallas_call x1, Pallas kernels, keep_partials(): pl.pallas_call(lambda *refs: keep_kernel(count, *refs), in_specs=[ANY] *...  4.51 us
    pallas_call x1, Pallas kernels, finish(): pl.pallas_call(finish_kernel, grid=(2,), in_specs=[pl.BlockSpec((tile, 1)...  2.95 us
    pallas_call x1, Pallas kernels, factors(): pl.pallas_call(lambda *refs: factors_kernel(cap, *refs), grid=(4,), in_sp...  2.13 us
  transfers between devices with their start and end apart: 23, of which 14 were waited for; matrix products, arithmetic and copies ran while one was open for 4% of the time, Pallas kernels for 12%

profile of v6, /device:TPU:0, one launch (start us, length us, event | category | flops | bytes accessed | tf_op | source)
XLA Modules:
  0.0 100.4 jit_solution(7593267734385841643)
XLA Ops:
  0.6 4.1 %collective-permute-start = (bf16[128,1024]{1,0:T(8,128)(2,1)}, bf16[128,1024]{1,0:T(8,128)(2,1)S(1)}, u32[]{:S(2)}, u32[]{:S(2)}) collective-permute-start(bf16[128,1024]{1,0:T(8,128)(2,1)} %refs_0_), channel_id=1, source_target_pairs={{0,16},{1,17},{2,18},{3,19},{4,20},{5,21},{6,22},{7,23},{8,24},{9,... | collective-permute-start | bytes 786440 | tf_op jit(solution)/shard_map/ppermute | solution.py:25
  4.7 1.6 %collective-permute-start.1 = (bf16[128,1024]{1,0:T(8,128)(2,1)}, bf16[128,1024]{1,0:T(8,128)(2,1)S(1)}, u32[]{:S(2)}, u32[]{:S(2)}) collective-permute-start(bf16[128,1024]{1,0:T(8,128)(2,1)} %refs_0_), channel_id=1, source_target_pairs={{0,8},{1,9},{2,10},{3,11},{4,12},{5,13},{6,14},{7,15},{8,0},{9,1},... | collective-permute-start | bytes 786440 | tf_op jit(solution)/shard_map/ppermute | solution.py:25
  6.3 1.3 %slice_bitcast_fusion.2 = (bf16[96,1024]{1,0:T(8,128)(2,1)S(1)}, bf16[96,1024]{1,0:T(8,128)(2,1)S(1)}, bf16[96,1024]{1,0:T(8,128)(2,1)S(1)}, bf16[96,1024]{1,0:T(8,128)(2,1)S(1)}) fusion(bf16[1,384,1024]{2,1,0:T(8,128)(2,1)} %param.9), kind=kLoop, calls=%fused_computation.11 | loop fusion | bytes 1572864 | tf_op jit(solution)/shard_map/slice | solution.py:417
  7.6 1.6 %collective-permute-start.3 = (bf16[96,1024]{1,0:T(8,128)(2,1)S(1)}, bf16[96,1024]{1,0:T(8,128)(2,1)S(1)}, u32[]{:S(2)}, u32[]{:S(2)}) collective-permute-start(bf16[96,1024]{1,0:T(8,128)(2,1)S(1)} %get-tuple-element.62), channel_id=1, source_target_pairs={{0,4},{1,5},{2,6},{3,7},{4,0},{5,1},{6,2},{7,3},{8,12},{9,13},{10,... | collective-permute-start | bytes 589832 | tf_op jit(solution)/shard_map/ppermute | solution.py:25
  9.2 1.5 %collective-permute-start.2 = (bf16[96,1024]{1,0:T(8,128)(2,1)S(1)}, bf16[96,1024]{1,0:T(8,128)(2,1)S(1)}, u32[]{:S(2)}, u32[]{:S(2)}) collective-permute-start(bf16[96,1024]{1,0:T(8,128)(2,1)S(1)} %get-tuple-element.63), channel_id=1, source_target_pairs={{0,2},{1,3},{2,0},{3,1},{4,6},{5,7},{6,4},{7,5},{8,10},{9,11},{10,... | collective-permute-start | bytes 589832 | tf_op jit(solution)/shard_map/ppermute | solution.py:25
  10.7 0.1 stack.23.refs_0_
  10.7 5.3 %pack_hidden.1 = (bf16[8,192,384]{2,1,0:T(8,128)(2,1)}, f32[16,128]{1,0:T(8,128)}) custom-call(s32[8,128]{1,0:T(8,128)} %bitcast.32, f32[8,128]{1,0:T(8,128)} %bitcast.28, bf16[1024,768]{1,0:T(8,128)(2,1)} %bitcast.26), custom_call_target="tpu_custom_call" | custom-call | flops 1207959552 | bytes 1572864 | tf_op jit(solution)/shard_map/pack_hidden/pallas_call | solution.py:127
  16.1 0.0 copy-start.10
  16.1 0.0 collective-permute-done.3.refs_14_
  16.1 0.0 collective-permute-done.2.refs_10_
  16.1 0.9 collective-permute-done.refs_2_.refs_1_
  17.0 0.2 collective-permute-done.1.refs_3_.refs_2_
  17.2 4.5 %all-to-all-start = ((bf16[8,192,384]{2,1,0:T(8,128)(2,1)}), bf16[8,192,384]{2,1,0:T(8,128)(2,1)}, u32[]{:S(2)}, u32[]{:S(2)}) async-start(bf16[8,192,384]{2,1,0:T(8,128)(2,1)} %get-tuple-element.45), calls=%async_computation | async-start | bytes 2359296 | tf_op jit(solution)/shard_map/all_to_all | solution.py:406
  21.7 1.5 %collective-permute-start.9 = (bf16[96,1024]{1,0:T(8,128)(2,1)S(1)}, bf16[96,1024]{1,0:T(8,128)(2,1)S(1)}, u32[]{:S(2)}, u32[]{:S(2)}) collective-permute-start(bf16[96,1024]{1,0:T(8,128)(2,1)S(1)} %get-tuple-element.60), channel_id=1, source_target_pairs={{0,4},{1,5},{2,6},{3,7},{4,0},{5,1},{6,2},{7,3},{8,12},{9,13},{10,... | collective-permute-start | bytes 589832 | tf_op jit(solution)/shard_map/ppermute | solution.py:25
  23.2 1.5 %collective-permute-start.7 = (bf16[96,1024]{1,0:T(8,128)(2,1)S(1)}, bf16[96,1024]{1,0:T(8,128)(2,1)S(1)}, u32[]{:S(2)}, u32[]{:S(2)}) collective-permute-start(bf16[96,1024]{1,0:T(8,128)(2,1)S(1)} %get-tuple-element.61), channel_id=1, source_target_pairs={{0,2},{1,3},{2,0},{3,1},{4,6},{5,7},{6,4},{7,5},{8,10},{9,11},{10,... | collective-permute-start | bytes 589832 | tf_op jit(solution)/shard_map/ppermute | solution.py:25
  24.7 0.1 slice_bitcast_fusion
  24.8 0.6 collective-permute-start.6
  25.3 0.5 collective-permute-start.5
  25.9 3.5 %collective-permute-done.9.refs_15_ = bf16[96,1024]{1,0:T(8,128)(2,1)S(1)} collective-permute-done((bf16[96,1024]{1,0:T(8,128)(2,1)S(1)}, bf16[96,1024]{1,0:T(8,128)(2,1)S(1)}, u32[]{:S(2)}, u32[]{:S(2)}) %collective-permute-start.9) | collective-permute-done | bytes 196640 | tf_op jit(solution)/shard_map/ppermute | solution.py:25
  29.4 1.6 %collective-permute-start.10 = (bf16[192,1024]{1,0:T(8,128)(2,1)S(1)}, bf16[192,1024]{1,0:T(8,128)(2,1)S(1)}, u32[]{:S(2)}, u32[]{:S(2)}) collective-permute-start(bf16[192,1024]{1,0:T(8,128)(2,1)S(1)} %pad_maximum_fusion.1), channel_id=1, source_target_pairs={{0,2},{1,3},{2,0},{3,1},{4,6},{5,7},{6,4},{7,5},{8,10},{9,11},{10,... | collective-permute-start | bytes 1179656 | tf_op jit(solution)/shard_map/ppermute | solution.py:25
  31.0 0.0 collective-permute-done.7.refs_11_
  31.0 1.6 %collective-permute-start.8 = (bf16[192,1024]{1,0:T(8,128)(2,1)S(1)}, bf16[192,1024]{1,0:T(8,128)(2,1)S(1)}, u32[]{:S(2)}, u32[]{:S(2)}) collective-permute-start(bf16[192,1024]{1,0:T(8,128)(2,1)S(1)} %pad_maximum_fusion), channel_id=1, source_target_pairs={{0,4},{1,5},{2,6},{3,7},{4,0},{5,1},{6,2},{7,3},{8,12},{9,13},{10,... | collective-permute-start | bytes 1179656 | tf_op jit(solution)/shard_map/ppermute | solution.py:25
  32.6 2.1 %collective-permute-start.4 = (bf16[128,1024]{1,0:T(8,128)(2,1)S(1)}, bf16[128,1024]{1,0:T(8,128)(2,1)S(1)}, u32[]{:S(2)}, u32[]{:S(2)}) collective-permute-start(bf16[128,1024]{1,0:T(8,128)(2,1)S(1)} %collective-permute-done.refs_2_.refs_1_), channel_id=1, source_target_pairs={{0,8},{1,9},{2,10},{3,11},{4,12},{5,13},{6,14},{7,15},{8,0},{9,1},... | collective-permute-start | bytes 786440 | tf_op jit(solution)/shard_map/ppermute | solution.py:25
  34.7 3.1 %collective-permute-done.6.refs_13_ = bf16[192,1024]{1,0:T(8,128)(2,1)S(1)} collective-permute-done((bf16[192,1024]{1,0:T(8,128)(2,1)S(1)}, bf16[192,1024]{1,0:T(8,128)(2,1)S(1)}, u32[]{:S(2)}, u32[]{:S(2)}) %collective-permute-start.6) | collective-permute-done | bytes 393248 | tf_op jit(solution)/shard_map/ppermute | solution.py:25
  37.8 0.0 collective-permute-start.12
  37.8 1.6 %collective-permute-done.5.refs_12_ = bf16[192,1024]{1,0:T(8,128)(2,1)S(1)} collective-permute-done((bf16[192,1024]{1,0:T(8,128)(2,1)S(1)}, bf16[192,1024]{1,0:T(8,128)(2,1)S(1)}, u32[]{:S(2)}, u32[]{:S(2)}) %collective-permute-start.5) | collective-permute-done | bytes 393248 | tf_op jit(solution)/shard_map/ppermute | solution.py:25
  39.4 0.0 collective-permute-start.11
  39.4 8.0 %collective-permute-done.4.refs_4_.refs_3_ = bf16[128,1024]{1,0:T(8,128)(2,1)S(1)} collective-permute-done((bf16[128,1024]{1,0:T(8,128)(2,1)S(1)}, bf16[128,1024]{1,0:T(8,128)(2,1)S(1)}, u32[]{:S(2)}, u32[]{:S(2)}) %collective-permute-start.4) | collective-permute-done | bytes 262176 | tf_op jit(solution)/shard_map/ppermute | solution.py:25
  47.4 0.0 collective-permute-start.13
  47.4 0.0 collective-permute-done.10.refs_17_
  47.4 0.0 collective-permute-done.8.refs_16_
  47.4 0.6 collective-permute-start.14
  48.0 0.0 collective-permute-done.11.refs_5_.refs_4_
  48.0 0.9 collective-permute-done.13.refs_7_.refs_6_
  48.9 0.0 collective-permute-done.12.refs_6_.refs_5_
  49.0 0.3 collective-permute-done.14.refs_8_.refs_7_
  49.3 1.9 %all-to-all-done.refs_18_ = bf16[8,192,384]{2,1,0:T(8,128)(2,1)} async-done(((bf16[8,192,384]{2,1,0:T(8,128)(2,1)}), bf16[8,192,384]{2,1,0:T(8,128)(2,1)}, u32[]{:S(2)}, u32[]{:S(2)}) %all-to-all-start) | async-done | bytes 1179680 | tf_op jit(solution)/shard_map/all_to_all | solution.py:406
  51.2 0.0 copy-done.4
  51.2 0.0 copy-done.17
  51.2 10.5 %middle.1 = (bf16[8,192,384]{2,1,0:T(8,128)(2,1)}, bf16[192,1024]{1,0:T(8,128)(2,1)}, bf16[192,1024]{1,0:T(8,128)(2,1)}, bf16[192,1024]{1,0:T(8,128)(2,1)}, bf16...) custom-call(s32[5]{0:T(128)S(1)} %stack.23.refs_0_, bf16[128,1024]{1,0:T(8,128)(2,1)S(1)} %copy-done.3, ...), custom_call_target="tpu_custom_call" | custom-call | flops 4831838208 | bytes 4194304 | tf_op jit(solution)/shard_map/middle/pallas_call | solution.py:288
  61.8 4.7 %all-to-all-start.1 = ((bf16[8,192,384]{2,1,0:T(8,128)(2,1)}), bf16[8,192,384]{2,1,0:T(8,128)(2,1)S(1)}, u32[]{:S(2)}, u32[]{:S(2)}) async-start(bf16[8,192,384]{2,1,0:T(8,128)(2,1)} %get-tuple-element.46), calls=%async_computation.1 | async-start | bytes 2359296 | tf_op jit(solution)/shard_map/all_to_all | solution.py:406
  66.5 1.5 %collective-permute-start.17 = (bf16[192,1024]{1,0:T(8,128)(2,1)}, bf16[192,1024]{1,0:T(8,128)(2,1)S(1)}, u32[]{:S(2)}, u32[]{:S(2)}) collective-permute-start(bf16[192,1024]{1,0:T(8,128)(2,1)} %get-tuple-element.53), channel_id=1, source_target_pairs={{0,2},{1,3},{2,0},{3,1},{4,6},{5,7},{6,4},{7,5},{8,10},{9,11},{10,... | collective-permute-start | bytes 1179656 | tf_op jit(solution)/shard_map/ppermute | solution.py:25
  68.0 1.5 %collective-permute-start.18 = (bf16[192,1024]{1,0:T(8,128)(2,1)S(1)}, bf16[192,1024]{1,0:T(8,128)(2,1)S(1)}, u32[]{:S(2)}, u32[]{:S(2)}) collective-permute-start(bf16[192,1024]{1,0:T(8,128)(2,1)S(1)} %copy-done.16), channel_id=1, source_target_pairs={{0,4},{1,5},{2,6},{3,7},{4,0},{5,1},{6,2},{7,3},{8,12},{9,13},{10,... | collective-permute-start | bytes 1179656 | tf_op jit(solution)/shard_map/ppermute | solution.py:25
  69.5 0.5 collective-permute-start.15
  70.1 0.5 collective-permute-start.16
  70.6 0.0 copy-done.5
  70.6 4.5 %keep_partials.1 = (f32[384,1024]{1,0:T(8,128)}, bf16[384,1024]{1,0:T(8,128)(2,1)}) custom-call(bf16[128,1024]{1,0:T(8,128)(2,1)S(1)} %copy-done.3, bf16[128,1024]{1,0:T(8,128)(2,1)S(1)} %collective-permute-done.refs_2_.refs_1_, bf16[128,1024]{1,0:T(8,128)(2,1)S(1)} %collective-permute-done.1.refs_3_.refs_2_, ...), custom_call_target="tpu_custom_call" | custom-call | flops 1610612736 | bytes 4194304 | tf_op jit(solution)/shard_map/keep_partials/pallas_call | solution.py:340
  75.1 0.0 copy-start
  75.1 0.0 copy-start.2
  75.1 3.5 %collective-permute-done.17 = bf16[192,1024]{1,0:T(8,128)(2,1)S(1)} collective-permute-done((bf16[192,1024]{1,0:T(8,128)(2,1)}, bf16[192,1024]{1,0:T(8,128)(2,1)S(1)}, u32[]{:S(2)}, u32[]{:S(2)}) %collective-permute-start.17) | collective-permute-done | bytes 393248 | tf_op jit(solution)/shard_map/ppermute | solution.py:25
  78.6 1.3 %collective-permute-done.18 = bf16[192,1024]{1,0:T(8,128)(2,1)S(1)} collective-permute-done((bf16[192,1024]{1,0:T(8,128)(2,1)S(1)}, bf16[192,1024]{1,0:T(8,128)(2,1)S(1)}, u32[]{:S(2)}, u32[]{:S(2)}) %collective-permute-start.18) | collective-permute-done | bytes 393248 | tf_op jit(solution)/shard_map/ppermute | solution.py:25
  79.9 1.4 %add_convert_fusion.1 = (bf16[192,1024]{1,0:T(8,128)(2,1)S(1)}, bf16[192,1024]{1,0:T(8,128)(2,1)S(1)}) fusion(bf16[192,1024]{1,0:T(8,128)(2,1)S(1)} %collective-permute-done.17, bf16[384,1024]{1,0:T(8,128)(2,1)} %get-tuple-element.52, bf16[192,1024]{1,0:T(8,128)(2,1)S(1)} %collective-permute-done.18), kind=kLoop, calls=%fused_computation.6 | loop fusion | flops 1572864 | bytes 2359296 | tf_op jit(solution)/shard_map/convert_element_type | solution.py:451
  81.4 1.6 %collective-permute-start.19 = (bf16[192,1024]{1,0:T(8,128)(2,1)S(1)}, bf16[192,1024]{1,0:T(8,128)(2,1)S(1)}, u32[]{:S(2)}, u32[]{:S(2)}) collective-permute-start(bf16[192,1024]{1,0:T(8,128)(2,1)S(1)} %get-tuple-element.58), channel_id=1, source_target_pairs={{0,4},{1,5},{2,6},{3,7},{4,0},{5,1},{6,2},{7,3},{8,12},{9,13},{10,... | collective-permute-start | bytes 1179656 | tf_op jit(solution)/shard_map/ppermute | solution.py:25
  83.0 0.5 collective-permute-start.20
  83.5 2.1 %factors.1 = (bf16[1024,768]{1,0:T(8,128)(2,1)S(1)}, s32[1024,1]{1,0:T(8,128)S(1)}) custom-call(f32[16,128]{1,0:T(8,128)S(1)} %copy-done.1, f32[8,128]{1,0:T(8,128)S(1)} %bitcast.29, bf16[1024,768]{1,0:T(8,128)(2,1)S(1)} %bitcast.27), custom_call_target="tpu_custom_call" | custom-call | tf_op jit(solution)/shard_map/factors/pallas_call | solution.py:170
  85.6 1.4 %collective-permute-done.15 = bf16[192,1024]{1,0:T(8,128)(2,1)S(1)} collective-permute-done((bf16[192,1024]{1,0:T(8,128)(2,1)}, bf16[192,1024]{1,0:T(8,128)(2,1)S(1)}, u32[]{:S(2)}, u32[]{:S(2)}) %collective-permute-start.15) | collective-permute-done | bytes 393248 | tf_op jit(solution)/shard_map/ppermute | solution.py:25
  87.1 1.3 %collective-permute-done.16 = bf16[192,1024]{1,0:T(8,128)(2,1)S(1)} collective-permute-done((bf16[192,1024]{1,0:T(8,128)(2,1)}, bf16[192,1024]{1,0:T(8,128)(2,1)S(1)}, u32[]{:S(2)}, u32[]{:S(2)}) %collective-permute-start.16) | collective-permute-done | bytes 393248 | tf_op jit(solution)/shard_map/ppermute | solution.py:25
  88.4 7.7 %collective-permute-done.19 = bf16[192,1024]{1,0:T(8,128)(2,1)S(1)} collective-permute-done((bf16[192,1024]{1,0:T(8,128)(2,1)S(1)}, bf16[192,1024]{1,0:T(8,128)(2,1)S(1)}, u32[]{:S(2)}, u32[]{:S(2)}) %collective-permute-start.19) | collective-permute-done | bytes 393248 | tf_op jit(solution)/shard_map/ppermute | solution.py:25
  96.1 0.1 convert_add_fusion.1
  96.2 0.0 collective-permute-done.20
  96.2 0.1 convert_add_fusion
  96.3 1.1 %fusion.1 = bf16[1,384,1024]{2,1,0:T(8,128)(2,1)} fusion(f32[384,1024]{1,0:T(8,128)S(1)} %copy-done.11, f32[192,1024]{1,0:T(8,128)S(1)} %convert_add_fusion, f32[192,1024]{1,0:T(8,128)S(1)} %convert_add_fusion.1), kind=kLoop, calls=%fused_computation.2 | loop fusion | flops 1179648 | bytes 3932160 | tf_op jit(solution)/shard_map/convert_element_type | solution.py:465
  97.4 0.0 all-to-all-done.1
  97.5 2.9 %finish.1 = bf16[1024,768]{1,0:T(8,128)(2,1)} custom-call(s32[1024,1]{1,0:T(8,128)S(1)} %get-tuple-element.31.column_ref, bf16[1024,768]{1,0:T(8,128)(2,1)S(1)} %get-tuple-element.32.factors_ref, bf16[1536,384]{1,0:T(8,128)(2,1)S(1)} %bitcast.25), custom_call_target="tpu_custom_call" | custom-call | flops 786432 | bytes 3145728 | tf_op jit(solution)/shard_map/finish/pallas_call | solution.py:376
  (32 shorter events, 0.1 us)
Async XLA Ops:
  0.6 16.3 %collective-permute-start = (bf16[128,1024]{1,0:T(8,128)(2,1)}, bf16[128,1024]{1,0:T(8,128)(2,1)S(1)}, u32[]{:S(2)}, u32[]{:S(2)}) collective-permute-start(bf16[128,1024]{1,0:T(8,128)(2,1)} %refs_0_), channel_id=1, source_target_pairs={{0,16},{1,17},{2,18},{3,19},{4,20},{5,21},{6,22},{7,23},{8,24},{9,... | collective-permute-start | bytes 786440 | tf_op jit(solution)/shard_map/ppermute | solution.py:25
  4.7 12.4 %collective-permute-start.1 = (bf16[128,1024]{1,0:T(8,128)(2,1)}, bf16[128,1024]{1,0:T(8,128)(2,1)S(1)}, u32[]{:S(2)}, u32[]{:S(2)}) collective-permute-start(bf16[128,1024]{1,0:T(8,128)(2,1)} %refs_0_), channel_id=1, source_target_pairs={{0,8},{1,9},{2,10},{3,11},{4,12},{5,13},{6,14},{7,15},{8,0},{9,1},... | collective-permute-start | bytes 786440 | tf_op jit(solution)/shard_map/ppermute | solution.py:25
  7.6 8.5 %collective-permute-start.3 = (bf16[96,1024]{1,0:T(8,128)(2,1)S(1)}, bf16[96,1024]{1,0:T(8,128)(2,1)S(1)}, u32[]{:S(2)}, u32[]{:S(2)}) collective-permute-start(bf16[96,1024]{1,0:T(8,128)(2,1)S(1)} %get-tuple-element.62), channel_id=1, source_target_pairs={{0,4},{1,5},{2,6},{3,7},{4,0},{5,1},{6,2},{7,3},{8,12},{9,13},{10,... | collective-permute-start | bytes 589832 | tf_op jit(solution)/shard_map/ppermute | solution.py:25
  9.2 7.0 %collective-permute-start.2 = (bf16[96,1024]{1,0:T(8,128)(2,1)S(1)}, bf16[96,1024]{1,0:T(8,128)(2,1)S(1)}, u32[]{:S(2)}, u32[]{:S(2)}) collective-permute-start(bf16[96,1024]{1,0:T(8,128)(2,1)S(1)} %get-tuple-element.63), channel_id=1, source_target_pairs={{0,2},{1,3},{2,0},{3,1},{4,6},{5,7},{6,4},{7,5},{8,10},{9,11},{10,... | collective-permute-start | bytes 589832 | tf_op jit(solution)/shard_map/ppermute | solution.py:25
  16.1 8.6 %copy-start.10 = (bf16[1,384,1024]{2,1,0:T(8,128)(2,1)S(1)}, bf16[1,384,1024]{2,1,0:T(8,128)(2,1)}, u32[]{:S(2)}) copy-start(bf16[1,384,1024]{2,1,0:T(8,128)(2,1)} %param.9) | copy-start | bytes 2359300
  17.2 34.0 %all-to-all-start = ((bf16[8,192,384]{2,1,0:T(8,128)(2,1)}), bf16[8,192,384]{2,1,0:T(8,128)(2,1)}, u32[]{:S(2)}, u32[]{:S(2)}) async-start(bf16[8,192,384]{2,1,0:T(8,128)(2,1)} %get-tuple-element.45), calls=%async_computation | async-start | bytes 2359296 | tf_op jit(solution)/shard_map/all_to_all | solution.py:406
  21.7 7.7 %collective-permute-start.9 = (bf16[96,1024]{1,0:T(8,128)(2,1)S(1)}, bf16[96,1024]{1,0:T(8,128)(2,1)S(1)}, u32[]{:S(2)}, u32[]{:S(2)}) collective-permute-start(bf16[96,1024]{1,0:T(8,128)(2,1)S(1)} %get-tuple-element.60), channel_id=1, source_target_pairs={{0,4},{1,5},{2,6},{3,7},{4,0},{5,1},{6,2},{7,3},{8,12},{9,13},{10,... | collective-permute-start | bytes 589832 | tf_op jit(solution)/shard_map/ppermute | solution.py:25
  23.2 16.2 %copy-start.3 = (bf16[128,1024]{1,0:T(8,128)(2,1)S(1)}, bf16[128,1024]{1,0:T(8,128)(2,1)}, u32[]{:S(2)}) copy-start(bf16[128,1024]{1,0:T(8,128)(2,1)} %refs_0_) | copy-start | bytes 786436
  23.2 7.8 %collective-permute-start.7 = (bf16[96,1024]{1,0:T(8,128)(2,1)S(1)}, bf16[96,1024]{1,0:T(8,128)(2,1)S(1)}, u32[]{:S(2)}, u32[]{:S(2)}) collective-permute-start(bf16[96,1024]{1,0:T(8,128)(2,1)S(1)} %get-tuple-element.61), channel_id=1, source_target_pairs={{0,2},{1,3},{2,0},{3,1},{4,6},{5,7},{6,4},{7,5},{8,10},{9,11},{10,... | collective-permute-start | bytes 589832 | tf_op jit(solution)/shard_map/ppermute | solution.py:25
  24.8 13.1 %collective-permute-start.6 = (bf16[192,1024]{1,0:T(8,128)(2,1)S(1)}, bf16[192,1024]{1,0:T(8,128)(2,1)S(1)}, u32[]{:S(2)}, u32[]{:S(2)}) collective-permute-start(bf16[192,1024]{1,0:T(8,128)(2,1)S(1)} %get-tuple-element.64), channel_id=1, source_target_pairs={{0,4},{1,5},{2,6},{3,7},{4,0},{5,1},{6,2},{7,3},{8,12},{9,13},{10,... | collective-permute-start | bytes 1179656 | tf_op jit(solution)/shard_map/ppermute | solution.py:25
  25.3 14.0 %collective-permute-start.5 = (bf16[192,1024]{1,0:T(8,128)(2,1)S(1)}, bf16[192,1024]{1,0:T(8,128)(2,1)S(1)}, u32[]{:S(2)}, u32[]{:S(2)}) collective-permute-start(bf16[192,1024]{1,0:T(8,128)(2,1)S(1)} %get-tuple-element.65), channel_id=1, source_target_pairs={{0,2},{1,3},{2,0},{3,1},{4,6},{5,7},{6,4},{7,5},{8,10},{9,11},{10,... | collective-permute-start | bytes 1179656 | tf_op jit(solution)/shard_map/ppermute | solution.py:25
  29.4 18.0 %collective-permute-start.10 = (bf16[192,1024]{1,0:T(8,128)(2,1)S(1)}, bf16[192,1024]{1,0:T(8,128)(2,1)S(1)}, u32[]{:S(2)}, u32[]{:S(2)}) collective-permute-start(bf16[192,1024]{1,0:T(8,128)(2,1)S(1)} %pad_maximum_fusion.1), channel_id=1, source_target_pairs={{0,2},{1,3},{2,0},{3,1},{4,6},{5,7},{6,4},{7,5},{8,10},{9,11},{10,... | collective-permute-start | bytes 1179656 | tf_op jit(solution)/shard_map/ppermute | solution.py:25
  31.0 16.4 %collective-permute-start.8 = (bf16[192,1024]{1,0:T(8,128)(2,1)S(1)}, bf16[192,1024]{1,0:T(8,128)(2,1)S(1)}, u32[]{:S(2)}, u32[]{:S(2)}) collective-permute-start(bf16[192,1024]{1,0:T(8,128)(2,1)S(1)} %pad_maximum_fusion), channel_id=1, source_target_pairs={{0,4},{1,5},{2,6},{3,7},{4,0},{5,1},{6,2},{7,3},{8,12},{9,13},{10,... | collective-permute-start | bytes 1179656 | tf_op jit(solution)/shard_map/ppermute | solution.py:25
  32.6 14.8 %collective-permute-start.4 = (bf16[128,1024]{1,0:T(8,128)(2,1)S(1)}, bf16[128,1024]{1,0:T(8,128)(2,1)S(1)}, u32[]{:S(2)}, u32[]{:S(2)}) collective-permute-start(bf16[128,1024]{1,0:T(8,128)(2,1)S(1)} %collective-permute-done.refs_2_.refs_1_), channel_id=1, source_target_pairs={{0,8},{1,9},{2,10},{3,11},{4,12},{5,13},{6,14},{7,15},{8,0},{9,1},... | collective-permute-start | bytes 786440 | tf_op jit(solution)/shard_map/ppermute | solution.py:25
  37.8 13.4 %copy-start.12 = (bf16[192,1024]{1,0:T(8,128)(2,1)}, bf16[192,1024]{1,0:T(8,128)(2,1)S(1)}, u32[]{:S(2)}) copy-start(bf16[192,1024]{1,0:T(8,128)(2,1)S(1)} %collective-permute-done.6.refs_13_) | copy-start | bytes 1179652
  37.8 11.1 %collective-permute-start.12 = (bf16[128,1024]{1,0:T(8,128)(2,1)S(1)}, bf16[128,1024]{1,0:T(8,128)(2,1)S(1)}, u32[]{:S(2)}, u32[]{:S(2)}) collective-permute-start(bf16[128,1024]{1,0:T(8,128)(2,1)S(1)} %collective-permute-done.refs_2_.refs_1_), channel_id=1, source_target_pairs={{0,1},{1,0},{2,3},{3,2},{4,5},{5,4},{6,7},{7,6},{8,9},{9,8},{10,11... | collective-permute-start | bytes 786440 | tf_op jit(solution)/shard_map/ppermute | solution.py:25
  39.4 9.6 %copy-start.13 = (bf16[192,1024]{1,0:T(8,128)(2,1)}, bf16[192,1024]{1,0:T(8,128)(2,1)S(1)}, u32[]{:S(2)}) copy-start(bf16[192,1024]{1,0:T(8,128)(2,1)S(1)} %collective-permute-done.5.refs_12_) | copy-start | bytes 1179652
  39.4 8.6 %collective-permute-start.11 = (bf16[128,1024]{1,0:T(8,128)(2,1)S(1)}, bf16[128,1024]{1,0:T(8,128)(2,1)S(1)}, u32[]{:S(2)}, u32[]{:S(2)}) collective-permute-start(bf16[128,1024]{1,0:T(8,128)(2,1)S(1)} %copy-done.3), channel_id=1, source_target_pairs={{0,1},{1,0},{2,3},{3,2},{4,5},{5,4},{6,7},{7,6},{8,9},{9,8},{10,11... | collective-permute-start | bytes 786440 | tf_op jit(solution)/shard_map/ppermute | solution.py:25
  47.4 1.5 %collective-permute-start.13 = (bf16[128,1024]{1,0:T(8,128)(2,1)S(1)}, bf16[128,1024]{1,0:T(8,128)(2,1)S(1)}, u32[]{:S(2)}, u32[]{:S(2)}) collective-permute-start(bf16[128,1024]{1,0:T(8,128)(2,1)S(1)} %collective-permute-done.1.refs_3_.refs_2_), channel_id=1, source_target_pairs={{0,1},{1,0},{2,3},{3,2},{4,5},{5,4},{6,7},{7,6},{8,9},{9,8},{10,11... | collective-permute-start | bytes 786440 | tf_op jit(solution)/shard_map/ppermute | solution.py:25
  47.4 1.5 %copy-start.14 = (bf16[192,1024]{1,0:T(8,128)(2,1)}, bf16[192,1024]{1,0:T(8,128)(2,1)S(1)}, u32[]{:S(2)}) copy-start(bf16[192,1024]{1,0:T(8,128)(2,1)S(1)} %collective-permute-done.10.refs_17_) | copy-start | bytes 1179652
  47.4 1.5 %copy-start.15 = (bf16[192,1024]{1,0:T(8,128)(2,1)}, bf16[192,1024]{1,0:T(8,128)(2,1)S(1)}, u32[]{:S(2)}) copy-start(bf16[192,1024]{1,0:T(8,128)(2,1)S(1)} %collective-permute-done.8.refs_16_) | copy-start | bytes 1179652
  47.4 1.9 %collective-permute-start.14 = (bf16[128,1024]{1,0:T(8,128)(2,1)S(1)}, bf16[128,1024]{1,0:T(8,128)(2,1)S(1)}, u32[]{:S(2)}, u32[]{:S(2)}) collective-permute-start(bf16[128,1024]{1,0:T(8,128)(2,1)S(1)} %collective-permute-done.4.refs_4_.refs_3_), channel_id=1, source_target_pairs={{0,1},{1,0},{2,3},{3,2},{4,5},{5,4},{6,7},{7,6},{8,9},{9,8},{10,11... | collective-permute-start | bytes 786440 | tf_op jit(solution)/shard_map/ppermute | solution.py:25
  48.0 3.2 %copy-start.6 = (bf16[128,1024]{1,0:T(8,128)(2,1)}, bf16[128,1024]{1,0:T(8,128)(2,1)S(1)}, u32[]{:S(2)}) copy-start(bf16[128,1024]{1,0:T(8,128)(2,1)S(1)} %collective-permute-done.11.refs_5_.refs_4_) | copy-start | bytes 786436
  48.9 2.3 %copy-start.8 = (bf16[128,1024]{1,0:T(8,128)(2,1)}, bf16[128,1024]{1,0:T(8,128)(2,1)S(1)}, u32[]{:S(2)}) copy-start(bf16[128,1024]{1,0:T(8,128)(2,1)S(1)} %collective-permute-done.13.refs_7_.refs_6_) | copy-start | bytes 786436
  49.0 2.2 %copy-start.4 = (bf16[128,1024]{1,0:T(8,128)(2,1)}, bf16[128,1024]{1,0:T(8,128)(2,1)S(1)}, u32[]{:S(2)}) copy-start(bf16[128,1024]{1,0:T(8,128)(2,1)S(1)} %collective-permute-done.12.refs_6_.refs_5_) | copy-start | bytes 786436
  49.3 1.9 %copy-start.17 = (bf16[128,1024]{1,0:T(8,128)(2,1)}, bf16[128,1024]{1,0:T(8,128)(2,1)S(1)}, u32[]{:S(2)}) copy-start(bf16[128,1024]{1,0:T(8,128)(2,1)S(1)} %collective-permute-done.14.refs_8_.refs_7_) | copy-start | bytes 786436
  61.8 6.2 %copy-start.16 = (bf16[192,1024]{1,0:T(8,128)(2,1)S(1)}, bf16[192,1024]{1,0:T(8,128)(2,1)}, u32[]{:S(2)}) copy-start(bf16[192,1024]{1,0:T(8,128)(2,1)} %get-tuple-element.54) | copy-start | bytes 1179652
  61.8 8.8 %copy-start.5 = (bf16[128,1024]{1,0:T(8,128)(2,1)S(1)}, bf16[128,1024]{1,0:T(8,128)(2,1)}, u32[]{:S(2)}) copy-start(bf16[128,1024]{1,0:T(8,128)(2,1)} %copy-done.4) | copy-start | bytes 786436
  61.8 8.8 %copy-start.7 = (bf16[128,1024]{1,0:T(8,128)(2,1)S(1)}, bf16[128,1024]{1,0:T(8,128)(2,1)}, u32[]{:S(2)}) copy-start(bf16[128,1024]{1,0:T(8,128)(2,1)} %copy-done.6) | copy-start | bytes 786436
  61.8 8.8 %copy-start.9 = (bf16[128,1024]{1,0:T(8,128)(2,1)S(1)}, bf16[128,1024]{1,0:T(8,128)(2,1)}, u32[]{:S(2)}) copy-start(bf16[128,1024]{1,0:T(8,128)(2,1)} %copy-done.8) | copy-start | bytes 786436
  61.8 35.6 %all-to-all-start.1 = ((bf16[8,192,384]{2,1,0:T(8,128)(2,1)}), bf16[8,192,384]{2,1,0:T(8,128)(2,1)S(1)}, u32[]{:S(2)}, u32[]{:S(2)}) async-start(bf16[8,192,384]{2,1,0:T(8,128)(2,1)} %get-tuple-element.46), calls=%async_computation.1 | async-start | bytes 2359296 | tf_op jit(solution)/shard_map/all_to_all | solution.py:406
  66.5 12.1 %collective-permute-start.17 = (bf16[192,1024]{1,0:T(8,128)(2,1)}, bf16[192,1024]{1,0:T(8,128)(2,1)S(1)}, u32[]{:S(2)}, u32[]{:S(2)}) collective-permute-start(bf16[192,1024]{1,0:T(8,128)(2,1)} %get-tuple-element.53), channel_id=1, source_target_pairs={{0,2},{1,3},{2,0},{3,1},{4,6},{5,7},{6,4},{7,5},{8,10},{9,11},{10,... | collective-permute-start | bytes 1179656 | tf_op jit(solution)/shard_map/ppermute | solution.py:25
  68.0 11.9 %collective-permute-start.18 = (bf16[192,1024]{1,0:T(8,128)(2,1)S(1)}, bf16[192,1024]{1,0:T(8,128)(2,1)S(1)}, u32[]{:S(2)}, u32[]{:S(2)}) collective-permute-start(bf16[192,1024]{1,0:T(8,128)(2,1)S(1)} %copy-done.16), channel_id=1, source_target_pairs={{0,4},{1,5},{2,6},{3,7},{4,0},{5,1},{6,2},{7,3},{8,12},{9,13},{10,... | collective-permute-start | bytes 1179656 | tf_op jit(solution)/shard_map/ppermute | solution.py:25
  69.5 17.5 %collective-permute-start.15 = (bf16[192,1024]{1,0:T(8,128)(2,1)}, bf16[192,1024]{1,0:T(8,128)(2,1)S(1)}, u32[]{:S(2)}, u32[]{:S(2)}) collective-permute-start(bf16[192,1024]{1,0:T(8,128)(2,1)} %get-tuple-element.49), channel_id=1, source_target_pairs={{0,2},{1,3},{2,0},{3,1},{4,6},{5,7},{6,4},{7,5},{8,10},{9,11},{10,... | collective-permute-start | bytes 1179656 | tf_op jit(solution)/shard_map/ppermute | solution.py:25
  70.1 18.3 %collective-permute-start.16 = (bf16[192,1024]{1,0:T(8,128)(2,1)}, bf16[192,1024]{1,0:T(8,128)(2,1)S(1)}, u32[]{:S(2)}, u32[]{:S(2)}) collective-permute-start(bf16[192,1024]{1,0:T(8,128)(2,1)} %get-tuple-element.50), channel_id=1, source_target_pairs={{0,4},{1,5},{2,6},{3,7},{4,0},{5,1},{6,2},{7,3},{8,12},{9,13},{10,... | collective-permute-start | bytes 1179656 | tf_op jit(solution)/shard_map/ppermute | solution.py:25
  75.1 8.4 %copy-start = (bf16[128,8,768]{2,1,0:T(8,128)(2,1)S(1)}, bf16[128,8,768]{2,1,0:T(8,128)(2,1)}, u32[]{:S(2)}) copy-start(bf16[128,8,768]{2,1,0:T(8,128)(2,1)} %param.8) | copy-start | bytes 4718596
  75.1 8.4 %copy-start.1 = (f32[16,128]{1,0:T(8,128)S(1)}, f32[16,128]{1,0:T(8,128)}, u32[]{:S(2)}) copy-start(f32[16,128]{1,0:T(8,128)} %get-tuple-element.30.refs_0_) | copy-start | bytes 24580
  75.1 8.4 %copy-start.2 = (f32[128,8]{0,1:T(8,128)S(1)}, f32[128,8]{0,1:T(8,128)}, u32[]{:S(2)}) copy-start(f32[128,8]{0,1:T(8,128)} %param.6) | copy-start | bytes 12292
  81.4 14.7 %collective-permute-start.19 = (bf16[192,1024]{1,0:T(8,128)(2,1)S(1)}, bf16[192,1024]{1,0:T(8,128)(2,1)S(1)}, u32[]{:S(2)}, u32[]{:S(2)}) collective-permute-start(bf16[192,1024]{1,0:T(8,128)(2,1)S(1)} %get-tuple-element.58), channel_id=1, source_target_pairs={{0,4},{1,5},{2,6},{3,7},{4,0},{5,1},{6,2},{7,3},{8,12},{9,13},{10,... | collective-permute-start | bytes 1179656 | tf_op jit(solution)/shard_map/ppermute | solution.py:25
  83.0 13.3 %collective-permute-start.20 = (bf16[192,1024]{1,0:T(8,128)(2,1)S(1)}, bf16[192,1024]{1,0:T(8,128)(2,1)S(1)}, u32[]{:S(2)}, u32[]{:S(2)}) collective-permute-start(bf16[192,1024]{1,0:T(8,128)(2,1)S(1)} %get-tuple-element.59), channel_id=1, source_target_pairs={{0,2},{1,3},{2,0},{3,1},{4,6},{5,7},{6,4},{7,5},{8,10},{9,11},{10,... | collective-permute-start | bytes 1179656 | tf_op jit(solution)/shard_map/ppermute | solution.py:25
  85.6 10.7 %copy-start.11 = (f32[384,1024]{1,0:T(8,128)S(1)}, f32[384,1024]{1,0:T(8,128)}, u32[]{:S(2)}) copy-start(f32[384,1024]{1,0:T(8,128)} %get-tuple-element.48) | copy-start | bytes 4718596

commit v7 on v6

--- a/solution.py
+++ b/solution.py
@@ -264,15 +264,16 @@
         copies.append(copy)
     for copy in weight_copies:
         copy.wait()
-    for first in range(0, count, 2):
-        both = transposed_dot(
-            grads[first * tokens : (first + 2) * tokens], weights[...]
+    for first in range(0, count, 4):
+        four = transposed_dot(
+            grads[first * tokens : (first + 4) * tokens], weights[...]
         ).astype(BF16)
-        for at in (first, first + 1):
-            side = both[(at - first) * tokens : (at - first + 1) * tokens]
+        for at in range(first, first + 4):
+            side = four[(at - first) * tokens : (at - first + 1) * tokens]
             for e in range(4):
                 slopes[at, e * tokens : (e + 1) * tokens] = side[:, e * width : (e + 1) * width]
             packed[at] = dot(pick[at], slopes[at]).astype(BF16)
+        for at in range(first, first + 4):
             copy = pltpu.make_async_copy(packed.at[at], out_ref.at[places[at]], psem.at[at])
             copy.start()
             copies.append(copy)
@@ -451,13 +452,9 @@
     to_y = (keep[half:].astype(F32) + from_x.astype(F32)).astype(BF16)
     to_x = (keep[:half].astype(F32) + from_y.astype(F32)).astype(BF16)
     last_y, last_x = swap(to_y, Y_BIT), swap(to_x, X_BIT)
-    total = own + jnp.concatenate(
-        [
-            mine_x.astype(F32) + last_y.astype(F32),
-            mine_y.astype(F32) + last_x.astype(F32),
-        ],
-        0,
-    )
+    part = own + jnp.concatenate([mine_x, mine_y], 0).astype(F32)
+    part, last_y, last_x = lax.optimization_barrier((part, last_y, last_x))
+    total = part + jnp.concatenate([last_y, last_x], 0).astype(F32)
     total = lax.psum_scatter(total, "dp", scatter_dimension=1, tiled=True)
 
     scale, column = factors(place, gates, flat_pre, cap)

time: 101 us -> 100 us (0.990)
  transfers between devices with their start and end apart: 23 -> 23, of which waited for: 14 -> 15; matrix products, arithmetic and copies ran while one was open for 4% -> 4% of each run, Pallas kernels for 12% -> 12%
where the time goes in v7:
time: 100 us
  waiting for transfers between devices  35.3 us (35%)
  starting transfers between devices  34.1 us (34%)
  Pallas kernels  25.3 us (25%)
  other arithmetic  3.07 us (3%)
  local copies, waits for them, and re-layouts  1.48 us (1%)
    ppermute x21, waiting for transfers between devices, swap(): return lax.ppermute(value, 'expert', [(j, j ^ bit) for j in range(count)])  33.4 us
    ppermute x21, starting transfers between devices, swap(): return lax.ppermute(value, 'expert', [(j, j ^ bit) for j in range(count)])  24.8 us
    pallas_call x1, Pallas kernels, middle(): pl.pallas_call(lambda *refs: middle_kernel(cap, count, *refs), in_specs=[...  10.4 us
    all_to_all x2, starting transfers between devices, exchange(): lax.all_to_all(chunks, 'expert', split_axis=0, concat_axis=0, tiled=True,...  9.23 us
    pallas_call x1, Pallas kernels, pack_hidden(): pl.pallas_call(lambda *refs: pack_kernel(cap, *refs), in_specs=[VMEM, VME...  5.34 us
    pallas_call x1, Pallas kernels, keep_partials(): pl.pallas_call(lambda *refs: keep_kernel(count, *refs), in_specs=[ANY] *...  4.51 us
    pallas_call x1, Pallas kernels, finish(): pl.pallas_call(finish_kernel, grid=(2,), in_specs=[pl.BlockSpec((tile, 1)...  2.95 us
    pallas_call x1, Pallas kernels, factors(): pl.pallas_call(lambda *refs: factors_kernel(cap, *refs), grid=(4,), in_sp...  2.13 us
  transfers between devices with their start and end apart: 23, of which 15 were waited for; matrix products, arithmetic and copies ran while one was open for 4% of the time, Pallas kernels for 12%

profile of v7, /device:TPU:0, one launch (start us, length us, event | category | flops | bytes accessed | tf_op | source)
XLA Modules:
  0.0 100.1 jit_solution(3530342730592283950)
XLA Ops:
  0.6 4.1 %collective-permute-start = (bf16[128,1024]{1,0:T(8,128)(2,1)}, bf16[128,1024]{1,0:T(8,128)(2,1)S(1)}, u32[]{:S(2)}, u32[]{:S(2)}) collective-permute-start(bf16[128,1024]{1,0:T(8,128)(2,1)} %refs_0_), channel_id=1, source_target_pairs={{0,16},{1,17},{2,18},{3,19},{4,20},{5,21},{6,22},{7,23},{8,24},{9,... | collective-permute-start | bytes 786440 | tf_op jit(solution)/shard_map/ppermute | solution.py:25
  4.7 1.6 %collective-permute-start.1 = (bf16[128,1024]{1,0:T(8,128)(2,1)}, bf16[128,1024]{1,0:T(8,128)(2,1)S(1)}, u32[]{:S(2)}, u32[]{:S(2)}) collective-permute-start(bf16[128,1024]{1,0:T(8,128)(2,1)} %refs_0_), channel_id=1, source_target_pairs={{0,8},{1,9},{2,10},{3,11},{4,12},{5,13},{6,14},{7,15},{8,0},{9,1},... | collective-permute-start | bytes 786440 | tf_op jit(solution)/shard_map/ppermute | solution.py:25
  6.3 1.3 %slice_bitcast_fusion.2 = (bf16[96,1024]{1,0:T(8,128)(2,1)S(1)}, bf16[96,1024]{1,0:T(8,128)(2,1)S(1)}, bf16[96,1024]{1,0:T(8,128)(2,1)S(1)}, bf16[96,1024]{1,0:T(8,128)(2,1)S(1)}) fusion(bf16[1,384,1024]{2,1,0:T(8,128)(2,1)} %param.9), kind=kLoop, calls=%fused_computation.9 | loop fusion | bytes 1572864 | tf_op jit(solution)/shard_map/slice | solution.py:418
  7.6 1.6 %collective-permute-start.3 = (bf16[96,1024]{1,0:T(8,128)(2,1)S(1)}, bf16[96,1024]{1,0:T(8,128)(2,1)S(1)}, u32[]{:S(2)}, u32[]{:S(2)}) collective-permute-start(bf16[96,1024]{1,0:T(8,128)(2,1)S(1)} %get-tuple-element.68), channel_id=1, source_target_pairs={{0,4},{1,5},{2,6},{3,7},{4,0},{5,1},{6,2},{7,3},{8,12},{9,13},{10,... | collective-permute-start | bytes 589832 | tf_op jit(solution)/shard_map/ppermute | solution.py:25
  9.2 1.5 %collective-permute-start.2 = (bf16[96,1024]{1,0:T(8,128)(2,1)S(1)}, bf16[96,1024]{1,0:T(8,128)(2,1)S(1)}, u32[]{:S(2)}, u32[]{:S(2)}) collective-permute-start(bf16[96,1024]{1,0:T(8,128)(2,1)S(1)} %get-tuple-element.69), channel_id=1, source_target_pairs={{0,2},{1,3},{2,0},{3,1},{4,6},{5,7},{6,4},{7,5},{8,10},{9,11},{10,... | collective-permute-start | bytes 589832 | tf_op jit(solution)/shard_map/ppermute | solution.py:25
  10.7 0.1 stack.23.refs_0_
  10.7 5.3 %pack_hidden.1 = (bf16[8,192,384]{2,1,0:T(8,128)(2,1)}, f32[16,128]{1,0:T(8,128)}) custom-call(s32[8,128]{1,0:T(8,128)} %bitcast.32, f32[8,128]{1,0:T(8,128)} %bitcast.28, bf16[1024,768]{1,0:T(8,128)(2,1)} %bitcast.26), custom_call_target="tpu_custom_call" | custom-call | flops 1207959552 | bytes 1572864 | tf_op jit(solution)/shard_map/pack_hidden/pallas_call | solution.py:127
  16.1 0.0 copy-start.10
  16.1 0.0 collective-permute-done.3.refs_14_
  16.1 0.0 collective-permute-done.2.refs_10_
  16.1 0.9 collective-permute-done.refs_2_.refs_1_
  17.0 0.2 collective-permute-done.1.refs_3_.refs_2_
  17.2 4.5 %all-to-all-start = ((bf16[8,192,384]{2,1,0:T(8,128)(2,1)}), bf16[8,192,384]{2,1,0:T(8,128)(2,1)}, u32[]{:S(2)}, u32[]{:S(2)}) async-start(bf16[8,192,384]{2,1,0:T(8,128)(2,1)} %get-tuple-element.48), calls=%async_computation | async-start | bytes 2359296 | tf_op jit(solution)/shard_map/all_to_all | solution.py:407
  21.7 1.5 %collective-permute-start.9 = (bf16[96,1024]{1,0:T(8,128)(2,1)S(1)}, bf16[96,1024]{1,0:T(8,128)(2,1)S(1)}, u32[]{:S(2)}, u32[]{:S(2)}) collective-permute-start(bf16[96,1024]{1,0:T(8,128)(2,1)S(1)} %get-tuple-element.66), channel_id=1, source_target_pairs={{0,4},{1,5},{2,6},{3,7},{4,0},{5,1},{6,2},{7,3},{8,12},{9,13},{10,... | collective-permute-start | bytes 589832 | tf_op jit(solution)/shard_map/ppermute | solution.py:25
  23.2 1.5 %collective-permute-start.7 = (bf16[96,1024]{1,0:T(8,128)(2,1)S(1)}, bf16[96,1024]{1,0:T(8,128)(2,1)S(1)}, u32[]{:S(2)}, u32[]{:S(2)}) collective-permute-start(bf16[96,1024]{1,0:T(8,128)(2,1)S(1)} %get-tuple-element.67), channel_id=1, source_target_pairs={{0,2},{1,3},{2,0},{3,1},{4,6},{5,7},{6,4},{7,5},{8,10},{9,11},{10,... | collective-permute-start | bytes 589832 | tf_op jit(solution)/shard_map/ppermute | solution.py:25
  24.7 0.1 slice_bitcast_fusion
  24.8 0.6 collective-permute-start.6
  25.3 0.5 collective-permute-start.5
  25.9 3.5 %collective-permute-done.9.refs_15_ = bf16[96,1024]{1,0:T(8,128)(2,1)S(1)} collective-permute-done((bf16[96,1024]{1,0:T(8,128)(2,1)S(1)}, bf16[96,1024]{1,0:T(8,128)(2,1)S(1)}, u32[]{:S(2)}, u32[]{:S(2)}) %collective-permute-start.9) | collective-permute-done | bytes 196640 | tf_op jit(solution)/shard_map/ppermute | solution.py:25
  29.4 1.6 %collective-permute-start.10 = (bf16[192,1024]{1,0:T(8,128)(2,1)S(1)}, bf16[192,1024]{1,0:T(8,128)(2,1)S(1)}, u32[]{:S(2)}, u32[]{:S(2)}) collective-permute-start(bf16[192,1024]{1,0:T(8,128)(2,1)S(1)} %pad_maximum_fusion.1), channel_id=1, source_target_pairs={{0,2},{1,3},{2,0},{3,1},{4,6},{5,7},{6,4},{7,5},{8,10},{9,11},{10,... | collective-permute-start | bytes 1179656 | tf_op jit(solution)/shard_map/ppermute | solution.py:25
  31.0 0.0 collective-permute-done.7.refs_11_
  31.0 1.6 %collective-permute-start.8 = (bf16[192,1024]{1,0:T(8,128)(2,1)S(1)}, bf16[192,1024]{1,0:T(8,128)(2,1)S(1)}, u32[]{:S(2)}, u32[]{:S(2)}) collective-permute-start(bf16[192,1024]{1,0:T(8,128)(2,1)S(1)} %pad_maximum_fusion), channel_id=1, source_target_pairs={{0,4},{1,5},{2,6},{3,7},{4,0},{5,1},{6,2},{7,3},{8,12},{9,13},{10,... | collective-permute-start | bytes 1179656 | tf_op jit(solution)/shard_map/ppermute | solution.py:25
  32.6 2.1 %collective-permute-start.4 = (bf16[128,1024]{1,0:T(8,128)(2,1)S(1)}, bf16[128,1024]{1,0:T(8,128)(2,1)S(1)}, u32[]{:S(2)}, u32[]{:S(2)}) collective-permute-start(bf16[128,1024]{1,0:T(8,128)(2,1)S(1)} %collective-permute-done.refs_2_.refs_1_), channel_id=1, source_target_pairs={{0,8},{1,9},{2,10},{3,11},{4,12},{5,13},{6,14},{7,15},{8,0},{9,1},... | collective-permute-start | bytes 786440 | tf_op jit(solution)/shard_map/ppermute | solution.py:25
  34.7 3.1 %collective-permute-done.6.refs_13_ = bf16[192,1024]{1,0:T(8,128)(2,1)S(1)} collective-permute-done((bf16[192,1024]{1,0:T(8,128)(2,1)S(1)}, bf16[192,1024]{1,0:T(8,128)(2,1)S(1)}, u32[]{:S(2)}, u32[]{:S(2)}) %collective-permute-start.6) | collective-permute-done | bytes 393248 | tf_op jit(solution)/shard_map/ppermute | solution.py:25
  37.8 0.0 collective-permute-start.12
  37.8 1.6 %collective-permute-done.5.refs_12_ = bf16[192,1024]{1,0:T(8,128)(2,1)S(1)} collective-permute-done((bf16[192,1024]{1,0:T(8,128)(2,1)S(1)}, bf16[192,1024]{1,0:T(8,128)(2,1)S(1)}, u32[]{:S(2)}, u32[]{:S(2)}) %collective-permute-start.5) | collective-permute-done | bytes 393248 | tf_op jit(solution)/shard_map/ppermute | solution.py:25
  39.4 0.0 collective-permute-start.11
  39.4 8.0 %collective-permute-done.4.refs_4_.refs_3_ = bf16[128,1024]{1,0:T(8,128)(2,1)S(1)} collective-permute-done((bf16[128,1024]{1,0:T(8,128)(2,1)S(1)}, bf16[128,1024]{1,0:T(8,128)(2,1)S(1)}, u32[]{:S(2)}, u32[]{:S(2)}) %collective-permute-start.4) | collective-permute-done | bytes 262176 | tf_op jit(solution)/shard_map/ppermute | solution.py:25
  47.4 0.0 collective-permute-start.13
  47.4 0.0 collective-permute-done.10.refs_17_
  47.4 0.0 collective-permute-done.8.refs_16_
  47.4 0.6 collective-permute-start.14
  48.0 0.0 collective-permute-done.11.refs_5_.refs_4_
  48.0 0.9 collective-permute-done.13.refs_7_.refs_6_
  48.9 0.0 collective-permute-done.12.refs_6_.refs_5_
  49.0 0.3 collective-permute-done.14.refs_8_.refs_7_
  49.3 1.9 %all-to-all-done.refs_18_ = bf16[8,192,384]{2,1,0:T(8,128)(2,1)} async-done(((bf16[8,192,384]{2,1,0:T(8,128)(2,1)}), bf16[8,192,384]{2,1,0:T(8,128)(2,1)}, u32[]{:S(2)}, u32[]{:S(2)}) %all-to-all-start) | async-done | bytes 1179680 | tf_op jit(solution)/shard_map/all_to_all | solution.py:407
  51.2 0.0 copy-done.4
  51.2 0.0 copy-done.17
  51.2 10.4 %middle.1 = (bf16[8,192,384]{2,1,0:T(8,128)(2,1)}, bf16[192,1024]{1,0:T(8,128)(2,1)}, bf16[192,1024]{1,0:T(8,128)(2,1)}, bf16[192,1024]{1,0:T(8,128)(2,1)}, bf16...) custom-call(s32[5]{0:T(128)S(1)} %stack.23.refs_0_, bf16[128,1024]{1,0:T(8,128)(2,1)S(1)} %copy-done.3, ...), custom_call_target="tpu_custom_call" | custom-call | flops 4831838208 | bytes 4194304 | tf_op jit(solution)/shard_map/middle/pallas_call | solution.py:289
  61.6 4.7 %all-to-all-start.1 = ((bf16[8,192,384]{2,1,0:T(8,128)(2,1)}), bf16[8,192,384]{2,1,0:T(8,128)(2,1)S(1)}, u32[]{:S(2)}, u32[]{:S(2)}) async-start(bf16[8,192,384]{2,1,0:T(8,128)(2,1)} %get-tuple-element.49), calls=%async_computation.1 | async-start | bytes 2359296 | tf_op jit(solution)/shard_map/all_to_all | solution.py:407
  66.4 1.5 %collective-permute-start.17 = (bf16[192,1024]{1,0:T(8,128)(2,1)}, bf16[192,1024]{1,0:T(8,128)(2,1)S(1)}, u32[]{:S(2)}, u32[]{:S(2)}) collective-permute-start(bf16[192,1024]{1,0:T(8,128)(2,1)} %get-tuple-element.57), channel_id=1, source_target_pairs={{0,2},{1,3},{2,0},{3,1},{4,6},{5,7},{6,4},{7,5},{8,10},{9,11},{10,... | collective-permute-start | bytes 1179656 | tf_op jit(solution)/shard_map/ppermute | solution.py:25
  67.8 0.0 copy-done.16
  67.8 1.5 %collective-permute-start.18 = (bf16[192,1024]{1,0:T(8,128)(2,1)S(1)}, bf16[192,1024]{1,0:T(8,128)(2,1)S(1)}, u32[]{:S(2)}, u32[]{:S(2)}) collective-permute-start(bf16[192,1024]{1,0:T(8,128)(2,1)S(1)} %copy-done.16), channel_id=1, source_target_pairs={{0,4},{1,5},{2,6},{3,7},{4,0},{5,1},{6,2},{7,3},{8,12},{9,13},{10,... | collective-permute-start | bytes 1179656 | tf_op jit(solution)/shard_map/ppermute | solution.py:25
  69.4 0.5 collective-permute-start.15
  69.9 0.5 collective-permute-start.16
  70.4 4.5 %keep_partials.1 = (f32[384,1024]{1,0:T(8,128)}, bf16[384,1024]{1,0:T(8,128)(2,1)}) custom-call(bf16[128,1024]{1,0:T(8,128)(2,1)S(1)} %copy-done.3, bf16[128,1024]{1,0:T(8,128)(2,1)S(1)} %collective-permute-done.refs_2_.refs_1_, bf16[128,1024]{1,0:T(8,128)(2,1)S(1)} %collective-permute-done.1.refs_3_.refs_2_, ...), custom_call_target="tpu_custom_call" | custom-call | flops 1610612736 | bytes 4194304 | tf_op jit(solution)/shard_map/keep_partials/pallas_call | solution.py:341
  74.9 0.0 copy-start
  75.0 0.0 copy-start.2
  75.0 3.5 %collective-permute-done.17 = bf16[192,1024]{1,0:T(8,128)(2,1)S(1)} collective-permute-done((bf16[192,1024]{1,0:T(8,128)(2,1)}, bf16[192,1024]{1,0:T(8,128)(2,1)S(1)}, u32[]{:S(2)}, u32[]{:S(2)}) %collective-permute-start.17) | collective-permute-done | bytes 393248 | tf_op jit(solution)/shard_map/ppermute | solution.py:25
  78.5 1.3 %collective-permute-done.18 = bf16[192,1024]{1,0:T(8,128)(2,1)S(1)} collective-permute-done((bf16[192,1024]{1,0:T(8,128)(2,1)S(1)}, bf16[192,1024]{1,0:T(8,128)(2,1)S(1)}, u32[]{:S(2)}, u32[]{:S(2)}) %collective-permute-start.18) | collective-permute-done | bytes 393248 | tf_op jit(solution)/shard_map/ppermute | solution.py:25
  79.8 1.5 %add_convert_fusion.1 = (bf16[192,1024]{1,0:T(8,128)(2,1)S(1)}, bf16[192,1024]{1,0:T(8,128)(2,1)S(1)}) fusion(bf16[192,1024]{1,0:T(8,128)(2,1)S(1)} %collective-permute-done.18, bf16[384,1024]{1,0:T(8,128)(2,1)} %get-tuple-element.56, bf16[192,1024]{1,0:T(8,128)(2,1)S(1)} %collective-permute-done.17), kind=kLoop, calls=%fused_computation.3 | loop fusion | flops 1572864 | bytes 2359296 | tf_op jit(solution)/shard_map/convert_element_type | solution.py:453
  81.3 0.6 collective-permute-start.20
  81.9 1.5 %collective-permute-start.19 = (bf16[192,1024]{1,0:T(8,128)(2,1)S(1)}, bf16[192,1024]{1,0:T(8,128)(2,1)S(1)}, u32[]{:S(2)}, u32[]{:S(2)}) collective-permute-start(bf16[192,1024]{1,0:T(8,128)(2,1)S(1)} %get-tuple-element.65), channel_id=1, source_target_pairs={{0,4},{1,5},{2,6},{3,7},{4,0},{5,1},{6,2},{7,3},{8,12},{9,13},{10,... | collective-permute-start | bytes 1179656 | tf_op jit(solution)/shard_map/ppermute | solution.py:25
  83.5 0.0 copy-done
  83.5 2.1 %factors.1 = (bf16[1024,768]{1,0:T(8,128)(2,1)S(1)}, s32[1024,1]{1,0:T(8,128)S(1)}) custom-call(f32[16,128]{1,0:T(8,128)S(1)} %copy-done.1, f32[8,128]{1,0:T(8,128)S(1)} %bitcast.29, bf16[1024,768]{1,0:T(8,128)(2,1)S(1)} %bitcast.27), custom_call_target="tpu_custom_call" | custom-call | tf_op jit(solution)/shard_map/factors/pallas_call | solution.py:170
  85.6 1.3 %collective-permute-done.15 = bf16[192,1024]{1,0:T(8,128)(2,1)S(1)} collective-permute-done((bf16[192,1024]{1,0:T(8,128)(2,1)}, bf16[192,1024]{1,0:T(8,128)(2,1)S(1)}, u32[]{:S(2)}, u32[]{:S(2)}) %collective-permute-start.15) | collective-permute-done | bytes 393248 | tf_op jit(solution)/shard_map/ppermute | solution.py:25
  86.9 1.3 %collective-permute-done.16 = bf16[192,1024]{1,0:T(8,128)(2,1)S(1)} collective-permute-done((bf16[192,1024]{1,0:T(8,128)(2,1)}, bf16[192,1024]{1,0:T(8,128)(2,1)S(1)}, u32[]{:S(2)}, u32[]{:S(2)}) %collective-permute-start.16) | collective-permute-done | bytes 393248 | tf_op jit(solution)/shard_map/ppermute | solution.py:25
  88.2 0.3 convert_add_fusion
  88.5 6.4 %collective-permute-done.20 = bf16[192,1024]{1,0:T(8,128)(2,1)S(1)} collective-permute-done((bf16[192,1024]{1,0:T(8,128)(2,1)S(1)}, bf16[192,1024]{1,0:T(8,128)(2,1)S(1)}, u32[]{:S(2)}, u32[]{:S(2)}) %collective-permute-start.20) | collective-permute-done | bytes 393248 | tf_op jit(solution)/shard_map/ppermute | solution.py:25
  94.9 1.0 collective-permute-done.19
  95.9 1.2 %fusion = bf16[1,384,1024]{2,1,0:T(8,128)(2,1)} fusion(f32[384,1024]{1,0:T(8,128)S(1)} %convert_add_fusion, bf16[192,1024]{1,0:T(8,128)(2,1)S(1)} %collective-permute-done.20, bf16[192,1024]{1,0:T(8,128)(2,1)S(1)} %collective-permute-done.19), kind=kLoop, calls=%fused_computation.2 | loop fusion | flops 2359296 | bytes 3145728 | tf_op jit(solution)/shard_map/convert_element_type | solution.py:462
  97.1 0.0 all-to-all-done.1
  97.1 2.9 %finish.1 = bf16[1024,768]{1,0:T(8,128)(2,1)} custom-call(s32[1024,1]{1,0:T(8,128)S(1)} %get-tuple-element.34.column_ref, bf16[1024,768]{1,0:T(8,128)(2,1)S(1)} %get-tuple-element.35.factors_ref, bf16[1536,384]{1,0:T(8,128)(2,1)S(1)} %bitcast.25), custom_call_target="tpu_custom_call" | custom-call | flops 786432 | bytes 3145728 | tf_op jit(solution)/shard_map/finish/pallas_call | solution.py:377
  (31 shorter events, 0.1 us)
Async XLA Ops:
  0.6 16.3 %collective-permute-start = (bf16[128,1024]{1,0:T(8,128)(2,1)}, bf16[128,1024]{1,0:T(8,128)(2,1)S(1)}, u32[]{:S(2)}, u32[]{:S(2)}) collective-permute-start(bf16[128,1024]{1,0:T(8,128)(2,1)} %refs_0_), channel_id=1, source_target_pairs={{0,16},{1,17},{2,18},{3,19},{4,20},{5,21},{6,22},{7,23},{8,24},{9,... | collective-permute-start | bytes 786440 | tf_op jit(solution)/shard_map/ppermute | solution.py:25
  4.7 12.4 %collective-permute-start.1 = (bf16[128,1024]{1,0:T(8,128)(2,1)}, bf16[128,1024]{1,0:T(8,128)(2,1)S(1)}, u32[]{:S(2)}, u32[]{:S(2)}) collective-permute-start(bf16[128,1024]{1,0:T(8,128)(2,1)} %refs_0_), channel_id=1, source_target_pairs={{0,8},{1,9},{2,10},{3,11},{4,12},{5,13},{6,14},{7,15},{8,0},{9,1},... | collective-permute-start | bytes 786440 | tf_op jit(solution)/shard_map/ppermute | solution.py:25
  7.6 8.5 %collective-permute-start.3 = (bf16[96,1024]{1,0:T(8,128)(2,1)S(1)}, bf16[96,1024]{1,0:T(8,128)(2,1)S(1)}, u32[]{:S(2)}, u32[]{:S(2)}) collective-permute-start(bf16[96,1024]{1,0:T(8,128)(2,1)S(1)} %get-tuple-element.68), channel_id=1, source_target_pairs={{0,4},{1,5},{2,6},{3,7},{4,0},{5,1},{6,2},{7,3},{8,12},{9,13},{10,... | collective-permute-start | bytes 589832 | tf_op jit(solution)/shard_map/ppermute | solution.py:25
  9.2 7.0 %collective-permute-start.2 = (bf16[96,1024]{1,0:T(8,128)(2,1)S(1)}, bf16[96,1024]{1,0:T(8,128)(2,1)S(1)}, u32[]{:S(2)}, u32[]{:S(2)}) collective-permute-start(bf16[96,1024]{1,0:T(8,128)(2,1)S(1)} %get-tuple-element.69), channel_id=1, source_target_pairs={{0,2},{1,3},{2,0},{3,1},{4,6},{5,7},{6,4},{7,5},{8,10},{9,11},{10,... | collective-permute-start | bytes 589832 | tf_op jit(solution)/shard_map/ppermute | solution.py:25
  16.1 8.6 %copy-start.10 = (bf16[1,384,1024]{2,1,0:T(8,128)(2,1)S(1)}, bf16[1,384,1024]{2,1,0:T(8,128)(2,1)}, u32[]{:S(2)}) copy-start(bf16[1,384,1024]{2,1,0:T(8,128)(2,1)} %param.9) | copy-start | bytes 2359300
  17.2 34.0 %all-to-all-start = ((bf16[8,192,384]{2,1,0:T(8,128)(2,1)}), bf16[8,192,384]{2,1,0:T(8,128)(2,1)}, u32[]{:S(2)}, u32[]{:S(2)}) async-start(bf16[8,192,384]{2,1,0:T(8,128)(2,1)} %get-tuple-element.48), calls=%async_computation | async-start | bytes 2359296 | tf_op jit(solution)/shard_map/all_to_all | solution.py:407
  21.7 7.7 %collective-permute-start.9 = (bf16[96,1024]{1,0:T(8,128)(2,1)S(1)}, bf16[96,1024]{1,0:T(8,128)(2,1)S(1)}, u32[]{:S(2)}, u32[]{:S(2)}) collective-permute-start(bf16[96,1024]{1,0:T(8,128)(2,1)S(1)} %get-tuple-element.66), channel_id=1, source_target_pairs={{0,4},{1,5},{2,6},{3,7},{4,0},{5,1},{6,2},{7,3},{8,12},{9,13},{10,... | collective-permute-start | bytes 589832 | tf_op jit(solution)/shard_map/ppermute | solution.py:25
  23.2 16.2 %copy-start.3 = (bf16[128,1024]{1,0:T(8,128)(2,1)S(1)}, bf16[128,1024]{1,0:T(8,128)(2,1)}, u32[]{:S(2)}) copy-start(bf16[128,1024]{1,0:T(8,128)(2,1)} %refs_0_) | copy-start | bytes 786436
  23.2 7.8 %collective-permute-start.7 = (bf16[96,1024]{1,0:T(8,128)(2,1)S(1)}, bf16[96,1024]{1,0:T(8,128)(2,1)S(1)}, u32[]{:S(2)}, u32[]{:S(2)}) collective-permute-start(bf16[96,1024]{1,0:T(8,128)(2,1)S(1)} %get-tuple-element.67), channel_id=1, source_target_pairs={{0,2},{1,3},{2,0},{3,1},{4,6},{5,7},{6,4},{7,5},{8,10},{9,11},{10,... | collective-permute-start | bytes 589832 | tf_op jit(solution)/shard_map/ppermute | solution.py:25
  24.8 13.1 %collective-permute-start.6 = (bf16[192,1024]{1,0:T(8,128)(2,1)S(1)}, bf16[192,1024]{1,0:T(8,128)(2,1)S(1)}, u32[]{:S(2)}, u32[]{:S(2)}) collective-permute-start(bf16[192,1024]{1,0:T(8,128)(2,1)S(1)} %get-tuple-element.70), channel_id=1, source_target_pairs={{0,4},{1,5},{2,6},{3,7},{4,0},{5,1},{6,2},{7,3},{8,12},{9,13},{10,... | collective-permute-start | bytes 1179656 | tf_op jit(solution)/shard_map/ppermute | solution.py:25
  25.3 14.0 %collective-permute-start.5 = (bf16[192,1024]{1,0:T(8,128)(2,1)S(1)}, bf16[192,1024]{1,0:T(8,128)(2,1)S(1)}, u32[]{:S(2)}, u32[]{:S(2)}) collective-permute-start(bf16[192,1024]{1,0:T(8,128)(2,1)S(1)} %get-tuple-element.71), channel_id=1, source_target_pairs={{0,2},{1,3},{2,0},{3,1},{4,6},{5,7},{6,4},{7,5},{8,10},{9,11},{10,... | collective-permute-start | bytes 1179656 | tf_op jit(solution)/shard_map/ppermute | solution.py:25
  29.4 18.0 %collective-permute-start.10 = (bf16[192,1024]{1,0:T(8,128)(2,1)S(1)}, bf16[192,1024]{1,0:T(8,128)(2,1)S(1)}, u32[]{:S(2)}, u32[]{:S(2)}) collective-permute-start(bf16[192,1024]{1,0:T(8,128)(2,1)S(1)} %pad_maximum_fusion.1), channel_id=1, source_target_pairs={{0,2},{1,3},{2,0},{3,1},{4,6},{5,7},{6,4},{7,5},{8,10},{9,11},{10,... | collective-permute-start | bytes 1179656 | tf_op jit(solution)/shard_map/ppermute | solution.py:25
  31.0 16.4 %collective-permute-start.8 = (bf16[192,1024]{1,0:T(8,128)(2,1)S(1)}, bf16[192,1024]{1,0:T(8,128)(2,1)S(1)}, u32[]{:S(2)}, u32[]{:S(2)}) collective-permute-start(bf16[192,1024]{1,0:T(8,128)(2,1)S(1)} %pad_maximum_fusion), channel_id=1, source_target_pairs={{0,4},{1,5},{2,6},{3,7},{4,0},{5,1},{6,2},{7,3},{8,12},{9,13},{10,... | collective-permute-start | bytes 1179656 | tf_op jit(solution)/shard_map/ppermute | solution.py:25
  32.6 14.8 %collective-permute-start.4 = (bf16[128,1024]{1,0:T(8,128)(2,1)S(1)}, bf16[128,1024]{1,0:T(8,128)(2,1)S(1)}, u32[]{:S(2)}, u32[]{:S(2)}) collective-permute-start(bf16[128,1024]{1,0:T(8,128)(2,1)S(1)} %collective-permute-done.refs_2_.refs_1_), channel_id=1, source_target_pairs={{0,8},{1,9},{2,10},{3,11},{4,12},{5,13},{6,14},{7,15},{8,0},{9,1},... | collective-permute-start | bytes 786440 | tf_op jit(solution)/shard_map/ppermute | solution.py:25
  37.8 13.4 %copy-start.12 = (bf16[192,1024]{1,0:T(8,128)(2,1)}, bf16[192,1024]{1,0:T(8,128)(2,1)S(1)}, u32[]{:S(2)}) copy-start(bf16[192,1024]{1,0:T(8,128)(2,1)S(1)} %collective-permute-done.6.refs_13_) | copy-start | bytes 1179652
  37.8 11.1 %collective-permute-start.12 = (bf16[128,1024]{1,0:T(8,128)(2,1)S(1)}, bf16[128,1024]{1,0:T(8,128)(2,1)S(1)}, u32[]{:S(2)}, u32[]{:S(2)}) collective-permute-start(bf16[128,1024]{1,0:T(8,128)(2,1)S(1)} %collective-permute-done.refs_2_.refs_1_), channel_id=1, source_target_pairs={{0,1},{1,0},{2,3},{3,2},{4,5},{5,4},{6,7},{7,6},{8,9},{9,8},{10,11... | collective-permute-start | bytes 786440 | tf_op jit(solution)/shard_map/ppermute | solution.py:25
  39.4 9.6 %copy-start.13 = (bf16[192,1024]{1,0:T(8,128)(2,1)}, bf16[192,1024]{1,0:T(8,128)(2,1)S(1)}, u32[]{:S(2)}) copy-start(bf16[192,1024]{1,0:T(8,128)(2,1)S(1)} %collective-permute-done.5.refs_12_) | copy-start | bytes 1179652
  39.4 8.6 %collective-permute-start.11 = (bf16[128,1024]{1,0:T(8,128)(2,1)S(1)}, bf16[128,1024]{1,0:T(8,128)(2,1)S(1)}, u32[]{:S(2)}, u32[]{:S(2)}) collective-permute-start(bf16[128,1024]{1,0:T(8,128)(2,1)S(1)} %copy-done.3), channel_id=1, source_target_pairs={{0,1},{1,0},{2,3},{3,2},{4,5},{5,4},{6,7},{7,6},{8,9},{9,8},{10,11... | collective-permute-start | bytes 786440 | tf_op jit(solution)/shard_map/ppermute | solution.py:25
  47.4 1.5 %collective-permute-start.13 = (bf16[128,1024]{1,0:T(8,128)(2,1)S(1)}, bf16[128,1024]{1,0:T(8,128)(2,1)S(1)}, u32[]{:S(2)}, u32[]{:S(2)}) collective-permute-start(bf16[128,1024]{1,0:T(8,128)(2,1)S(1)} %collective-permute-done.1.refs_3_.refs_2_), channel_id=1, source_target_pairs={{0,1},{1,0},{2,3},{3,2},{4,5},{5,4},{6,7},{7,6},{8,9},{9,8},{10,11... | collective-permute-start | bytes 786440 | tf_op jit(solution)/shard_map/ppermute | solution.py:25
  47.4 1.5 %copy-start.14 = (bf16[192,1024]{1,0:T(8,128)(2,1)}, bf16[192,1024]{1,0:T(8,128)(2,1)S(1)}, u32[]{:S(2)}) copy-start(bf16[192,1024]{1,0:T(8,128)(2,1)S(1)} %collective-permute-done.10.refs_17_) | copy-start | bytes 1179652
  47.4 1.5 %copy-start.15 = (bf16[192,1024]{1,0:T(8,128)(2,1)}, bf16[192,1024]{1,0:T(8,128)(2,1)S(1)}, u32[]{:S(2)}) copy-start(bf16[192,1024]{1,0:T(8,128)(2,1)S(1)} %collective-permute-done.8.refs_16_) | copy-start | bytes 1179652
  47.4 1.9 %collective-permute-start.14 = (bf16[128,1024]{1,0:T(8,128)(2,1)S(1)}, bf16[128,1024]{1,0:T(8,128)(2,1)S(1)}, u32[]{:S(2)}, u32[]{:S(2)}) collective-permute-start(bf16[128,1024]{1,0:T(8,128)(2,1)S(1)} %collective-permute-done.4.refs_4_.refs_3_), channel_id=1, source_target_pairs={{0,1},{1,0},{2,3},{3,2},{4,5},{5,4},{6,7},{7,6},{8,9},{9,8},{10,11... | collective-permute-start | bytes 786440 | tf_op jit(solution)/shard_map/ppermute | solution.py:25
  48.0 3.2 %copy-start.6 = (bf16[128,1024]{1,0:T(8,128)(2,1)}, bf16[128,1024]{1,0:T(8,128)(2,1)S(1)}, u32[]{:S(2)}) copy-start(bf16[128,1024]{1,0:T(8,128)(2,1)S(1)} %collective-permute-done.11.refs_5_.refs_4_) | copy-start | bytes 786436
  48.9 2.3 %copy-start.8 = (bf16[128,1024]{1,0:T(8,128)(2,1)}, bf16[128,1024]{1,0:T(8,128)(2,1)S(1)}, u32[]{:S(2)}) copy-start(bf16[128,1024]{1,0:T(8,128)(2,1)S(1)} %collective-permute-done.13.refs_7_.refs_6_) | copy-start | bytes 786436
  49.0 2.2 %copy-start.4 = (bf16[128,1024]{1,0:T(8,128)(2,1)}, bf16[128,1024]{1,0:T(8,128)(2,1)S(1)}, u32[]{:S(2)}) copy-start(bf16[128,1024]{1,0:T(8,128)(2,1)S(1)} %collective-permute-done.12.refs_6_.refs_5_) | copy-start | bytes 786436
  49.3 1.9 %copy-start.17 = (bf16[128,1024]{1,0:T(8,128)(2,1)}, bf16[128,1024]{1,0:T(8,128)(2,1)S(1)}, u32[]{:S(2)}) copy-start(bf16[128,1024]{1,0:T(8,128)(2,1)S(1)} %collective-permute-done.14.refs_8_.refs_7_) | copy-start | bytes 786436
  61.6 6.2 %copy-start.16 = (bf16[192,1024]{1,0:T(8,128)(2,1)S(1)}, bf16[192,1024]{1,0:T(8,128)(2,1)}, u32[]{:S(2)}) copy-start(bf16[192,1024]{1,0:T(8,128)(2,1)} %get-tuple-element.58) | copy-start | bytes 1179652
  61.6 8.8 %copy-start.5 = (bf16[128,1024]{1,0:T(8,128)(2,1)S(1)}, bf16[128,1024]{1,0:T(8,128)(2,1)}, u32[]{:S(2)}) copy-start(bf16[128,1024]{1,0:T(8,128)(2,1)} %copy-done.4) | copy-start | bytes 786436
  61.6 8.8 %copy-start.7 = (bf16[128,1024]{1,0:T(8,128)(2,1)S(1)}, bf16[128,1024]{1,0:T(8,128)(2,1)}, u32[]{:S(2)}) copy-start(bf16[128,1024]{1,0:T(8,128)(2,1)} %copy-done.6) | copy-start | bytes 786436
  61.6 8.8 %copy-start.9 = (bf16[128,1024]{1,0:T(8,128)(2,1)S(1)}, bf16[128,1024]{1,0:T(8,128)(2,1)}, u32[]{:S(2)}) copy-start(bf16[128,1024]{1,0:T(8,128)(2,1)} %copy-done.8) | copy-start | bytes 786436
  61.6 35.5 %all-to-all-start.1 = ((bf16[8,192,384]{2,1,0:T(8,128)(2,1)}), bf16[8,192,384]{2,1,0:T(8,128)(2,1)S(1)}, u32[]{:S(2)}, u32[]{:S(2)}) async-start(bf16[8,192,384]{2,1,0:T(8,128)(2,1)} %get-tuple-element.49), calls=%async_computation.1 | async-start | bytes 2359296 | tf_op jit(solution)/shard_map/all_to_all | solution.py:407
  66.4 12.1 %collective-permute-start.17 = (bf16[192,1024]{1,0:T(8,128)(2,1)}, bf16[192,1024]{1,0:T(8,128)(2,1)S(1)}, u32[]{:S(2)}, u32[]{:S(2)}) collective-permute-start(bf16[192,1024]{1,0:T(8,128)(2,1)} %get-tuple-element.57), channel_id=1, source_target_pairs={{0,2},{1,3},{2,0},{3,1},{4,6},{5,7},{6,4},{7,5},{8,10},{9,11},{10,... | collective-permute-start | bytes 1179656 | tf_op jit(solution)/shard_map/ppermute | solution.py:25
  67.8 11.9 %collective-permute-start.18 = (bf16[192,1024]{1,0:T(8,128)(2,1)S(1)}, bf16[192,1024]{1,0:T(8,128)(2,1)S(1)}, u32[]{:S(2)}, u32[]{:S(2)}) collective-permute-start(bf16[192,1024]{1,0:T(8,128)(2,1)S(1)} %copy-done.16), channel_id=1, source_target_pairs={{0,4},{1,5},{2,6},{3,7},{4,0},{5,1},{6,2},{7,3},{8,12},{9,13},{10,... | collective-permute-start | bytes 1179656 | tf_op jit(solution)/shard_map/ppermute | solution.py:25
  69.4 17.5 %collective-permute-start.15 = (bf16[192,1024]{1,0:T(8,128)(2,1)}, bf16[192,1024]{1,0:T(8,128)(2,1)S(1)}, u32[]{:S(2)}, u32[]{:S(2)}) collective-permute-start(bf16[192,1024]{1,0:T(8,128)(2,1)} %get-tuple-element.52), channel_id=1, source_target_pairs={{0,2},{1,3},{2,0},{3,1},{4,6},{5,7},{6,4},{7,5},{8,10},{9,11},{10,... | collective-permute-start | bytes 1179656 | tf_op jit(solution)/shard_map/ppermute | solution.py:25
  69.9 18.3 %collective-permute-start.16 = (bf16[192,1024]{1,0:T(8,128)(2,1)}, bf16[192,1024]{1,0:T(8,128)(2,1)S(1)}, u32[]{:S(2)}, u32[]{:S(2)}) collective-permute-start(bf16[192,1024]{1,0:T(8,128)(2,1)} %get-tuple-element.53), channel_id=1, source_target_pairs={{0,4},{1,5},{2,6},{3,7},{4,0},{5,1},{6,2},{7,3},{8,12},{9,13},{10,... | collective-permute-start | bytes 1179656 | tf_op jit(solution)/shard_map/ppermute | solution.py:25
  74.9 8.5 %copy-start = (bf16[128,8,768]{2,1,0:T(8,128)(2,1)S(1)}, bf16[128,8,768]{2,1,0:T(8,128)(2,1)}, u32[]{:S(2)}) copy-start(bf16[128,8,768]{2,1,0:T(8,128)(2,1)} %param.8) | copy-start | bytes 4718596
  75.0 8.5 %copy-start.1 = (f32[16,128]{1,0:T(8,128)S(1)}, f32[16,128]{1,0:T(8,128)}, u32[]{:S(2)}) copy-start(f32[16,128]{1,0:T(8,128)} %get-tuple-element.33.refs_0_) | copy-start | bytes 24580
  75.0 8.5 %copy-start.2 = (f32[128,8]{0,1:T(8,128)S(1)}, f32[128,8]{0,1:T(8,128)}, u32[]{:S(2)}) copy-start(f32[128,8]{0,1:T(8,128)} %param.6) | copy-start | bytes 12292
  79.8 8.4 %copy-start.11 = (f32[384,1024]{1,0:T(8,128)S(1)}, f32[384,1024]{1,0:T(8,128)}, u32[]{:S(2)}) copy-start(f32[384,1024]{1,0:T(8,128)} %get-tuple-element.51) | copy-start | bytes 4718596
  81.3 13.6 %collective-permute-start.20 = (bf16[192,1024]{1,0:T(8,128)(2,1)S(1)}, bf16[192,1024]{1,0:T(8,128)(2,1)S(1)}, u32[]{:S(2)}, u32[]{:S(2)}) collective-permute-start(bf16[192,1024]{1,0:T(8,128)(2,1)S(1)} %get-tuple-element.64), channel_id=1, source_target_pairs={{0,2},{1,3},{2,0},{3,1},{4,6},{5,7},{6,4},{7,5},{8,10},{9,11},{10,... | collective-permute-start | bytes 1179656 | tf_op jit(solution)/shard_map/ppermute | solution.py:25
  81.9 14.0 %collective-permute-start.19 = (bf16[192,1024]{1,0:T(8,128)(2,1)S(1)}, bf16[192,1024]{1,0:T(8,128)(2,1)S(1)}, u32[]{:S(2)}, u32[]{:S(2)}) collective-permute-start(bf16[192,1024]{1,0:T(8,128)(2,1)S(1)} %get-tuple-element.65), channel_id=1, source_target_pairs={{0,4},{1,5},{2,6},{3,7},{4,0},{5,1},{6,2},{7,3},{8,12},{9,13},{10,... | collective-permute-start | bytes 1179656 | tf_op jit(solution)/shard_map/ppermute | solution.py:25

commit v8 on v7

--- a/solution.py
+++ b/solution.py
@@ -137,7 +137,7 @@
             pltpu.VMEM((members * cap, rows), BF16),
             pltpu.SemaphoreType.DMA,
         ],
-        compiler_params=params(60),
+        compiler_params=params(40),
         cost_estimate=cost(2 * members * cap * rows * width, 2 * rows * both),
         name="pack_hidden",
     )(ids.T, gates.T, flat_pre)

time: 100 us -> 101 us (1.010)
  local copies, waits for them, and re-layouts: 1.48 us -> 9.56 us
  waiting for transfers between devices: 35.3 us -> 28.1 us
    unnamed x36 -> x38, local copies, waits for them, and re-layouts: 0.08 us -> 6.34 us
    ppermute x21, waiting for transfers between devices: 33.4 us -> 27.2 us  [swap(): return lax.ppermute(value, 'expert', [(j, j ^ bit) for j in range(count)])]
    slice x1, local copies, waits for them, and re-layouts: 0.05 us -> 1.17 us  [per_device(): x_b, y_a = (swap(own_w[half:], X_BIT), swap(own_w[:half], Y_BIT))]
    all_to_all x2, waiting for transfers between devices: 1.87 us -> 0.84 us  [exchange(): lax.all_to_all(chunks, 'expert', split_axis=0, concat_axis=0, tiled=True,...]
  transfers between devices with their start and end apart: 23 -> 23, of which waited for: 15 -> 12; matrix products, arithmetic and copies ran while one was open for 4% -> 6% of each run, Pallas kernels for 12% -> 11%
where the time goes in v8:
time: 101 us; the launch traced here: 100 us
  starting transfers between devices  34.3 us (34%)
  waiting for transfers between devices  28.1 us (28%)
  Pallas kernels  24.7 us (24%)
  local copies, waits for them, and re-layouts  9.56 us (9%)
  other arithmetic  3.07 us (3%)
    ppermute x21, waiting for transfers between devices, swap(): return lax.ppermute(value, 'expert', [(j, j ^ bit) for j in range(count)])  27.2 us
    ppermute x21, starting transfers between devices, swap(): return lax.ppermute(value, 'expert', [(j, j ^ bit) for j in range(count)])  24.8 us
    pallas_call x1, Pallas kernels, middle(): pl.pallas_call(lambda *refs: middle_kernel(cap, count, *refs), in_specs=[...  10.3 us
    all_to_all x2, starting transfers between devices, exchange(): lax.all_to_all(chunks, 'expert', split_axis=0, concat_axis=0, tiled=True,...  9.49 us
    unnamed x38, local copies, waits for them, and re-layouts  6.34 us
    pallas_call x1, Pallas kernels, pack_hidden(): pl.pallas_call(lambda *refs: pack_kernel(cap, *refs), in_specs=[VMEM, VME...  4.75 us
    pallas_call x1, Pallas kernels, keep_partials(): pl.pallas_call(lambda *refs: keep_kernel(count, *refs), in_specs=[ANY] *...  4.5 us
    pallas_call x1, Pallas kernels, finish(): pl.pallas_call(finish_kernel, grid=(2,), in_specs=[pl.BlockSpec((tile, 1)...  2.95 us
  transfers between devices with their start and end apart: 23, of which 12 were waited for; matrix products, arithmetic and copies ran while one was open for 6% of the time, Pallas kernels for 11%

profile of v8, /device:TPU:0, one launch (start us, length us, event | category | flops | bytes accessed | tf_op | source)
XLA Modules:
  0.0 100.5 jit_solution(12195845956621990834)
XLA Ops:
  0.7 4.1 %collective-permute-start = (bf16[128,1024]{1,0:T(8,128)(2,1)}, bf16[128,1024]{1,0:T(8,128)(2,1)S(1)}, u32[]{:S(2)}, u32[]{:S(2)}) collective-permute-start(bf16[128,1024]{1,0:T(8,128)(2,1)} %refs_0_), channel_id=1, source_target_pairs={{0,16},{1,17},{2,18},{3,19},{4,20},{5,21},{6,22},{7,23},{8,24},{9,... | collective-permute-start | bytes 786440 | tf_op jit(solution)/shard_map/ppermute | solution.py:25
  4.8 1.6 %collective-permute-start.1 = (bf16[128,1024]{1,0:T(8,128)(2,1)}, bf16[128,1024]{1,0:T(8,128)(2,1)S(1)}, u32[]{:S(2)}, u32[]{:S(2)}) collective-permute-start(bf16[128,1024]{1,0:T(8,128)(2,1)} %refs_0_), channel_id=1, source_target_pairs={{0,8},{1,9},{2,10},{3,11},{4,12},{5,13},{6,14},{7,15},{8,0},{9,1},... | collective-permute-start | bytes 786440 | tf_op jit(solution)/shard_map/ppermute | solution.py:25
  6.3 2.0 %slice_bitcast_fusion.2 = (bf16[96,1024]{1,0:T(8,128)(2,1)}, bf16[96,1024]{1,0:T(8,128)(2,1)S(1)}, bf16[96,1024]{1,0:T(8,128)(2,1)S(1)}, bf16[96,1024]{1,0:T(8,128)(2,1)S(1)}) fusion(bf16[1,384,1024]{2,1,0:T(8,128)(2,1)} %param.9), kind=kLoop, calls=%fused_computation.9 | loop fusion | bytes 1572864 | tf_op jit(solution)/shard_map/slice | solution.py:418
  8.3 1.5 %collective-permute-start.3 = (bf16[96,1024]{1,0:T(8,128)(2,1)S(1)}, bf16[96,1024]{1,0:T(8,128)(2,1)S(1)}, u32[]{:S(2)}, u32[]{:S(2)}) collective-permute-start(bf16[96,1024]{1,0:T(8,128)(2,1)S(1)} %get-tuple-element.68), channel_id=1, source_target_pairs={{0,4},{1,5},{2,6},{3,7},{4,0},{5,1},{6,2},{7,3},{8,12},{9,13},{10,... | collective-permute-start | bytes 589832 | tf_op jit(solution)/shard_map/ppermute | solution.py:25
  9.8 1.5 %collective-permute-start.2 = (bf16[96,1024]{1,0:T(8,128)(2,1)S(1)}, bf16[96,1024]{1,0:T(8,128)(2,1)S(1)}, u32[]{:S(2)}, u32[]{:S(2)}) collective-permute-start(bf16[96,1024]{1,0:T(8,128)(2,1)S(1)} %get-tuple-element.69), channel_id=1, source_target_pairs={{0,2},{1,3},{2,0},{3,1},{4,6},{5,7},{6,4},{7,5},{8,10},{9,11},{10,... | collective-permute-start | bytes 589832 | tf_op jit(solution)/shard_map/ppermute | solution.py:25
  11.3 0.1 stack.23.refs_0_
  11.4 4.7 %pack_hidden.1 = (bf16[8,192,384]{2,1,0:T(8,128)(2,1)}, f32[16,128]{1,0:T(8,128)S(1)}) custom-call(s32[8,128]{1,0:T(8,128)S(1)} %bitcast.30, f32[8,128]{1,0:T(8,128)S(1)} %bitcast.28, bf16[1024,768]{1,0:T(8,128)(2,1)S(1)} %bitcast.26), custom_call_target="tpu_custom_call" | custom-call | flops 1207959552 | bytes 1572864 | tf_op jit(solution)/shard_map/pack_hidden/pallas_call | solution.py:127
  16.2 0.0 collective-permute-done.3.refs_14_
  16.2 0.0 collective-permute-done.2.refs_10_
  16.2 0.8 collective-permute-done.refs_2_.refs_1_
  17.0 0.2 collective-permute-done.1.refs_3_.refs_2_
  17.2 4.5 %all-to-all-start = ((bf16[8,192,384]{2,1,0:T(8,128)(2,1)}), bf16[8,192,384]{2,1,0:T(8,128)(2,1)}, u32[]{:S(2)}, u32[]{:S(2)}) async-start(bf16[8,192,384]{2,1,0:T(8,128)(2,1)} %get-tuple-element.48), calls=%async_computation | async-start | bytes 2359296 | tf_op jit(solution)/shard_map/all_to_all | solution.py:407
  21.7 1.5 %collective-permute-start.9 = (bf16[96,1024]{1,0:T(8,128)(2,1)}, bf16[96,1024]{1,0:T(8,128)(2,1)S(1)}, u32[]{:S(2)}, u32[]{:S(2)}) collective-permute-start(bf16[96,1024]{1,0:T(8,128)(2,1)} %get-tuple-element.66), channel_id=1, source_target_pairs={{0,4},{1,5},{2,6},{3,7},{4,0},{5,1},{6,2},{7,3},{8,12},{9,13},{10,... | collective-permute-start | bytes 589832 | tf_op jit(solution)/shard_map/ppermute | solution.py:25
  23.2 1.5 %collective-permute-start.7 = (bf16[96,1024]{1,0:T(8,128)(2,1)S(1)}, bf16[96,1024]{1,0:T(8,128)(2,1)S(1)}, u32[]{:S(2)}, u32[]{:S(2)}) collective-permute-start(bf16[96,1024]{1,0:T(8,128)(2,1)S(1)} %get-tuple-element.67), channel_id=1, source_target_pairs={{0,2},{1,3},{2,0},{3,1},{4,6},{5,7},{6,4},{7,5},{8,10},{9,11},{10,... | collective-permute-start | bytes 589832 | tf_op jit(solution)/shard_map/ppermute | solution.py:25
  24.7 1.2 %slice_bitcast_fusion = (bf16[192,1024]{1,0:T(8,128)(2,1)S(1)}, bf16[192,1024]{1,0:T(8,128)(2,1)S(1)}) fusion(bf16[1,384,1024]{2,1,0:T(8,128)(2,1)} %param.9), kind=kLoop, calls=%fused_computation.7 | loop fusion | bytes 1572864 | tf_op jit(solution)/shard_map/slice | solution.py:423
  25.9 0.6 collective-permute-start.6
  26.5 0.5 collective-permute-start.5
  27.0 2.6 %collective-permute-done.9.refs_15_ = bf16[96,1024]{1,0:T(8,128)(2,1)S(1)} collective-permute-done((bf16[96,1024]{1,0:T(8,128)(2,1)}, bf16[96,1024]{1,0:T(8,128)(2,1)S(1)}, u32[]{:S(2)}, u32[]{:S(2)}) %collective-permute-start.9) | collective-permute-done | bytes 196640 | tf_op jit(solution)/shard_map/ppermute | solution.py:25
  29.7 1.6 %collective-permute-start.10 = (bf16[192,1024]{1,0:T(8,128)(2,1)S(1)}, bf16[192,1024]{1,0:T(8,128)(2,1)S(1)}, u32[]{:S(2)}, u32[]{:S(2)}) collective-permute-start(bf16[192,1024]{1,0:T(8,128)(2,1)S(1)} %pad_maximum_fusion.1), channel_id=1, source_target_pairs={{0,2},{1,3},{2,0},{3,1},{4,6},{5,7},{6,4},{7,5},{8,10},{9,11},{10,... | collective-permute-start | bytes 1179656 | tf_op jit(solution)/shard_map/ppermute | solution.py:25
  31.2 0.0 collective-permute-done.7.refs_11_
  31.2 1.6 %collective-permute-start.8 = (bf16[192,1024]{1,0:T(8,128)(2,1)S(1)}, bf16[192,1024]{1,0:T(8,128)(2,1)S(1)}, u32[]{:S(2)}, u32[]{:S(2)}) collective-permute-start(bf16[192,1024]{1,0:T(8,128)(2,1)S(1)} %pad_maximum_fusion), channel_id=1, source_target_pairs={{0,4},{1,5},{2,6},{3,7},{4,0},{5,1},{6,2},{7,3},{8,12},{9,13},{10,... | collective-permute-start | bytes 1179656 | tf_op jit(solution)/shard_map/ppermute | solution.py:25
  32.8 2.1 %collective-permute-start.4 = (bf16[128,1024]{1,0:T(8,128)(2,1)S(1)}, bf16[128,1024]{1,0:T(8,128)(2,1)S(1)}, u32[]{:S(2)}, u32[]{:S(2)}) collective-permute-start(bf16[128,1024]{1,0:T(8,128)(2,1)S(1)} %collective-permute-done.refs_2_.refs_1_), channel_id=1, source_target_pairs={{0,8},{1,9},{2,10},{3,11},{4,12},{5,13},{6,14},{7,15},{8,0},{9,1},... | collective-permute-start | bytes 786440 | tf_op jit(solution)/shard_map/ppermute | solution.py:25
  34.9 3.1 %collective-permute-done.6.refs_13_ = bf16[192,1024]{1,0:T(8,128)(2,1)S(1)} collective-permute-done((bf16[192,1024]{1,0:T(8,128)(2,1)S(1)}, bf16[192,1024]{1,0:T(8,128)(2,1)S(1)}, u32[]{:S(2)}, u32[]{:S(2)}) %collective-permute-start.6) | collective-permute-done | bytes 393248 | tf_op jit(solution)/shard_map/ppermute | solution.py:25
  38.1 0.0 collective-permute-start.12
  38.1 1.3 %collective-permute-done.5.refs_12_ = bf16[192,1024]{1,0:T(8,128)(2,1)S(1)} collective-permute-done((bf16[192,1024]{1,0:T(8,128)(2,1)S(1)}, bf16[192,1024]{1,0:T(8,128)(2,1)S(1)}, u32[]{:S(2)}, u32[]{:S(2)}) %collective-permute-start.5) | collective-permute-done | bytes 393248 | tf_op jit(solution)/shard_map/ppermute | solution.py:25
  39.4 0.0 collective-permute-start.11
  39.4 8.0 %collective-permute-done.4.refs_4_.refs_3_ = bf16[128,1024]{1,0:T(8,128)(2,1)S(1)} collective-permute-done((bf16[128,1024]{1,0:T(8,128)(2,1)S(1)}, bf16[128,1024]{1,0:T(8,128)(2,1)S(1)}, u32[]{:S(2)}, u32[]{:S(2)}) %collective-permute-start.4) | collective-permute-done | bytes 262176 | tf_op jit(solution)/shard_map/ppermute | solution.py:25
  47.4 0.0 collective-permute-start.13
  47.4 0.0 collective-permute-done.10.refs_17_
  47.5 0.0 collective-permute-done.8.refs_16_
  47.5 0.6 collective-permute-start.14
  48.0 0.0 collective-permute-done.11.refs_5_.refs_4_
  48.0 0.9 collective-permute-done.13.refs_7_.refs_6_
  49.0 0.0 collective-permute-done.12.refs_6_.refs_5_
  49.0 0.7 copy-done.11
  49.7 0.7 copy-done.7
  50.4 0.0 collective-permute-done.14.refs_8_.refs_7_
  50.4 0.8 all-to-all-done.refs_18_
  51.2 10.3 %middle.1 = (bf16[8,192,384]{2,1,0:T(8,128)(2,1)}, bf16[192,1024]{1,0:T(8,128)(2,1)}, bf16[192,1024]{1,0:T(8,128)(2,1)}, bf16[192,1024]{1,0:T(8,128)(2,1)}, bf16...) custom-call(s32[5]{0:T(128)S(1)} %stack.23.refs_0_, bf16[128,1024]{1,0:T(8,128)(2,1)S(1)} %copy-done.4, ...), custom_call_target="tpu_custom_call" | custom-call | flops 4831838208 | bytes 4194304 | tf_op jit(solution)/shard_map/middle/pallas_call | solution.py:289
  61.6 5.0 %all-to-all-start.1 = ((bf16[8,192,384]{2,1,0:T(8,128)(2,1)}), bf16[8,192,384]{2,1,0:T(8,128)(2,1)S(1)}, u32[]{:S(2)}, u32[]{:S(2)}) async-start(bf16[8,192,384]{2,1,0:T(8,128)(2,1)} %get-tuple-element.49), calls=%async_computation.1 | async-start | bytes 2359296 | tf_op jit(solution)/shard_map/all_to_all | solution.py:407
  66.6 1.5 %collective-permute-start.17 = (bf16[192,1024]{1,0:T(8,128)(2,1)}, bf16[192,1024]{1,0:T(8,128)(2,1)S(1)}, u32[]{:S(2)}, u32[]{:S(2)}) collective-permute-start(bf16[192,1024]{1,0:T(8,128)(2,1)} %get-tuple-element.57), channel_id=1, source_target_pairs={{0,2},{1,3},{2,0},{3,1},{4,6},{5,7},{6,4},{7,5},{8,10},{9,11},{10,... | collective-permute-start | bytes 1179656 | tf_op jit(solution)/shard_map/ppermute | solution.py:25
  68.0 1.5 %collective-permute-start.18 = (bf16[192,1024]{1,0:T(8,128)(2,1)}, bf16[192,1024]{1,0:T(8,128)(2,1)S(1)}, u32[]{:S(2)}, u32[]{:S(2)}) collective-permute-start(bf16[192,1024]{1,0:T(8,128)(2,1)} %get-tuple-element.58), channel_id=1, source_target_pairs={{0,4},{1,5},{2,6},{3,7},{4,0},{5,1},{6,2},{7,3},{8,12},{9,13},{10,... | collective-permute-start | bytes 1179656 | tf_op jit(solution)/shard_map/ppermute | solution.py:25
  69.6 0.5 collective-permute-start.15
  70.1 0.5 collective-permute-start.16
  70.6 0.9 copy-done.6
  71.6 0.9 copy-done.8
  72.5 0.9 copy-done.10
  73.5 0.9 copy-done.12
  74.4 4.5 %keep_partials.1 = (f32[384,1024]{1,0:T(8,128)}, bf16[384,1024]{1,0:T(8,128)(2,1)}) custom-call(bf16[128,1024]{1,0:T(8,128)(2,1)S(1)} %copy-done.4, bf16[128,1024]{1,0:T(8,128)(2,1)S(1)} %collective-permute-done.refs_2_.refs_1_, bf16[128,1024]{1,0:T(8,128)(2,1)S(1)} %collective-permute-done.1.refs_3_.refs_2_, bf16[128,1024]{1,0:T(8,128)(2,1)S(1)} %copy-done.6, ...), custom_call_target="tpu_custom_call" | custom-call | flops 1610612736 | bytes 4194304 | tf_op jit(solution)/shard_map/keep_partials/pallas_call | solution.py:341
  78.9 1.3 %collective-permute-done.18 = bf16[192,1024]{1,0:T(8,128)(2,1)S(1)} collective-permute-done((bf16[192,1024]{1,0:T(8,128)(2,1)}, bf16[192,1024]{1,0:T(8,128)(2,1)S(1)}, u32[]{:S(2)}, u32[]{:S(2)}) %collective-permute-start.18) | collective-permute-done | bytes 393248 | tf_op jit(solution)/shard_map/ppermute | solution.py:25
  80.2 1.5 %add_convert_fusion.1 = (bf16[192,1024]{1,0:T(8,128)(2,1)S(1)}, bf16[192,1024]{1,0:T(8,128)(2,1)S(1)}) fusion(bf16[192,1024]{1,0:T(8,128)(2,1)S(1)} %collective-permute-done.18, bf16[384,1024]{1,0:T(8,128)(2,1)} %get-tuple-element.56, bf16[192,1024]{1,0:T(8,128)(2,1)S(1)} %collective-permute-done.17), kind=kLoop, calls=%fused_computation.3 | loop fusion | flops 1572864 | bytes 2359296 | tf_op jit(solution)/shard_map/convert_element_type | solution.py:453
  81.8 0.6 collective-permute-start.20
  82.4 1.5 %collective-permute-start.19 = (bf16[192,1024]{1,0:T(8,128)(2,1)S(1)}, bf16[192,1024]{1,0:T(8,128)(2,1)S(1)}, u32[]{:S(2)}, u32[]{:S(2)}) collective-permute-start(bf16[192,1024]{1,0:T(8,128)(2,1)S(1)} %get-tuple-element.65), channel_id=1, source_target_pairs={{0,4},{1,5},{2,6},{3,7},{4,0},{5,1},{6,2},{7,3},{8,12},{9,13},{10,... | collective-permute-start | bytes 1179656 | tf_op jit(solution)/shard_map/ppermute | solution.py:25
  83.9 2.1 %factors.1 = (bf16[1024,768]{1,0:T(8,128)(2,1)S(1)}, s32[1024,1]{1,0:T(8,128)S(1)}) custom-call(f32[16,128]{1,0:T(8,128)S(1)} %get-tuple-element.33.refs_0_, f32[8,128]{1,0:T(8,128)S(1)} %bitcast.29, bf16[1024,768]{1,0:T(8,128)(2,1)S(1)} %bitcast.27), custom_call_target="tpu_custom_call" | custom-call | tf_op jit(solution)/shard_map/factors/pallas_call | solution.py:170
  86.0 0.0 copy-start.1
  86.0 1.1 %copy-done.1 = bf16[1024,768]{1,0:T(8,128)(2,1)} copy-done((bf16[1024,768]{1,0:T(8,128)(2,1)}, bf16[1024,768]{1,0:T(8,128)(2,1)S(1)}, u32[]{:S(2)}) %copy-start.1) | copy-done | bytes 1572888
  87.1 0.0 collective-permute-done.15
  87.2 1.5 %collective-permute-done.16 = bf16[192,1024]{1,0:T(8,128)(2,1)S(1)} collective-permute-done((bf16[192,1024]{1,0:T(8,128)(2,1)}, bf16[192,1024]{1,0:T(8,128)(2,1)S(1)}, u32[]{:S(2)}, u32[]{:S(2)}) %collective-permute-start.16) | collective-permute-done | bytes 393248 | tf_op jit(solution)/shard_map/ppermute | solution.py:25
  88.6 0.3 convert_add_fusion
  89.0 0.0 copy-start.2
  89.0 6.2 %collective-permute-done.20 = bf16[192,1024]{1,0:T(8,128)(2,1)S(1)} collective-permute-done((bf16[192,1024]{1,0:T(8,128)(2,1)S(1)}, bf16[192,1024]{1,0:T(8,128)(2,1)S(1)}, u32[]{:S(2)}, u32[]{:S(2)}) %collective-permute-start.20) | collective-permute-done | bytes 393248 | tf_op jit(solution)/shard_map/ppermute | solution.py:25
  95.1 1.2 %collective-permute-done.19 = bf16[192,1024]{1,0:T(8,128)(2,1)S(1)} collective-permute-done((bf16[192,1024]{1,0:T(8,128)(2,1)S(1)}, bf16[192,1024]{1,0:T(8,128)(2,1)S(1)}, u32[]{:S(2)}, u32[]{:S(2)}) %collective-permute-start.19) | collective-permute-done | bytes 393248 | tf_op jit(solution)/shard_map/ppermute | solution.py:25
  96.4 1.2 %fusion = bf16[1,384,1024]{2,1,0:T(8,128)(2,1)} fusion(f32[384,1024]{1,0:T(8,128)S(1)} %convert_add_fusion, bf16[192,1024]{1,0:T(8,128)(2,1)S(1)} %collective-permute-done.20, bf16[192,1024]{1,0:T(8,128)(2,1)S(1)} %collective-permute-done.19), kind=kLoop, calls=%fused_computation.2 | loop fusion | flops 2359296 | bytes 3145728 | tf_op jit(solution)/shard_map/convert_element_type | solution.py:462
  97.5 2.9 %finish.1 = bf16[1024,768]{1,0:T(8,128)(2,1)} custom-call(s32[1024,1]{1,0:T(8,128)S(1)} %get-tuple-element.34.column_ref, bf16[1024,768]{1,0:T(8,128)(2,1)S(1)} %copy-done.2, bf16[1536,384]{1,0:T(8,128)(2,1)S(1)} %bitcast.25), custom_call_target="tpu_custom_call" | custom-call | flops 786432 | bytes 3145728 | tf_op jit(solution)/shard_map/finish/pallas_call | solution.py:377
  (33 shorter events, 0.1 us)
Async XLA Ops:
  0.6 10.8 %copy-start = (bf16[128,8,768]{2,1,0:T(8,128)(2,1)S(1)}, bf16[128,8,768]{2,1,0:T(8,128)(2,1)}, u32[]{:S(2)}) copy-start(bf16[128,8,768]{2,1,0:T(8,128)(2,1)} %param.8) | copy-start | bytes 4718596
  0.6 10.8 %copy-start.13 = (s32[128,8]{0,1:T(8,128)S(1)}, s32[128,8]{0,1:T(8,128)}, u32[]{:S(2)}) copy-start(s32[128,8]{0,1:T(8,128)} %param.7) | copy-start | bytes 12292
  0.7 10.8 %copy-start.3 = (f32[128,8]{0,1:T(8,128)S(1)}, f32[128,8]{0,1:T(8,128)}, u32[]{:S(2)}) copy-start(f32[128,8]{0,1:T(8,128)} %param.6) | copy-start | bytes 12292
  0.7 16.3 %collective-permute-start = (bf16[128,1024]{1,0:T(8,128)(2,1)}, bf16[128,1024]{1,0:T(8,128)(2,1)S(1)}, u32[]{:S(2)}, u32[]{:S(2)}) collective-permute-start(bf16[128,1024]{1,0:T(8,128)(2,1)} %refs_0_), channel_id=1, source_target_pairs={{0,16},{1,17},{2,18},{3,19},{4,20},{5,21},{6,22},{7,23},{8,24},{9,... | collective-permute-start | bytes 786440 | tf_op jit(solution)/shard_map/ppermute | solution.py:25
  4.8 12.4 %collective-permute-start.1 = (bf16[128,1024]{1,0:T(8,128)(2,1)}, bf16[128,1024]{1,0:T(8,128)(2,1)S(1)}, u32[]{:S(2)}, u32[]{:S(2)}) collective-permute-start(bf16[128,1024]{1,0:T(8,128)(2,1)} %refs_0_), channel_id=1, source_target_pairs={{0,8},{1,9},{2,10},{3,11},{4,12},{5,13},{6,14},{7,15},{8,0},{9,1},... | collective-permute-start | bytes 786440 | tf_op jit(solution)/shard_map/ppermute | solution.py:25
  8.3 7.9 %collective-permute-start.3 = (bf16[96,1024]{1,0:T(8,128)(2,1)S(1)}, bf16[96,1024]{1,0:T(8,128)(2,1)S(1)}, u32[]{:S(2)}, u32[]{:S(2)}) collective-permute-start(bf16[96,1024]{1,0:T(8,128)(2,1)S(1)} %get-tuple-element.68), channel_id=1, source_target_pairs={{0,4},{1,5},{2,6},{3,7},{4,0},{5,1},{6,2},{7,3},{8,12},{9,13},{10,... | collective-permute-start | bytes 589832 | tf_op jit(solution)/shard_map/ppermute | solution.py:25
  9.8 6.4 %collective-permute-start.2 = (bf16[96,1024]{1,0:T(8,128)(2,1)S(1)}, bf16[96,1024]{1,0:T(8,128)(2,1)S(1)}, u32[]{:S(2)}, u32[]{:S(2)}) collective-permute-start(bf16[96,1024]{1,0:T(8,128)(2,1)S(1)} %get-tuple-element.69), channel_id=1, source_target_pairs={{0,2},{1,3},{2,0},{3,1},{4,6},{5,7},{6,4},{7,5},{8,10},{9,11},{10,... | collective-permute-start | bytes 589832 | tf_op jit(solution)/shard_map/ppermute | solution.py:25
  17.2 34.0 %all-to-all-start = ((bf16[8,192,384]{2,1,0:T(8,128)(2,1)}), bf16[8,192,384]{2,1,0:T(8,128)(2,1)}, u32[]{:S(2)}, u32[]{:S(2)}) async-start(bf16[8,192,384]{2,1,0:T(8,128)(2,1)} %get-tuple-element.48), calls=%async_computation | async-start | bytes 2359296 | tf_op jit(solution)/shard_map/all_to_all | solution.py:407
  21.7 7.9 %collective-permute-start.9 = (bf16[96,1024]{1,0:T(8,128)(2,1)}, bf16[96,1024]{1,0:T(8,128)(2,1)S(1)}, u32[]{:S(2)}, u32[]{:S(2)}) collective-permute-start(bf16[96,1024]{1,0:T(8,128)(2,1)} %get-tuple-element.66), channel_id=1, source_target_pairs={{0,4},{1,5},{2,6},{3,7},{4,0},{5,1},{6,2},{7,3},{8,12},{9,13},{10,... | collective-permute-start | bytes 589832 | tf_op jit(solution)/shard_map/ppermute | solution.py:25
  23.2 16.2 %copy-start.4 = (bf16[128,1024]{1,0:T(8,128)(2,1)S(1)}, bf16[128,1024]{1,0:T(8,128)(2,1)}, u32[]{:S(2)}) copy-start(bf16[128,1024]{1,0:T(8,128)(2,1)} %refs_0_) | copy-start | bytes 786436
  23.2 8.0 %collective-permute-start.7 = (bf16[96,1024]{1,0:T(8,128)(2,1)S(1)}, bf16[96,1024]{1,0:T(8,128)(2,1)S(1)}, u32[]{:S(2)}, u32[]{:S(2)}) collective-permute-start(bf16[96,1024]{1,0:T(8,128)(2,1)S(1)} %get-tuple-element.67), channel_id=1, source_target_pairs={{0,2},{1,3},{2,0},{3,1},{4,6},{5,7},{6,4},{7,5},{8,10},{9,11},{10,... | collective-permute-start | bytes 589832 | tf_op jit(solution)/shard_map/ppermute | solution.py:25
  25.9 12.2 %collective-permute-start.6 = (bf16[192,1024]{1,0:T(8,128)(2,1)S(1)}, bf16[192,1024]{1,0:T(8,128)(2,1)S(1)}, u32[]{:S(2)}, u32[]{:S(2)}) collective-permute-start(bf16[192,1024]{1,0:T(8,128)(2,1)S(1)} %get-tuple-element.70), channel_id=1, source_target_pairs={{0,4},{1,5},{2,6},{3,7},{4,0},{5,1},{6,2},{7,3},{8,12},{9,13},{10,... | collective-permute-start | bytes 1179656 | tf_op jit(solution)/shard_map/ppermute | solution.py:25
  26.5 12.9 %collective-permute-start.5 = (bf16[192,1024]{1,0:T(8,128)(2,1)S(1)}, bf16[192,1024]{1,0:T(8,128)(2,1)S(1)}, u32[]{:S(2)}, u32[]{:S(2)}) collective-permute-start(bf16[192,1024]{1,0:T(8,128)(2,1)S(1)} %get-tuple-element.71), channel_id=1, source_target_pairs={{0,2},{1,3},{2,0},{3,1},{4,6},{5,7},{6,4},{7,5},{8,10},{9,11},{10,... | collective-permute-start | bytes 1179656 | tf_op jit(solution)/shard_map/ppermute | solution.py:25
  29.7 17.8 %collective-permute-start.10 = (bf16[192,1024]{1,0:T(8,128)(2,1)S(1)}, bf16[192,1024]{1,0:T(8,128)(2,1)S(1)}, u32[]{:S(2)}, u32[]{:S(2)}) collective-permute-start(bf16[192,1024]{1,0:T(8,128)(2,1)S(1)} %pad_maximum_fusion.1), channel_id=1, source_target_pairs={{0,2},{1,3},{2,0},{3,1},{4,6},{5,7},{6,4},{7,5},{8,10},{9,11},{10,... | collective-permute-start | bytes 1179656 | tf_op jit(solution)/shard_map/ppermute | solution.py:25
  31.2 16.2 %collective-permute-start.8 = (bf16[192,1024]{1,0:T(8,128)(2,1)S(1)}, bf16[192,1024]{1,0:T(8,128)(2,1)S(1)}, u32[]{:S(2)}, u32[]{:S(2)}) collective-permute-start(bf16[192,1024]{1,0:T(8,128)(2,1)S(1)} %pad_maximum_fusion), channel_id=1, source_target_pairs={{0,4},{1,5},{2,6},{3,7},{4,0},{5,1},{6,2},{7,3},{8,12},{9,13},{10,... | collective-permute-start | bytes 1179656 | tf_op jit(solution)/shard_map/ppermute | solution.py:25
  32.8 14.6 %collective-permute-start.4 = (bf16[128,1024]{1,0:T(8,128)(2,1)S(1)}, bf16[128,1024]{1,0:T(8,128)(2,1)S(1)}, u32[]{:S(2)}, u32[]{:S(2)}) collective-permute-start(bf16[128,1024]{1,0:T(8,128)(2,1)S(1)} %collective-permute-done.refs_2_.refs_1_), channel_id=1, source_target_pairs={{0,8},{1,9},{2,10},{3,11},{4,12},{5,13},{6,14},{7,15},{8,0},{9,1},... | collective-permute-start | bytes 786440 | tf_op jit(solution)/shard_map/ppermute | solution.py:25
  38.0 10.9 %copy-start.15 = (bf16[192,1024]{1,0:T(8,128)(2,1)}, bf16[192,1024]{1,0:T(8,128)(2,1)S(1)}, u32[]{:S(2)}) copy-start(bf16[192,1024]{1,0:T(8,128)(2,1)S(1)} %collective-permute-done.6.refs_13_) | copy-start | bytes 1179652
  38.1 10.9 %collective-permute-start.12 = (bf16[128,1024]{1,0:T(8,128)(2,1)S(1)}, bf16[128,1024]{1,0:T(8,128)(2,1)S(1)}, u32[]{:S(2)}, u32[]{:S(2)}) collective-permute-start(bf16[128,1024]{1,0:T(8,128)(2,1)S(1)} %collective-permute-done.refs_2_.refs_1_), channel_id=1, source_target_pairs={{0,1},{1,0},{2,3},{3,2},{4,5},{5,4},{6,7},{7,6},{8,9},{9,8},{10,11... | collective-permute-start | bytes 786440 | tf_op jit(solution)/shard_map/ppermute | solution.py:25
  39.4 9.6 %copy-start.16 = (bf16[192,1024]{1,0:T(8,128)(2,1)}, bf16[192,1024]{1,0:T(8,128)(2,1)S(1)}, u32[]{:S(2)}) copy-start(bf16[192,1024]{1,0:T(8,128)(2,1)S(1)} %collective-permute-done.5.refs_12_) | copy-start | bytes 1179652
  39.4 8.6 %collective-permute-start.11 = (bf16[128,1024]{1,0:T(8,128)(2,1)S(1)}, bf16[128,1024]{1,0:T(8,128)(2,1)S(1)}, u32[]{:S(2)}, u32[]{:S(2)}) collective-permute-start(bf16[128,1024]{1,0:T(8,128)(2,1)S(1)} %copy-done.4), channel_id=1, source_target_pairs={{0,1},{1,0},{2,3},{3,2},{4,5},{5,4},{6,7},{7,6},{8,9},{9,8},{10,11... | collective-permute-start | bytes 786440 | tf_op jit(solution)/shard_map/ppermute | solution.py:25
  47.4 14.1 %copy-start.5 = (bf16[128,1024]{1,0:T(8,128)(2,1)}, bf16[128,1024]{1,0:T(8,128)(2,1)S(1)}, u32[]{:S(2)}) copy-start(bf16[128,1024]{1,0:T(8,128)(2,1)S(1)} %collective-permute-done.4.refs_4_.refs_3_) | copy-start | bytes 786436
  47.4 1.5 %collective-permute-start.13 = (bf16[128,1024]{1,0:T(8,128)(2,1)S(1)}, bf16[128,1024]{1,0:T(8,128)(2,1)S(1)}, u32[]{:S(2)}, u32[]{:S(2)}) collective-permute-start(bf16[128,1024]{1,0:T(8,128)(2,1)S(1)} %collective-permute-done.1.refs_3_.refs_2_), channel_id=1, source_target_pairs={{0,1},{1,0},{2,3},{3,2},{4,5},{5,4},{6,7},{7,6},{8,9},{9,8},{10,11... | collective-permute-start | bytes 786440 | tf_op jit(solution)/shard_map/ppermute | solution.py:25
  47.5 1.6 %copy-start.17 = (bf16[192,1024]{1,0:T(8,128)(2,1)}, bf16[192,1024]{1,0:T(8,128)(2,1)S(1)}, u32[]{:S(2)}) copy-start(bf16[192,1024]{1,0:T(8,128)(2,1)S(1)} %collective-permute-done.10.refs_17_) | copy-start | bytes 1179652
  47.5 1.5 %copy-start.18 = (bf16[192,1024]{1,0:T(8,128)(2,1)}, bf16[192,1024]{1,0:T(8,128)(2,1)S(1)}, u32[]{:S(2)}) copy-start(bf16[192,1024]{1,0:T(8,128)(2,1)S(1)} %collective-permute-done.8.refs_16_) | copy-start | bytes 1179652
  47.5 2.9 %collective-permute-start.14 = (bf16[128,1024]{1,0:T(8,128)(2,1)S(1)}, bf16[128,1024]{1,0:T(8,128)(2,1)}, u32[]{:S(2)}, u32[]{:S(2)}) collective-permute-start(bf16[128,1024]{1,0:T(8,128)(2,1)S(1)} %collective-permute-done.4.refs_4_.refs_3_), channel_id=1, source_target_pairs={{0,1},{1,0},{2,3},{3,2},{4,5},{5,4},{6,7},{7,6},{8,9},{9,8},{10,11... | collective-permute-start | bytes 786440 | tf_op jit(solution)/shard_map/ppermute | solution.py:25
  48.0 1.0 copy-start.9
  49.0 0.7 copy-start.11
  49.7 0.7 copy-start.7
  61.6 35.9 %all-to-all-start.1 = ((bf16[8,192,384]{2,1,0:T(8,128)(2,1)}), bf16[8,192,384]{2,1,0:T(8,128)(2,1)S(1)}, u32[]{:S(2)}, u32[]{:S(2)}) async-start(bf16[8,192,384]{2,1,0:T(8,128)(2,1)} %get-tuple-element.49), calls=%async_computation.1 | async-start | bytes 2359296 | tf_op jit(solution)/shard_map/all_to_all | solution.py:407
  66.6 12.4 %collective-permute-start.17 = (bf16[192,1024]{1,0:T(8,128)(2,1)}, bf16[192,1024]{1,0:T(8,128)(2,1)S(1)}, u32[]{:S(2)}, u32[]{:S(2)}) collective-permute-start(bf16[192,1024]{1,0:T(8,128)(2,1)} %get-tuple-element.57), channel_id=1, source_target_pairs={{0,2},{1,3},{2,0},{3,1},{4,6},{5,7},{6,4},{7,5},{8,10},{9,11},{10,... | collective-permute-start | bytes 1179656 | tf_op jit(solution)/shard_map/ppermute | solution.py:25
  68.0 12.2 %collective-permute-start.18 = (bf16[192,1024]{1,0:T(8,128)(2,1)}, bf16[192,1024]{1,0:T(8,128)(2,1)S(1)}, u32[]{:S(2)}, u32[]{:S(2)}) collective-permute-start(bf16[192,1024]{1,0:T(8,128)(2,1)} %get-tuple-element.58), channel_id=1, source_target_pairs={{0,4},{1,5},{2,6},{3,7},{4,0},{5,1},{6,2},{7,3},{8,12},{9,13},{10,... | collective-permute-start | bytes 1179656 | tf_op jit(solution)/shard_map/ppermute | solution.py:25
  69.6 17.6 %collective-permute-start.15 = (bf16[192,1024]{1,0:T(8,128)(2,1)}, bf16[192,1024]{1,0:T(8,128)(2,1)S(1)}, u32[]{:S(2)}, u32[]{:S(2)}) collective-permute-start(bf16[192,1024]{1,0:T(8,128)(2,1)} %get-tuple-element.52), channel_id=1, source_target_pairs={{0,2},{1,3},{2,0},{3,1},{4,6},{5,7},{6,4},{7,5},{8,10},{9,11},{10,... | collective-permute-start | bytes 1179656 | tf_op jit(solution)/shard_map/ppermute | solution.py:25
  70.1 18.5 %collective-permute-start.16 = (bf16[192,1024]{1,0:T(8,128)(2,1)}, bf16[192,1024]{1,0:T(8,128)(2,1)S(1)}, u32[]{:S(2)}, u32[]{:S(2)}) collective-permute-start(bf16[192,1024]{1,0:T(8,128)(2,1)} %get-tuple-element.53), channel_id=1, source_target_pairs={{0,4},{1,5},{2,6},{3,7},{4,0},{5,1},{6,2},{7,3},{8,12},{9,13},{10,... | collective-permute-start | bytes 1179656 | tf_op jit(solution)/shard_map/ppermute | solution.py:25
  70.6 0.9 copy-start.6
  71.6 0.9 copy-start.8
  72.5 0.9 copy-start.10
  73.5 0.9 copy-start.12
  80.2 8.4 %copy-start.14 = (f32[384,1024]{1,0:T(8,128)S(1)}, f32[384,1024]{1,0:T(8,128)}, u32[]{:S(2)}) copy-start(f32[384,1024]{1,0:T(8,128)} %get-tuple-element.51) | copy-start | bytes 4718596
  81.8 13.4 %collective-permute-start.20 = (bf16[192,1024]{1,0:T(8,128)(2,1)S(1)}, bf16[192,1024]{1,0:T(8,128)(2,1)S(1)}, u32[]{:S(2)}, u32[]{:S(2)}) collective-permute-start(bf16[192,1024]{1,0:T(8,128)(2,1)S(1)} %get-tuple-element.64), channel_id=1, source_target_pairs={{0,2},{1,3},{2,0},{3,1},{4,6},{5,7},{6,4},{7,5},{8,10},{9,11},{10,... | collective-permute-start | bytes 1179656 | tf_op jit(solution)/shard_map/ppermute | solution.py:25
  82.4 14.0 %collective-permute-start.19 = (bf16[192,1024]{1,0:T(8,128)(2,1)S(1)}, bf16[192,1024]{1,0:T(8,128)(2,1)S(1)}, u32[]{:S(2)}, u32[]{:S(2)}) collective-permute-start(bf16[192,1024]{1,0:T(8,128)(2,1)S(1)} %get-tuple-element.65), channel_id=1, source_target_pairs={{0,4},{1,5},{2,6},{3,7},{4,0},{5,1},{6,2},{7,3},{8,12},{9,13},{10,... | collective-permute-start | bytes 1179656 | tf_op jit(solution)/shard_map/ppermute | solution.py:25
  86.0 1.1 %copy-start.1 = (bf16[1024,768]{1,0:T(8,128)(2,1)}, bf16[1024,768]{1,0:T(8,128)(2,1)S(1)}, u32[]{:S(2)}) copy-start(bf16[1024,768]{1,0:T(8,128)(2,1)S(1)} %get-tuple-element.35.factors_ref) | copy-start | bytes 4718596
  89.0 8.6 %copy-start.2 = (bf16[1024,768]{1,0:T(8,128)(2,1)S(1)}, bf16[1024,768]{1,0:T(8,128)(2,1)}, u32[]{:S(2)}) copy-start(bf16[1024,768]{1,0:T(8,128)(2,1)} %copy-done.1) | copy-start | bytes 4718596
